TPU v7x, 32 devices: a whole 2x2x4 slice. The times are simulated.
32 devices in a mesh: rep: 16 (over z, x, core), shard: 2 (over y).
Axes of the slice: x: 2, y: 2, z: 4, core: 2. Of those that a mesh axis runs over, the one named last changes fastest.
Arguments:
- tokens: bfloat16 [128, 256, 1024], P(('rep', 'shard')), may hold values from -6 to 6
- cotangent: bfloat16 [128, 256, 1024], P(('rep', 'shard')), may hold values from -6 to 6
- lengths: int32 [32, 3], P(('rep', 'shard')), may hold values from 1 to 4, 8 in all within a row
- adapter_index: int32 [96], P(('rep', 'shard')), may hold values from 0 to 7
- assignment: int32 [256], replicated, may hold values from 0 to 255, each once
- first_gain: float32 [1024], replicated, may hold values from 0.5 to 1.5
- mixer_weight: bfloat16 [1024, 4120], P('shard'), may hold values from -0.1875 to 0.1875
- mixer_down: bfloat16 [128, 1024], P('shard'), may hold values from -0.1875 to 0.1875
- mixer_up: bfloat16 [128, 4120], P('shard'), may hold values from -1.5 to 1.5
- filter_taps: float32 [4, 1792], replicated, may hold values from -3 to 3
- filter_bias: float32 [1792], replicated, may hold values from -3 to 3
- step_bias: float32 [24], replicated, may hold values from -6 to -3
- decay_rate: float32 [24], replicated, may hold values from 0.1 to 8
- skip_gain: float32 [24], replicated, may hold values from 0.5 to 1.5
- state_gain: float32 [1536], replicated, may hold values from 0.5 to 1.5
- merge_weight: bfloat16 [2048, 1024], P('shard'), may hold values from -0.125 to 0.125
- merge_down: bfloat16 [128, 2048], P('shard'), may hold values from -0.125 to 0.125
- merge_up: bfloat16 [128, 1024], P('shard'), may hold values from -1.5 to 1.5
- second_gain: float32 [1024], replicated, may hold values from 0.5 to 1.5
- expand_weight: bfloat16 [1024, 4096], P('shard'), may hold values from -0.1875 to 0.1875
- expand_down: bfloat16 [128, 1024], P('shard'), may hold values from -0.1875 to 0.1875
- expand_up: bfloat16 [128, 4096], P('shard'), may hold values from -1.5 to 1.5
- reduce_weight: bfloat16 [2048, 1024], P('shard'), may hold values from -0.125 to 0.125
- reduce_down: bfloat16 [128, 2048], P('shard'), may hold values from -0.125 to 0.125
- reduce_up: bfloat16 [128, 1024], P('shard'), may hold values from -1.5 to 1.5
Outputs:
- mixed: bfloat16 [128, 256, 1024], P(('rep', 'shard'))
- grad_tokens: float32 [128, 256, 1024], P(('rep', 'shard'))
- grad_mixer_down: float32 [128, 1024], P('shard')
- grad_mixer_up: float32 [128, 4120], P('shard')
- grad_merge_down: float32 [128, 2048], P('shard')
- grad_merge_up: float32 [128, 1024], P('shard')
- grad_expand_down: float32 [128, 1024], P('shard')
- grad_expand_up: float32 [128, 4096], P('shard')
- grad_reduce_down: float32 [128, 2048], P('shard')
- grad_reduce_up: float32 [128, 1024], P('shard')
Inputs may be any that keep to these rules, and one draw needn't show every extreme that they name: `lengths`: row b lists, in length units of 128 tokens, the 3 sequences of group b in order; each row sums to 8 and has largest entry 4. `assignment`: a permutation: every length unit of the input appears once.
All inputs are finite; a program needn't handle non-finite values.
Results may differ from a plain program's by a relative error of at most 0.014.
Values may be sent and summed in bfloat16 or wider, within the bound.
No kernel may reach another device: no remote copies, remote signals or barrier semaphores. Data moves between devices by JAX's collectives and lax.ppermute only.
A program may use at most 640 MiB of HBM per device.

v0:
```python
import jax
import jax.numpy as jnp
from jax import lax
from jax.sharding import PartitionSpec as P

FF = 2048
SSM_HEADS = 24
HEAD_P = 64
STATE = 128
ATT_HEADS = 8
KV_HEADS = 2
HEAD_DIM = 64
CONV = 4
RANK = 16
ADAPTERS = 8
SPAN = 128
SEQ_SLOTS = 3
QBLK = 512
DSSM = 1536
XBC = 1792


EPS = 1e-05
ADAPT_SCALE = 0.5
ROPE_BASE = 100000000000.0
NEG = -1e30
HIGH = lax.Precision.HIGHEST


def rms_norm(value, gain):
    return value * lax.rsqrt(jnp.mean(value * value, axis=-1, keepdims=True) + EPS) * gain


def layout(lengths_row, adapter_row, row_count):
    sizes = lengths_row * SPAN
    finish = jnp.cumsum(sizes)
    begin = finish - sizes
    places = jnp.arange(row_count, dtype=jnp.int32)
    member = (places[:, None] >= begin[None, :]) & (places[:, None] < finish[None, :])
    slots = jnp.arange(SEQ_SLOTS, dtype=jnp.int32)
    segment = jnp.sum(jnp.where(member, slots[None, :], 0), axis=1)
    position = places - jnp.sum(jnp.where(member, begin[None, :], 0), axis=1)
    heads_at = jnp.arange(row_count // SPAN, dtype=jnp.int32) * SPAN
    restart = jnp.any(heads_at[:, None] == begin[None, :], axis=1).astype(jnp.float32)
    lag_masks = jnp.stack([(position >= shift_by).astype(jnp.float32) for shift_by in range(CONV)])
    columns = jnp.arange(SEQ_SLOTS * RANK, dtype=jnp.int32)
    selector = (columns[None, :] // RANK == segment[:, None]).astype(jnp.bfloat16)
    wanted = jnp.repeat(adapter_row, RANK) * RANK + columns % RANK
    picker = (jnp.arange(ADAPTERS * RANK, dtype=jnp.int32)[None, :] == wanted[:, None]).astype(
        jnp.bfloat16
    )
    return (position, segment, restart, lag_masks, selector, picker)


def rotate(flat, position, heads, direction):
    half_dim = HEAD_DIM // 2
    frequency = ROPE_BASE ** (-2.0 * jnp.arange(half_dim, dtype=jnp.float32) / HEAD_DIM)
    angles = position.astype(jnp.float32)[:, None] * frequency[None, :]
    cosine = jnp.cos(angles)[:, None, :]
    sines = direction * jnp.sin(angles)[:, None, :]
    shaped = flat.reshape(flat.shape[0], heads, HEAD_DIM)
    leading = shaped[..., :half_dim]
    trailing = shaped[..., half_dim:]
    turned = jnp.concatenate(
        [leading * cosine - trailing * sines, trailing * cosine + leading * sines], axis=-1
    )
    return turned.reshape(flat.shape)


def state_scan(inputs_x, vector_b, vector_c, delta, decay_rate, restart):
    row_count = inputs_x.shape[0]
    blocks_n = row_count // SPAN
    inputs_x = inputs_x.reshape(blocks_n, SPAN, SSM_HEADS, HEAD_P)
    vector_b = vector_b.reshape(blocks_n, SPAN, STATE)
    vector_c = vector_c.reshape(blocks_n, SPAN, STATE)
    delta = delta.reshape(blocks_n, SPAN, SSM_HEADS)
    lower = jnp.arange(SPAN)[:, None] >= jnp.arange(SPAN)[None, :]

    def advance(state, pieces):
        block_x, block_b, block_c, block_d, block_r = pieces
        state = state * (1.0 - block_r)
        running = jnp.cumsum(-block_d * decay_rate[None, :], axis=0)
        gaps = jnp.where(lower[:, :, None], running[:, None, :] - running[None, :, :], NEG)
        decays = jnp.exp(gaps)
        inner = jnp.dot(block_c, block_b.T, precision=HIGH)
        weights = inner[:, :, None] * decays * block_d[None, :, :]
        local = jnp.einsum("ijh,jhp->ihp", weights, block_x, precision=HIGH)
        carried = jnp.exp(running)[:, :, None] * jnp.einsum(
            "in,hpn->ihp", block_c, state, precision=HIGH
        )
        tail = jnp.exp(running[-1][None, :] - running) * block_d
        state = jnp.exp(running[-1])[:, None, None] * state + jnp.einsum(
            "jh,jhp,jn->hpn", tail, block_x, block_b, precision=HIGH
        )
        return (state, local + carried)

    initial = jnp.zeros((SSM_HEADS, HEAD_P, STATE), jnp.float32)
    _, outputs = lax.scan(advance, initial, (inputs_x, vector_b, vector_c, delta, restart))
    return outputs.reshape(row_count, SSM_HEADS * HEAD_P)


def mamba_mix(
    gate_part,
    conv_part,
    step_part,
    filter_taps,
    filter_bias,
    step_bias,
    decay_rate,
    skip_gain,
    state_gain,
    lag_masks,
    restart,
):
    row_count = conv_part.shape[0]
    summed = filter_bias[None, :]
    for shift_by in range(CONV):
        moved = jnp.pad(conv_part, ((shift_by, 0), (0, 0)))[:row_count]
        summed = summed + filter_taps[shift_by][None, :] * moved * lag_masks[shift_by][:, None]
    convolved = jax.nn.silu(summed)
    inputs_x = convolved[:, :DSSM]
    vector_b = convolved[:, DSSM : DSSM + STATE]
    vector_c = convolved[:, DSSM + STATE :]
    delta = jax.nn.softplus(step_part + step_bias[None, :])
    scanned = state_scan(inputs_x, vector_b, vector_c, delta, decay_rate, restart)
    scanned = scanned + jnp.repeat(skip_gain, HEAD_P)[None, :] * inputs_x
    return rms_norm(scanned * jax.nn.silu(gate_part), state_gain)


def swiglu(value):
    return jax.nn.silu(value[:, :FF]) * value[:, FF:]


def attend(queries, keys_low, values_low, segment):
    row_count = queries.shape[0]
    per_group = ATT_HEADS // KV_HEADS
    query_h = queries.reshape(row_count, KV_HEADS, per_group, HEAD_DIM)
    key_h = keys_low.reshape(row_count, KV_HEADS, HEAD_DIM)
    value_h = values_low.reshape(row_count, KV_HEADS, HEAD_DIM)
    places = jnp.arange(row_count, dtype=jnp.int32)
    score_scale = HEAD_DIM ** (-0.5)
    outputs = []
    log_totals = []
    for number in range(row_count // QBLK):
        begin_row = number * QBLK
        end_row = begin_row + QBLK
        scores = (
            jnp.einsum(
                "qhgd,khd->hgqk",
                query_h[begin_row:end_row],
                key_h[:end_row],
                preferred_element_type=jnp.float32,
            )
            * score_scale
        )
        allowed = (segment[begin_row:end_row, None] == segment[None, :end_row]) & (
            places[begin_row:end_row, None] >= places[None, :end_row]
        )
        scores = jnp.where(allowed, scores, NEG)
        row_peak = jnp.max(scores, axis=-1, keepdims=True)
        raised = jnp.exp(scores - row_peak)
        denominator = jnp.sum(raised, axis=-1, keepdims=True)
        probability = (raised / denominator).astype(jnp.bfloat16)
        blended = jnp.einsum(
            "hgqk,khd->qhgd", probability, value_h[:end_row], preferred_element_type=jnp.float32
        )
        outputs.append(blended.reshape(QBLK, ATT_HEADS * HEAD_DIM))
        log_totals.append(row_peak + jnp.log(denominator))
    return (jnp.concatenate(outputs, axis=0), log_totals)


def attend_back(queries, keys_low, values_low, grad_low, log_totals, segment):
    row_count = queries.shape[0]
    per_group = ATT_HEADS // KV_HEADS
    query_h = queries.reshape(row_count, KV_HEADS, per_group, HEAD_DIM)
    key_h = keys_low.reshape(row_count, KV_HEADS, HEAD_DIM)
    value_h = values_low.reshape(row_count, KV_HEADS, HEAD_DIM)
    grad_h = grad_low.reshape(row_count, KV_HEADS, per_group, HEAD_DIM)
    places = jnp.arange(row_count, dtype=jnp.int32)
    score_scale = HEAD_DIM ** (-0.5)
    grad_keys = jnp.zeros((row_count, KV_HEADS, HEAD_DIM), jnp.float32)
    grad_values = jnp.zeros((row_count, KV_HEADS, HEAD_DIM), jnp.float32)
    pieces = []
    for number in range(row_count // QBLK):
        begin_row = number * QBLK
        end_row = begin_row + QBLK
        query_b = query_h[begin_row:end_row]
        grad_b = grad_h[begin_row:end_row]
        scores = (
            jnp.einsum(
                "qhgd,khd->hgqk", query_b, key_h[:end_row], preferred_element_type=jnp.float32
            )
            * score_scale
        )
        allowed = (segment[begin_row:end_row, None] == segment[None, :end_row]) & (
            places[begin_row:end_row, None] >= places[None, :end_row]
        )
        scores = jnp.where(allowed, scores, NEG)
        probability = jnp.exp(scores - log_totals[number])
        grad_prob = jnp.einsum(
            "qhgd,khd->hgqk", grad_b, value_h[:end_row], preferred_element_type=jnp.float32
        )
        inner = jnp.sum(probability * grad_prob, axis=-1, keepdims=True)
        grad_score = (probability * (grad_prob - inner)).astype(jnp.bfloat16)
        grad_query = (
            jnp.einsum(
                "hgqk,khd->qhgd", grad_score, key_h[:end_row], preferred_element_type=jnp.float32
            )
            * score_scale
        )
        pieces.append(grad_query.reshape(QBLK, ATT_HEADS * HEAD_DIM))
        grad_keys = grad_keys.at[:end_row].add(
            jnp.einsum("hgqk,qhgd->khd", grad_score, query_b, preferred_element_type=jnp.float32)
            * score_scale
        )
        grad_values = grad_values.at[:end_row].add(
            jnp.einsum(
                "hgqk,qhgd->khd",
                probability.astype(jnp.bfloat16),
                grad_b,
                preferred_element_type=jnp.float32,
            )
        )
    return (
        jnp.concatenate(pieces, axis=0),
        grad_keys.reshape(row_count, KV_HEADS * HEAD_DIM),
        grad_values.reshape(row_count, KV_HEADS * HEAD_DIM),
    )


def project(hidden, weight, lower, upper, picker, selector):
    lower_pick = jnp.dot(picker, lower, preferred_element_type=jnp.float32).astype(jnp.bfloat16)
    upper_pick = jnp.dot(picker, upper, preferred_element_type=jnp.float32).astype(jnp.bfloat16)
    middle = (
        jnp.einsum("ri,ai->ra", hidden, lower_pick, preferred_element_type=jnp.float32) * selector
    ).astype(jnp.bfloat16)
    result = jnp.dot(hidden, weight, preferred_element_type=jnp.float32) + ADAPT_SCALE * jnp.dot(
        middle, upper_pick, preferred_element_type=jnp.float32
    )
    return (result, middle, lower_pick, upper_pick)


def project_back(grad, hidden, middle, weight, lower_pick, upper_pick, picker, selector):
    grad_low = grad.astype(jnp.bfloat16)
    grad_middle = (
        ADAPT_SCALE
        * jnp.einsum("ro,ao->ra", grad_low, upper_pick, preferred_element_type=jnp.float32)
    ).astype(jnp.bfloat16) * selector
    grad_hidden = jnp.einsum(
        "ro,io->ri", grad_low, weight, preferred_element_type=jnp.float32
    ) + jnp.dot(grad_middle, lower_pick, preferred_element_type=jnp.float32)
    picker_wide = picker.astype(jnp.float32)
    lower_part = jnp.einsum("ra,ri->ai", grad_middle, hidden, preferred_element_type=jnp.float32)
    upper_part = ADAPT_SCALE * jnp.einsum(
        "ra,ro->ao", middle, grad_low, preferred_element_type=jnp.float32
    )
    grad_lower = jnp.einsum("sa,si->ai", picker_wide, lower_part, precision=HIGH)
    grad_upper = jnp.einsum("sa,so->ao", picker_wide, upper_part, precision=HIGH)
    return (grad_hidden, (grad_lower, grad_upper))


def fetch(weight, lower, upper):
    return (
        lax.all_gather(weight, "shard", axis=0, tiled=True),
        lax.all_gather(lower, "shard", axis=0, tiled=True),
        lax.all_gather(upper, "shard", axis=0, tiled=True),
    )


def refetch(weight):
    return lax.all_gather(weight, "shard", axis=0, tiled=True)


def settle_all(mixer_grads, merge_grads, expand_grads, reduce_grads):
    owned = (
        lax.psum_scatter(
            mixer_grads[0].astype(jnp.bfloat16), "shard", scatter_dimension=0, tiled=True
        ).astype(jnp.float32),
        lax.psum_scatter(
            mixer_grads[1].astype(jnp.bfloat16), "shard", scatter_dimension=0, tiled=True
        ).astype(jnp.float32),
        lax.psum_scatter(
            merge_grads[0].astype(jnp.bfloat16), "shard", scatter_dimension=0, tiled=True
        ).astype(jnp.float32),
        lax.psum_scatter(
            merge_grads[1].astype(jnp.bfloat16), "shard", scatter_dimension=0, tiled=True
        ).astype(jnp.float32),
        lax.psum_scatter(
            expand_grads[0].astype(jnp.bfloat16), "shard", scatter_dimension=0, tiled=True
        ).astype(jnp.float32),
        lax.psum_scatter(
            expand_grads[1].astype(jnp.bfloat16), "shard", scatter_dimension=0, tiled=True
        ).astype(jnp.float32),
        lax.psum_scatter(
            reduce_grads[0].astype(jnp.bfloat16), "shard", scatter_dimension=0, tiled=True
        ).astype(jnp.float32),
        lax.psum_scatter(
            reduce_grads[1].astype(jnp.bfloat16), "shard", scatter_dimension=0, tiled=True
        ).astype(jnp.float32),
    )
    return lax.psum(
        (owned[0], owned[1], owned[2], owned[3], owned[4], owned[5], owned[6], owned[7]), "rep"
    )


def arrive(tokens, cotangent, assignment):
    stripe = tokens.shape[0]
    feature_width = tokens.shape[2]
    rep_count = lax.axis_size("rep")
    shard_count = lax.axis_size("shard")
    groups = rep_count * shard_count
    per_device = assignment.shape[0] // groups

    def select_units(value):
        taken = jnp.take(value, assignment, axis=1)
        return jnp.transpose(taken.reshape(stripe, groups, per_device, feature_width), (1, 2, 0, 3))

    outgoing_tokens = select_units(tokens)
    outgoing_grads = select_units(cotangent)
    incoming = (
        lax.all_to_all(outgoing_tokens, ("rep", "shard"), split_axis=0, concat_axis=2, tiled=True),
        lax.all_to_all(outgoing_grads, ("rep", "shard"), split_axis=0, concat_axis=2, tiled=True),
    )
    total_rows = per_device * stripe * groups
    return (
        incoming[0].reshape(total_rows, feature_width),
        incoming[1].reshape(total_rows, feature_width),
    )


def depart(mixed_wide, grad_wide, assignment, stripe):
    feature_width = mixed_wide.shape[1]
    rep_count = lax.axis_size("rep")
    shard_count = lax.axis_size("shard")
    groups = rep_count * shard_count
    per_device = assignment.shape[0] // groups
    first_out = mixed_wide.reshape(1, per_device, stripe * groups, feature_width)
    second_out = grad_wide.reshape(1, per_device, stripe * groups, feature_width)
    incoming = (
        lax.all_to_all(
            first_out.astype(jnp.bfloat16),
            ("rep", "shard"),
            split_axis=2,
            concat_axis=0,
            tiled=True,
        ).astype(first_out.dtype),
        lax.all_to_all(
            second_out.astype(jnp.bfloat16),
            ("rep", "shard"),
            split_axis=2,
            concat_axis=0,
            tiled=True,
        ).astype(second_out.dtype),
    )
    inverse = jnp.argsort(assignment)

    def place_units(value):
        units = value.reshape(groups * per_device, stripe, feature_width)
        return jnp.transpose(jnp.take(units, inverse, axis=0), (1, 0, 2))

    return (place_units(incoming[0]).astype(jnp.bfloat16), place_units(incoming[1]))


def on_device(
    tokens,
    cotangent,
    lengths,
    adapter_index,
    assignment,
    first_gain,
    mixer_weight,
    mixer_down,
    mixer_up,
    filter_taps,
    filter_bias,
    step_bias,
    decay_rate,
    skip_gain,
    state_gain,
    merge_weight,
    merge_down,
    merge_up,
    second_gain,
    expand_weight,
    expand_down,
    expand_up,
    reduce_weight,
    reduce_down,
    reduce_up,
):
    work_tokens, work_cotangent = arrive(tokens, cotangent, assignment)
    row_count = work_tokens.shape[0]
    position, segment, restart, lag_masks, selector, picker = layout(
        lengths[0], adapter_index, row_count
    )
    residual = work_tokens.astype(jnp.float32)

    def first_norm(value):
        return rms_norm(value, first_gain)

    def second_norm(value):
        return rms_norm(value, second_gain)

    def mamba_piece(gate_part, conv_part, step_part):
        return mamba_mix(
            gate_part,
            conv_part,
            step_part,
            filter_taps,
            filter_bias,
            step_bias,
            decay_rate,
            skip_gain,
            state_gain,
            lag_masks,
            restart,
        )

    normed, first_back = jax.vjp(first_norm, residual)
    hidden = normed.astype(jnp.bfloat16)
    mixer_full = fetch(mixer_weight, mixer_down, mixer_up)
    united, mixer_mid, mixer_lpick, mixer_upick = project(
        hidden, mixer_full[0], mixer_full[1], mixer_full[2], picker, selector
    )
    offset = DSSM + XBC + SSM_HEADS
    query_width = ATT_HEADS * HEAD_DIM
    key_width = KV_HEADS * HEAD_DIM
    mamba_out, mamba_back = jax.vjp(
        mamba_piece, united[:, :DSSM], united[:, DSSM : DSSM + XBC], united[:, DSSM + XBC : offset]
    )
    queries = rotate(united[:, offset : offset + query_width], position, ATT_HEADS, 1.0).astype(
        jnp.bfloat16
    )
    keys_low = rotate(
        united[:, offset + query_width : offset + query_width + key_width], position, KV_HEADS, 1.0
    ).astype(jnp.bfloat16)
    values_low = united[:, offset + query_width + key_width :].astype(jnp.bfloat16)
    attended, log_totals = attend(queries, keys_low, values_low, segment)
    joined = jnp.concatenate(
        [mamba_out.astype(jnp.bfloat16), attended.astype(jnp.bfloat16)], axis=1
    )
    merge_full = fetch(merge_weight, merge_down, merge_up)
    branch, merge_mid, merge_lpick, merge_upick = project(
        joined, merge_full[0], merge_full[1], merge_full[2], picker, selector
    )
    middle = residual + branch
    second, second_back = jax.vjp(second_norm, middle)
    second_low = second.astype(jnp.bfloat16)
    expand_full = fetch(expand_weight, expand_down, expand_up)
    expanded, expand_mid, expand_lpick, expand_upick = project(
        second_low, expand_full[0], expand_full[1], expand_full[2], picker, selector
    )
    active, active_back = jax.vjp(swiglu, expanded)
    active_low = active.astype(jnp.bfloat16)
    reduce_full = fetch(reduce_weight, reduce_down, reduce_up)
    shrunk, reduce_mid, reduce_lpick, reduce_upick = project(
        active_low, reduce_full[0], reduce_full[1], reduce_full[2], picker, selector
    )
    mixed_wide = middle + shrunk
    grad_top = work_cotangent.astype(jnp.float32)
    reduce_matrix = reduce_full[0]
    reduce_matrix = refetch(reduce_weight)
    grad_active, reduce_grads = project_back(
        grad_top,
        active_low,
        reduce_mid,
        reduce_matrix,
        reduce_lpick,
        reduce_upick,
        picker,
        selector,
    )
    (grad_expanded,) = active_back(grad_active)
    expand_matrix = expand_full[0]
    expand_matrix = refetch(expand_weight)
    grad_second, expand_grads = project_back(
        grad_expanded,
        second_low,
        expand_mid,
        expand_matrix,
        expand_lpick,
        expand_upick,
        picker,
        selector,
    )
    (grad_normed,) = second_back(grad_second)
    grad_middle = grad_top + grad_normed
    merge_matrix = merge_full[0]
    merge_matrix = refetch(merge_weight)
    grad_joined, merge_grads = project_back(
        grad_middle, joined, merge_mid, merge_matrix, merge_lpick, merge_upick, picker, selector
    )
    grad_attended = grad_joined[:, DSSM:].astype(jnp.bfloat16)
    grad_queries, grad_keys, grad_values = attend_back(
        queries, keys_low, values_low, grad_attended, log_totals, segment
    )
    grad_gate, grad_conv, grad_step = mamba_back(grad_joined[:, :DSSM])
    grad_united = jnp.concatenate(
        [
            grad_gate,
            grad_conv,
            grad_step,
            rotate(grad_queries, position, ATT_HEADS, -1.0),
            rotate(grad_keys, position, KV_HEADS, -1.0),
            grad_values,
        ],
        axis=1,
    )
    mixer_matrix = mixer_full[0]
    mixer_matrix = refetch(mixer_weight)
    grad_hidden, mixer_grads = project_back(
        grad_united, hidden, mixer_mid, mixer_matrix, mixer_lpick, mixer_upick, picker, selector
    )
    (grad_first,) = first_back(grad_hidden)
    work_grad = grad_middle + grad_first
    mixed, grad_tokens = depart(mixed_wide, work_grad, assignment, tokens.shape[0])
    final = settle_all(mixer_grads, merge_grads, expand_grads, reduce_grads)
    return (
        mixed,
        grad_tokens,
        final[0],
        final[1],
        final[2],
        final[3],
        final[4],
        final[5],
        final[6],
        final[7],
    )


def solution(mesh):
    placed = (
        P(("rep", "shard"), None, None),
        P(("rep", "shard"), None, None),
        P(("rep", "shard"), None),
        P(("rep", "shard")),
        P(),
        P(),
        P("shard", None),
        P("shard", None),
        P("shard", None),
        P(),
        P(),
        P(),
        P(),
        P(),
        P(),
        P("shard", None),
        P("shard", None),
        P("shard", None),
        P(),
        P("shard", None),
        P("shard", None),
        P("shard", None),
        P("shard", None),
        P("shard", None),
        P("shard", None),
    )
    return jax.shard_map(
        on_device,
        mesh=mesh,
        in_specs=placed,
        out_specs=(
            P(("rep", "shard"), None, None),
            P(("rep", "shard"), None, None),
            P("shard", None),
            P("shard", None),
            P("shard", None),
            P("shard", None),
            P("shard", None),
            P("shard", None),
            P("shard", None),
            P("shard", None),
        ),
        check_vma=False,
    )
```

profile of v0, /device:TPU:0, one launch (start us, length us, event | category | flops | bytes accessed | tf_op | source)
XLA Modules:
  0.0 1767.1 jit_solution(348000668679048255)
XLA Ops:
  14.9 8.2 gather_fusion
  52.1 21.5 %all_gather.41 = bf16[128,1024]{1,0:T(8,128)(2,1)S(1)} all-gather(bf16[64,1024]{1,0:T(8,128)(2,1)S(1)} %copy-done.86), channel_id=1, replica_groups=mesh['rep'=16,'shard'=2] {'shard'}, dimensions={0}, use_global_device_ids=true | all-gather | bytes 393216 | tf_op jit(solution)/shard_map/all_gather | solution.py:265
  88.8 14.2 all_gather.44
  103.0 14.6 all_gather.50
  124.4 28.3 %all_gather.51 = bf16[128,1024]{1,0:T(8,128)(2,1)S(1)} all-gather(bf16[64,1024]{1,0:T(8,128)(2,1)} %param.69), channel_id=1, replica_groups=mesh['rep'=16,'shard'=2] {'shard'}, dimensions={0}, use_global_device_ids=true | all-gather | bytes 393216 | tf_op jit(solution)/shard_map/all_gather | solution.py:266
  193.2 10.9 fusion.257
  204.1 77.9 %all-gather.7.cloned.1.call-done = bf16[1024,4120]{0,1:T(8,128)(2,1)} async-done(((bf16[512,4120]{0,1:T(8,128)(2,1)}), bf16[1024,4120]{0,1:T(8,128)(2,1)}) %all-gather.7.cloned.1.call-update) | async-done | bytes 8437776 | tf_op jit(solution)/shard_map/all_gather | solution.py:264
  282.0 15.4 fusion.254
  297.4 13.4 fusion.250
  315.0 9.2 fusion.154
  353.5 367.5 %while.77 = (s32[]{:T(128)}, f32[24,64,128]{2,1,0:T(8,128)S(1)}, f32[8,128,24,64]{1,0,3,2:T(8,128)}, f32[8]{0:T(128)S(1)}, f32[8,128,128,24]{2,1,3,0:T(8,128)}, ...) while((s32[]{:T(128)}, f32[24,64,128]{2,1,0:T(8,128)S(1)}, ...), condition=%wide.region_7.9_spmd.clone.clone, body=%wide.region_5.8_spmd.clone.clone.sunk | while | flops 937049088 | bytes 17875808 | solution.py:98
  367.2 20.7 %dynamic_update_slice.220 = f32[8,128,24,64]{1,0,3,2:T(8,128)} dynamic-update-slice(f32[8,128,24,64]{1,0,3,2:T(8,128)} %get-tuple-element.2129, f32[1,128,24,64]{1,0,3,2:T(1,128)S(1)} %bitcast.662, s32[]{:T(128)} %get-tuple-element.2127, s32[]{:T(128)} %constant.364.clone.1..sunk.1, s32[]{:T(128)} %constant.364.clone.1..sunk.1, s32[]{:T(128)} %constant.364.clone.1..sunk.1) | dynamic-update-slice | bytes 1572868 | tf_op jit(solution)/shard_map/jvp()/while/body/jit(dynamic_update_index_in_dim)/dynamic_update_slice | solution.py:98
  413.2 20.7 %dynamic_update_slice.220 = f32[8,128,24,64]{1,0,3,2:T(8,128)} dynamic-update-slice(f32[8,128,24,64]{1,0,3,2:T(8,128)} %get-tuple-element.2129, f32[1,128,24,64]{1,0,3,2:T(1,128)S(1)} %bitcast.662, s32[]{:T(128)} %get-tuple-element.2127, s32[]{:T(128)} %constant.364.clone.1..sunk.1, s32[]{:T(128)} %constant.364.clone.1..sunk.1, s32[]{:T(128)} %constant.364.clone.1..sunk.1) | dynamic-update-slice | bytes 1572868 | tf_op jit(solution)/shard_map/jvp()/while/body/jit(dynamic_update_index_in_dim)/dynamic_update_slice | solution.py:98
  459.1 20.7 %dynamic_update_slice.220 = f32[8,128,24,64]{1,0,3,2:T(8,128)} dynamic-update-slice(f32[8,128,24,64]{1,0,3,2:T(8,128)} %get-tuple-element.2129, f32[1,128,24,64]{1,0,3,2:T(1,128)S(1)} %bitcast.662, s32[]{:T(128)} %get-tuple-element.2127, s32[]{:T(128)} %constant.364.clone.1..sunk.1, s32[]{:T(128)} %constant.364.clone.1..sunk.1, s32[]{:T(128)} %constant.364.clone.1..sunk.1) | dynamic-update-slice | bytes 1572868 | tf_op jit(solution)/shard_map/jvp()/while/body/jit(dynamic_update_index_in_dim)/dynamic_update_slice | solution.py:98
  504.9 20.7 %dynamic_update_slice.220 = f32[8,128,24,64]{1,0,3,2:T(8,128)} dynamic-update-slice(f32[8,128,24,64]{1,0,3,2:T(8,128)} %get-tuple-element.2129, f32[1,128,24,64]{1,0,3,2:T(1,128)S(1)} %bitcast.662, s32[]{:T(128)} %get-tuple-element.2127, s32[]{:T(128)} %constant.364.clone.1..sunk.1, s32[]{:T(128)} %constant.364.clone.1..sunk.1, s32[]{:T(128)} %constant.364.clone.1..sunk.1) | dynamic-update-slice | bytes 1572868 | tf_op jit(solution)/shard_map/jvp()/while/body/jit(dynamic_update_index_in_dim)/dynamic_update_slice | solution.py:98
  550.7 20.7 %dynamic_update_slice.220 = f32[8,128,24,64]{1,0,3,2:T(8,128)} dynamic-update-slice(f32[8,128,24,64]{1,0,3,2:T(8,128)} %get-tuple-element.2129, f32[1,128,24,64]{1,0,3,2:T(1,128)S(1)} %bitcast.662, s32[]{:T(128)} %get-tuple-element.2127, s32[]{:T(128)} %constant.364.clone.1..sunk.1, s32[]{:T(128)} %constant.364.clone.1..sunk.1, s32[]{:T(128)} %constant.364.clone.1..sunk.1) | dynamic-update-slice | bytes 1572868 | tf_op jit(solution)/shard_map/jvp()/while/body/jit(dynamic_update_index_in_dim)/dynamic_update_slice | solution.py:98
  596.6 20.7 %dynamic_update_slice.220 = f32[8,128,24,64]{1,0,3,2:T(8,128)} dynamic-update-slice(f32[8,128,24,64]{1,0,3,2:T(8,128)} %get-tuple-element.2129, f32[1,128,24,64]{1,0,3,2:T(1,128)S(1)} %bitcast.662, s32[]{:T(128)} %get-tuple-element.2127, s32[]{:T(128)} %constant.364.clone.1..sunk.1, s32[]{:T(128)} %constant.364.clone.1..sunk.1, s32[]{:T(128)} %constant.364.clone.1..sunk.1) | dynamic-update-slice | bytes 1572868 | tf_op jit(solution)/shard_map/jvp()/while/body/jit(dynamic_update_index_in_dim)/dynamic_update_slice | solution.py:98
  642.5 20.7 %dynamic_update_slice.220 = f32[8,128,24,64]{1,0,3,2:T(8,128)} dynamic-update-slice(f32[8,128,24,64]{1,0,3,2:T(8,128)} %get-tuple-element.2129, f32[1,128,24,64]{1,0,3,2:T(1,128)S(1)} %bitcast.662, s32[]{:T(128)} %get-tuple-element.2127, s32[]{:T(128)} %constant.364.clone.1..sunk.1, s32[]{:T(128)} %constant.364.clone.1..sunk.1, s32[]{:T(128)} %constant.364.clone.1..sunk.1) | dynamic-update-slice | bytes 1572868 | tf_op jit(solution)/shard_map/jvp()/while/body/jit(dynamic_update_index_in_dim)/dynamic_update_slice | solution.py:98
  688.2 20.7 %dynamic_update_slice.220 = f32[8,128,24,64]{1,0,3,2:T(8,128)} dynamic-update-slice(f32[8,128,24,64]{1,0,3,2:T(8,128)} %get-tuple-element.2129, f32[1,128,24,64]{1,0,3,2:T(1,128)S(1)} %bitcast.662, s32[]{:T(128)} %get-tuple-element.2127, s32[]{:T(128)} %constant.364.clone.1..sunk.1, s32[]{:T(128)} %constant.364.clone.1..sunk.1, s32[]{:T(128)} %constant.364.clone.1..sunk.1) | dynamic-update-slice | bytes 1572868 | tf_op jit(solution)/shard_map/jvp()/while/body/jit(dynamic_update_index_in_dim)/dynamic_update_slice | solution.py:98
  721.6 8.6 multiply_reduce_fusion.1
  742.9 9.2 fusion.126
  766.0 8.0 fusion.242
  778.4 11.7 fusion.255
  790.1 8.2 multiply_add_fusion.1
  798.3 14.9 fusion.205
  813.2 8.4 fusion.203
  822.1 16.4 fusion.243
  883.8 11.6 fusion.170
  898.0 14.0 fusion.123
  911.9 9.3 fusion.184
  951.3 464.3 %while.76 = (s32[]{:T(128)}, f32[24,64,128]{2,1,0:T(8,128)S(1)}, f32[8,128,24,64]{1,0,3,2:T(8,128)}, f32[8,128,128]{2,1,0:T(8,128)}, f32[8,128,128]{2,1,0:T(8,12...) while((s32[]{:T(128)}, f32[24,64,128]{2,1,0:T(8,128)S(1)}, ...), condition=%wide.region_26.29_spmd.clone, body=%wide.region_17.28_spmd.clone.sunk | while | flops 1869991936 | bytes 24512936 | solution.py:98
  960.7 20.8 %dynamic_update_slice.208 = f32[8,128,24,64]{1,0,3,2:T(8,128)} dynamic-update-slice(f32[8,128,24,64]{1,0,3,2:T(8,128)} %get-tuple-element.2220, f32[1,128,24,64]{1,0,3,2:T(1,128)S(1)} %bitcast.654, s32[]{:T(128)S(6)} %sub.429, s32[]{:T(128)} %constant.364.clone.1..sunk, s32[]{:T(128)} %constant.364.clone.1..sunk, s32[]{:T(128)} %constant.364.clone.1..sunk) | dynamic-update-slice | bytes 1572868 | tf_op jit(solution)/shard_map/transpose(jvp())/while/body/jit(dynamic_update_index_in_dim)/dynamic_update_slice | solution.py:98
  1018.7 20.8 %dynamic_update_slice.208 = f32[8,128,24,64]{1,0,3,2:T(8,128)} dynamic-update-slice(f32[8,128,24,64]{1,0,3,2:T(8,128)} %get-tuple-element.2220, f32[1,128,24,64]{1,0,3,2:T(1,128)S(1)} %bitcast.654, s32[]{:T(128)S(6)} %sub.429, s32[]{:T(128)} %constant.364.clone.1..sunk, s32[]{:T(128)} %constant.364.clone.1..sunk, s32[]{:T(128)} %constant.364.clone.1..sunk) | dynamic-update-slice | bytes 1572868 | tf_op jit(solution)/shard_map/transpose(jvp())/while/body/jit(dynamic_update_index_in_dim)/dynamic_update_slice | solution.py:98
  1076.6 20.8 %dynamic_update_slice.208 = f32[8,128,24,64]{1,0,3,2:T(8,128)} dynamic-update-slice(f32[8,128,24,64]{1,0,3,2:T(8,128)} %get-tuple-element.2220, f32[1,128,24,64]{1,0,3,2:T(1,128)S(1)} %bitcast.654, s32[]{:T(128)S(6)} %sub.429, s32[]{:T(128)} %constant.364.clone.1..sunk, s32[]{:T(128)} %constant.364.clone.1..sunk, s32[]{:T(128)} %constant.364.clone.1..sunk) | dynamic-update-slice | bytes 1572868 | tf_op jit(solution)/shard_map/transpose(jvp())/while/body/jit(dynamic_update_index_in_dim)/dynamic_update_slice | solution.py:98
  1134.6 20.8 %dynamic_update_slice.208 = f32[8,128,24,64]{1,0,3,2:T(8,128)} dynamic-update-slice(f32[8,128,24,64]{1,0,3,2:T(8,128)} %get-tuple-element.2220, f32[1,128,24,64]{1,0,3,2:T(1,128)S(1)} %bitcast.654, s32[]{:T(128)S(6)} %sub.429, s32[]{:T(128)} %constant.364.clone.1..sunk, s32[]{:T(128)} %constant.364.clone.1..sunk, s32[]{:T(128)} %constant.364.clone.1..sunk) | dynamic-update-slice | bytes 1572868 | tf_op jit(solution)/shard_map/transpose(jvp())/while/body/jit(dynamic_update_index_in_dim)/dynamic_update_slice | solution.py:98
  1192.6 20.8 %dynamic_update_slice.208 = f32[8,128,24,64]{1,0,3,2:T(8,128)} dynamic-update-slice(f32[8,128,24,64]{1,0,3,2:T(8,128)} %get-tuple-element.2220, f32[1,128,24,64]{1,0,3,2:T(1,128)S(1)} %bitcast.654, s32[]{:T(128)S(6)} %sub.429, s32[]{:T(128)} %constant.364.clone.1..sunk, s32[]{:T(128)} %constant.364.clone.1..sunk, s32[]{:T(128)} %constant.364.clone.1..sunk) | dynamic-update-slice | bytes 1572868 | tf_op jit(solution)/shard_map/transpose(jvp())/while/body/jit(dynamic_update_index_in_dim)/dynamic_update_slice | solution.py:98
  1250.6 20.8 %dynamic_update_slice.208 = f32[8,128,24,64]{1,0,3,2:T(8,128)} dynamic-update-slice(f32[8,128,24,64]{1,0,3,2:T(8,128)} %get-tuple-element.2220, f32[1,128,24,64]{1,0,3,2:T(1,128)S(1)} %bitcast.654, s32[]{:T(128)S(6)} %sub.429, s32[]{:T(128)} %constant.364.clone.1..sunk, s32[]{:T(128)} %constant.364.clone.1..sunk, s32[]{:T(128)} %constant.364.clone.1..sunk) | dynamic-update-slice | bytes 1572868 | tf_op jit(solution)/shard_map/transpose(jvp())/while/body/jit(dynamic_update_index_in_dim)/dynamic_update_slice | solution.py:98
  1308.6 20.8 %dynamic_update_slice.208 = f32[8,128,24,64]{1,0,3,2:T(8,128)} dynamic-update-slice(f32[8,128,24,64]{1,0,3,2:T(8,128)} %get-tuple-element.2220, f32[1,128,24,64]{1,0,3,2:T(1,128)S(1)} %bitcast.654, s32[]{:T(128)S(6)} %sub.429, s32[]{:T(128)} %constant.364.clone.1..sunk, s32[]{:T(128)} %constant.364.clone.1..sunk, s32[]{:T(128)} %constant.364.clone.1..sunk) | dynamic-update-slice | bytes 1572868 | tf_op jit(solution)/shard_map/transpose(jvp())/while/body/jit(dynamic_update_index_in_dim)/dynamic_update_slice | solution.py:98
  1366.6 20.8 %dynamic_update_slice.208 = f32[8,128,24,64]{1,0,3,2:T(8,128)} dynamic-update-slice(f32[8,128,24,64]{1,0,3,2:T(8,128)} %get-tuple-element.2220, f32[1,128,24,64]{1,0,3,2:T(1,128)S(1)} %bitcast.654, s32[]{:T(128)S(6)} %sub.429, s32[]{:T(128)} %constant.364.clone.1..sunk, s32[]{:T(128)} %constant.364.clone.1..sunk, s32[]{:T(128)} %constant.364.clone.1..sunk) | dynamic-update-slice | bytes 1572868 | tf_op jit(solution)/shard_map/transpose(jvp())/while/body/jit(dynamic_update_index_in_dim)/dynamic_update_slice | solution.py:98
  1415.7 8.7 bitcast_add_fusion
  1424.8 11.0 multiply_multiply_fusion.2
  1444.5 14.0 fusion.168
  1467.8 14.9 fusion.258
  1503.6 13.2 fusion.241
  1562.6 10.5 reduce-scatter.21.cloned.1.call-done
  1573.1 32.0 %reduce-scatter.19.cloned.1.call-done = bf16[64,4096]{1,0:T(8,128)(2,1)} async-done(((bf16[128,4096]{1,0:T(8,128)(2,1)}), bf16[64,4096]{1,0:T(8,128)(2,1)}) %reduce-scatter.19.cloned.1.call-update) | async-done | bytes 524304 | tf_op jit(solution)/shard_map/reduce_scatter | solution.py:291
  1605.1 22.1 %reduce-scatter.11.cloned.1.call-done = bf16[64,4120]{1,0:T(8,128)(2,1)} async-done(((bf16[128,4120]{1,0:T(8,128)(2,1)}), bf16[64,4120]{1,0:T(8,128)(2,1)}) %reduce-scatter.11.cloned.1.call-update) | async-done | bytes 527376 | tf_op jit(solution)/shard_map/reduce_scatter | solution.py:279
  1627.2 98.3 %all-reduce.17 = (f32[64,1024]{1,0:T(8,128)}, f32[64,4120]{1,0:T(8,128)}, f32[64,2048]{1,0:T(8,128)}, f32[64,1024]{1,0:T(8,128)}, f32[64,1024]{1,0:T(8,128)}, /*...) all-reduce(bf16[64,1024]{1,0:T(8,128)(2,1)} %reduce-scatter.9.clone, ...), channel_id=1, replica_groups=mesh['rep'=16,'shard'=2] {'rep'}, use_global_device_ids=true, to_apply=%region_31.34 | all-reduce | flops 1050112 | bytes 6300672 | tf_op jit(solution)/shard_map/psum | solution.py:301
  (987 shorter events, 858.1 us)
Async XLA Ops:
  7.2 153.0 %all-gather.15.cloned.1.call-start = ((), (), s32[]{:S(2)}) async-start(), calls=%async_computation.16 | async-start | bytes 1572864 | tf_op jit(solution)/shard_map/all_gather | solution.py:266
  7.9 154.6 %all-gather.9.cloned.1.call-start = ((), (), s32[]{:S(2)}) async-start(), calls=%async_computation.13 | async-start | bytes 1622016 | tf_op jit(solution)/shard_map/all_gather | solution.py:266
  8.7 184.5 %all-gather.17.cloned.1.call-start = ((), (), s32[]{:S(2)}) async-start(), calls=%async_computation.17 | async-start | bytes 6291456 | tf_op jit(solution)/shard_map/all_gather | solution.py:264
  9.4 272.6 %all-gather.7.cloned.1.call-start = ((), (), s32[]{:S(2)}) async-start(), calls=%async_computation.12 | async-start | bytes 12656640 | tf_op jit(solution)/shard_map/all_gather | solution.py:264
  10.0 755.9 %all-gather.11.cloned.1.call-start = ((), (), s32[]{:S(2)}) async-start(), calls=%async_computation.14 | async-start | bytes 6291456 | tf_op jit(solution)/shard_map/all_gather | solution.py:264
  37.8 14.3 copy-start.86
  37.8 35.8 %copy-start.87 = (bf16[64,1024]{1,0:T(8,128)(2,1)S(1)}, bf16[64,1024]{1,0:T(8,128)(2,1)}, u32[]{:S(2)}) copy-start(bf16[64,1024]{1,0:T(8,128)(2,1)} %param.62) | copy-start | bytes 393220
  37.8 43.0 %copy-start.88 = (bf16[64,1024]{1,0:T(8,128)(2,1)S(1)}, bf16[64,1024]{1,0:T(8,128)(2,1)}, u32[]{:S(2)}) copy-start(bf16[64,1024]{1,0:T(8,128)(2,1)} %param.65) | copy-start | bytes 393220
  37.8 50.2 %copy-start.124 = (f32[4,1792]{1,0:T(4,128)S(1)}, f32[4,1792]{1,0:T(4,128)}, u32[]{:S(2)}) copy-start(f32[4,1792]{1,0:T(4,128)} %param.54) | copy-start | bytes 86020
  37.8 50.9 %copy-start.76 = (bf16[64,2048]{1,0:T(8,128)(2,1)S(1)}, bf16[64,2048]{1,0:T(8,128)(2,1)}, u32[]{:S(2)}) copy-start(bf16[64,2048]{1,0:T(8,128)(2,1)} %param.61) | copy-start | bytes 786436
  37.8 79.7 %all-to-all-start = ((bf16[32,8,4,1024]{3,2,1,0:T(4,128)(2,1)}), bf16[32,8,4,1024]{3,2,1,0:T(4,128)(2,1)}, u32[]{:S(2)}, u32[]{:S(2)}) async-start(bf16[32,8,4,1024]{3,2,1,0:T(4,128)(2,1)} %bitcast.506), calls=%async_computation | async-start | bytes 4194304 | tf_op jit(solution)/shard_map/all_to_all | solution.py:321
  45.3 57.7 %copy-start.77 = (bf16[64,2048]{1,0:T(8,128)(2,1)S(1)}, bf16[64,2048]{1,0:T(8,128)(2,1)}, u32[]{:S(2)}) copy-start(bf16[64,2048]{1,0:T(8,128)(2,1)} %param.68) | copy-start | bytes 786436
  45.3 733.1 %all-gather.13.cloned.1.call-start = ((), (), s32[]{:S(2)}) async-start(), calls=%async_computation.15 | async-start | bytes 12582912 | tf_op jit(solution)/shard_map/all_gather | solution.py:264
  47.2 674.4 %copy-start.82 = (f32[1536]{0:T(1024)}, f32[1536]{0:T(1024)S(1)}, u32[]{:S(2)}) copy-start(f32[1536]{0:T(1024)S(1)} %mul.1108) | copy-start | bytes 18436
  87.9 103.8 %copy-start.107 = (s32[48]{0:T(128)}, s32[48]{0:T(128)S(1)}, u32[]{:S(2)}) copy-start(s32[48]{0:T(128)S(1)} %and_select_fusion) | copy-start | bytes 580
  88.1 103.7 %copy-start.45 = (s32[1024]{0:T(1024)}, s32[1024]{0:T(1024)S(1)}, u32[]{:S(2)}) copy-start(s32[1024]{0:T(1024)S(1)} %get-tuple-element.1517) | copy-start | bytes 12292
  117.5 49.5 %copy-start.89 = (s32[48]{0:T(128)}, s32[48]{0:T(128)S(1)}, u32[]{:S(2)}) copy-start(s32[48]{0:T(128)S(1)} %fusion.235) | copy-start | bytes 580
  117.6 61.0 %all-to-all-start.2 = ((bf16[32,8,4,1024]{3,2,1,0:T(4,128)(2,1)}), bf16[32,8,4,1024]{3,2,1,0:T(4,128)(2,1)}, u32[]{:S(2)}, u32[]{:S(2)}) async-start(bf16[32,8,4,1024]{3,2,1,0:T(4,128)(2,1)} %bitcast.666), calls=%async_computation.2 | async-start | bytes 4194304 | tf_op jit(solution)/shard_map/all_to_all | solution.py:322
  124.4 1438.1 %reduce-scatter.17.cloned.1.call-start = ((), (), s32[]{:S(2)}) async-start(), calls=%async_computation.22 | async-start | bytes 393216 | tf_op jit(solution)/shard_map/reduce_scatter | solution.py:288
  153.9 35.8 %copy-start.59 = (bf16[48,1024]{1,0:T(8,128)(2,1)}, bf16[48,1024]{1,0:T(8,128)(2,1)S(1)}, u32[]{:S(2)}) copy-start(bf16[48,1024]{1,0:T(8,128)(2,1)S(1)} %convolution_convert_fusion.15) | copy-start | bytes 294916
  155.8 35.9 %copy-start.63 = (bf16[48,1024]{1,0:T(8,128)(2,1)}, bf16[48,1024]{1,0:T(8,128)(2,1)S(1)}, u32[]{:S(2)}) copy-start(bf16[48,1024]{1,0:T(8,128)(2,1)S(1)} %convolution_convert_fusion.12) | copy-start | bytes 294916
  157.1 573.3 %copy-start.33 = (f32[1024,32]{0,1:T(8,128)}, f32[1024,32]{0,1:T(8,128)S(1)}, u32[]{:S(2)}) copy-start(f32[1024,32]{0,1:T(8,128)S(1)} %get-tuple-element.1685) | copy-start | bytes 393220
  164.1 133.4 %copy-start.31 = (bf16[48,4120]{1,0:T(8,128)(2,1)}, bf16[48,4120]{1,0:T(8,128)(2,1)S(1)}, u32[]{:S(2)}) copy-start(bf16[48,4120]{1,0:T(8,128)(2,1)S(1)} %convolution_convert_fusion.1) | copy-start | bytes 1186564
  191.8 105.7 %copy-start.48 = (bf16[1024,48]{0,1:T(8,128)(2,1)}, bf16[1024,48]{0,1:T(8,128)(2,1)S(1)}, u32[]{:S(2)}) copy-start(bf16[1024,48]{0,1:T(8,128)(2,1)S(1)} %fusion.192) | copy-start | bytes 294916
  733.3 18.7 %copy-start.78 = (f32[2,4,512]{2,1,0:T(4,128)}, f32[2,4,512]{2,1,0:T(4,128)S(1)}, u32[]{:S(2)}) copy-start(f32[2,4,512]{2,1,0:T(4,128)S(1)} %get-tuple-element.1698) | copy-start | bytes 49156
  734.6 17.5 copy-start.99
  742.2 14.9 copy-start.80
  742.8 22.2 %copy-start.35 = (bf16[1024,1536]{0,1:T(8,128)(2,1)}, bf16[1024,1536]{0,1:T(8,128)(2,1)S(1)}, u32[]{:S(2)}) copy-start(bf16[1024,1536]{0,1:T(8,128)(2,1)S(1)} %multiply_convert_fusion.1) | copy-start | bytes 9437188
  896.7 665.9 %reduce-scatter.15.cloned.1.call-start = ((), (), s32[]{:S(2)}) async-start(), calls=%async_computation.21 | async-start | bytes 393216 | tf_op jit(solution)/shard_map/reduce_scatter | solution.py:285
  897.9 23.3 %slice-start = ((s8[16777216]{0:T(1024)(128)(4,1)}), s8[4194304]{0:T(1024)(128)(4,1)S(1)}, s32[]{:S(2)}) async-start(s8[16777216]{0:T(1024)(128)(4,1)} %bitcast.646), calls=%async_computation.26 | async-start | bytes 8388608
  897.9 23.3 %slice-start.1 = ((s8[16777216]{0:T(1024)(128)(4,1)}), s8[4194304]{0:T(1024)(128)(4,1)S(1)}, s32[]{:S(2)}) async-start(s8[16777216]{0:T(1024)(128)(4,1)} %bitcast.646), calls=%async_computation.27 | async-start | bytes 8388608
  897.9 23.3 %slice-start.2 = ((s8[16777216]{0:T(1024)(128)(4,1)}), s8[4194304]{0:T(1024)(128)(4,1)S(1)}, s32[]{:S(2)}) async-start(s8[16777216]{0:T(1024)(128)(4,1)} %bitcast.646), calls=%async_computation.28 | async-start | bytes 8388608
  1444.5 17.5 copy-start.56
  1444.5 18.2 %copy-start.32 = (bf16[48,4120]{1,0:T(8,128)(2,1)S(1)}, bf16[48,4120]{1,0:T(8,128)(2,1)}, u32[]{:S(2)}) copy-start(bf16[48,4120]{1,0:T(8,128)(2,1)} %copy-done.31) | copy-start | bytes 1186564
  1444.5 18.2 %copy-start.47 = (s32[1024]{0:T(1024)S(1)}, s32[1024]{0:T(1024)}, u32[]{:S(2)}) copy-start(s32[1024]{0:T(1024)} %copy-done.45) | copy-start | bytes 12292
  1444.5 18.2 %copy-start.109 = (s32[48]{0:T(128)S(1)}, s32[48]{0:T(128)}, u32[]{:S(2)}) copy-start(s32[48]{0:T(128)} %copy-done.107) | copy-start | bytes 580
  1467.7 15.0 copy-start.60
  1467.7 15.0 copy-start.127
  1467.7 94.8 %reduce-scatter.9.cloned.1.call-start = ((), (), s32[]{:S(2)}) async-start(), calls=%async_computation.18 | async-start | bytes 393216 | tf_op jit(solution)/shard_map/reduce_scatter | solution.py:276
  1467.8 14.9 copy-start.6
  1497.0 53.5 %all-to-all-start.3 = ((bf16[1,8,128,1024]{3,1,0,2:T(8,128)(2,1)}), bf16[1,8,128,1024]{3,1,0,2:T(8,128)(2,1)}, u32[]{:S(2)}, u32[]{:S(2)}) async-start(bf16[1,8,128,1024]{3,1,0,2:T(8,128)(2,1)} %copy.331), calls=%async_computation.3 | async-start | bytes 4194304 | tf_op jit(solution)/shard_map/all_to_all | solution.py:347
  1501.8 60.8 %reduce-scatter.23.cloned.1.call-start = ((), (), s32[]{:S(2)}) async-start(), calls=%async_computation.25 | async-start | bytes 393216 | tf_op jit(solution)/shard_map/reduce_scatter | solution.py:297
  1503.5 14.9 copy-start.73
  1503.6 59.0 %reduce-scatter.13.cloned.1.call-start = ((), (), s32[]{:S(2)}) async-start(), calls=%async_computation.20 | async-start | bytes 786432 | tf_op jit(solution)/shard_map/reduce_scatter | solution.py:282
  1518.4 54.8 %reduce-scatter.21.cloned.1.call-start = ((), (), s32[]{:S(2)}) async-start(), calls=%async_computation.24 | async-start | bytes 786432 | tf_op jit(solution)/shard_map/reduce_scatter | solution.py:294
  1523.0 82.2 %reduce-scatter.19.cloned.1.call-start = ((), (), s32[]{:S(2)}) async-start(), calls=%async_computation.23 | async-start | bytes 1572864 | tf_op jit(solution)/shard_map/reduce_scatter | solution.py:291
  1550.5 196.5 %all-to-all-start.1 = ((bf16[1,8,128,1024]{3,1,0,2:T(8,128)(2,1)}), bf16[1,8,128,1024]{3,1,0,2:T(8,128)(2,1)S(1)}, u32[]{:S(2)}, u32[]{:S(2)}) async-start(bf16[1,8,128,1024]{3,1,0,2:T(8,128)(2,1)} %copy.302), calls=%async_computation.1 | async-start | bytes 4194304 | tf_op jit(solution)/shard_map/all_to_all | solution.py:340
  1554.2 73.1 %reduce-scatter.11.cloned.1.call-start = ((), (), s32[]{:S(2)}) async-start(), calls=%async_computation.19 | async-start | bytes 1622016 | tf_op jit(solution)/shard_map/reduce_scatter | solution.py:279
  (132 other events, 941.8 us)
Sparse Core Ops, SparseCore 0:
  9.6 23.9 all-gather.14
  35.2 43.8 all-gather.8
  80.6 92.8 all-gather.16
  174.9 107.0 all-gather.6
  283.4 56.7 all-gather.10
  341.6 103.9 all-gather.12
  896.8 11.7 reduce-scatter.16
  1467.8 11.7 reduce-scatter.14
  1487.4 11.7 reduce-scatter.8
  1505.2 15.4 reduce-scatter.22
  1523.5 20.7 reduce-scatter.12
  1547.1 26.0 reduce-scatter.20
  1576.0 29.1 reduce-scatter.18
  1607.9 19.2 reduce-scatter.10
where the time goes:
time: 1800 us; the launch traced here: 1770 us
  local copies, waits for them, and re-layouts  570 us (32%)
  matrix products  539 us (30%)
  other arithmetic  271 us (15%)
  blocking collectives  191 us (11%)
  waiting for transfers between devices  154 us (9%)
  starting transfers between devices  23.3 us (1%)
    dynamic_update_slice x88, local copies, waits for them, and re-layouts, state_scan(): lax.scan(advance, initial, (inputs_x, vector_b, vector_c, delta, restart))  368 us
    dot_general x24, matrix products, advance(): local = jnp.einsum('ijh,jhp->ihp', weights, block_x, precision=HIGH)  99.9 us
    psum x1, blocking collectives, settle_all(): lax.psum((owned[0], owned[1], owned[2], owned[3], owned[4], owned[5], own...  98.3 us
    all_gather x4, waiting for transfers between devices, fetch(): lax.all_gather(weight, 'shard', axis=0, tiled=True)  78 us
    dynamic_update_slice x40, other arithmetic, state_scan(): lax.scan(advance, initial, (inputs_x, vector_b, vector_c, delta, restart))  70.6 us
    dot_general x24, matrix products, advance(): jnp.einsum('in,hpn->ihp', block_c, state, precision=HIGH)  65 us
    dot_general x24, matrix products, advance(): jnp.einsum('jh,jhp,jn->hpn', tail, block_x, block_b, precision=HIGH)  59.5 us
    all_gather x4, blocking collectives, fetch(): lax.all_gather(lower, 'shard', axis=0, tiled=True)  57.3 us
  transfers between devices with their start and end apart: 18, of which 5 were waited for; matrix products, arithmetic and copies ran while one was open for 70% of the time, Pallas kernels for 0%

commit v1 on v0

v1 whole, which is shorter than its diff:
```python
import functools

import jax
import jax.numpy as jnp
from jax import lax
from jax.experimental import pallas as pl
from jax.experimental.pallas import tpu as pltpu
from jax.sharding import PartitionSpec as P

SSM_HEADS = 24
STATE = 128
SPAN = 128
DSSM = 1536
XBC = 1792
CONV = 4
EPS = 1e-05
NEG = -1e30
HIGH = lax.Precision.HIGHEST
F32 = jnp.float32
BF16 = jnp.bfloat16
PAIRS = DSSM // 128
HALO = 8
GATE_C = slice(0, 1536)
QUERY_C = slice(1536, 2048)
KV_C = slice(2048, 2304)
CONV_C = slice(2304, 4096)
STEP_C = slice(4096, 4224)
UNITED = 4224


def dot_nn(a, b):
    return lax.dot_general(a, b, (((1,), (0,)), ((), ())), preferred_element_type=F32)


def dot_nt(a, b):
    return lax.dot_general(a, b, (((1,), (1,)), ((), ())), preferred_element_type=F32)


def dot_exact(a, b):
    return lax.dot_general(
        a, b, (((1,), (0,)), ((), ())), precision=HIGH, preferred_element_type=F32
    )


def split_two(value):
    high = value.astype(BF16)
    return high, (value - high.astype(F32)).astype(BF16)


def spread(value, wide):
    high, rest = split_two(value)
    return dot_nn(jnp.concatenate([high, rest], axis=1), wide)


def gather_heads(value, wide):
    high, rest = split_two(value)
    narrow = wide[:SPAN]
    return dot_nt(high, narrow) + dot_nt(rest, narrow)


def softplus(value):
    return jnp.maximum(value, 0.0) + jnp.log1p(jnp.exp(-jnp.abs(value)))


def sigmoid(value):
    return 1.0 / (1.0 + jnp.exp(-value))


def iota2(dim):
    return lax.broadcasted_iota(jnp.int32, (SPAN, SPAN), dim)


def strip(number):
    return slice(number * 128, (number + 1) * 128)


def filtered(ext, taps_ref, bias_ref, cols):
    total = bias_ref[0:1, cols]
    for lag in range(CONV):
        total = total + taps_ref[lag : lag + 1, cols] * ext[HALO - lag : HALO - lag + SPAN, cols]
    return total


def mamba_forward_kernel(
    restart_ref,
    united_ref,
    attended_ref,
    taps_ref,
    bias_ref,
    step_bias_ref,
    decay_ref,
    skip_ref,
    gain_ref,
    wide_ref,
    out_ref,
    scan_ref,
    start_ref,
    ext,
    state,
    delta_w,
    grow_w,
    tail_w,
    gated_s,
):
    chunk = pl.program_id(0)
    gate_ref = united_ref.at[:, GATE_C]
    conv_ref = united_ref.at[:, CONV_C]
    step_ref = united_ref.at[:, STEP_C]
    out_ref[:, DSSM:] = attended_ref[...]

    @pl.when(restart_ref[chunk] == 1)
    def _():
        state[...] = jnp.zeros_like(state)
        ext[0:HALO, :] = jnp.zeros((HALO, XBC), F32)

    ext[HALO:, :] = conv_ref[...]
    start_ref[0] = state[...]

    step = step_ref[...] + step_bias_ref[0:1, :]
    delta = softplus(step)
    slopes = -delta * decay_ref[0:1, :]
    lower = iota2(0) >= iota2(1)
    running = dot_exact(lower.astype(F32), slopes)
    running_t = running.T
    delta_w[...] = spread(delta, wide_ref[...])
    grow_w[...] = spread(jnp.exp(running), wide_ref[...])
    tail_w[...] = spread(jnp.exp(running[SPAN - 1 :] - running), wide_ref[...])

    def convolved(cols):
        summed = filtered(ext, taps_ref, bias_ref, cols)
        return summed * sigmoid(summed)

    vec_b = convolved(slice(DSSM, DSSM + STATE))
    vec_c = convolved(slice(DSSM + STATE, XBC))
    inner = lax.dot_general(
        vec_c, vec_b, (((1,), (1,)), ((), ())), precision=HIGH, preferred_element_type=F32
    )
    low_c = vec_c.astype(BF16)
    low_bt = vec_b.T.astype(BF16)
    left = iota2(1) < 64
    squares = jnp.zeros((SPAN, SPAN), F32)
    for pair in range(PAIRS):
        cols = strip(pair)
        xs = convolved(cols)
        xd = xs * delta_w[:, cols]
        weights = []
        for head in (2 * pair, 2 * pair + 1):
            gap = running[:, head : head + 1] - running_t[head : head + 1, :]
            decays = jnp.exp(jnp.where(lower, gap, NEG))
            weights.append((inner * decays).astype(BF16))
        stacked = jnp.concatenate(
            [jnp.where(left, xd, 0.0).astype(BF16), jnp.where(left, 0.0, xd).astype(BF16)], axis=0
        )
        local = dot_nn(jnp.concatenate(weights, axis=1), stacked)
        before = state[:, cols]
        scan = local + grow_w[:, cols] * dot_nn(low_c, before.astype(BF16))
        scan_ref[:, cols] = scan
        state[:, cols] = grow_w[SPAN - 1 : SPAN, cols] * before + dot_nn(
            low_bt, (tail_w[:, cols] * xd).astype(BF16)
        )
        gate = gate_ref[:, cols]
        gated = (scan + skip_ref[0:1, cols] * xs) * (gate * sigmoid(gate))
        gated_s[:, cols] = gated
        squares = squares + gated * gated
    scale = lax.rsqrt(jnp.sum(squares, axis=1, keepdims=True) * (1.0 / DSSM) + EPS)
    for pair in range(PAIRS):
        cols = strip(pair)
        out_ref[:, cols] = (gated_s[:, cols] * scale * gain_ref[0:1, cols]).astype(BF16)
    ext[0:HALO, :] = ext[SPAN : SPAN + HALO, :]


def mamba_backward_kernel(
    restart_ref,
    united_ref,
    above_ref,
    scan_ref,
    start_ref,
    grad_ref,
    dquery_ref,
    dkv_ref,
    taps_ref,
    bias_ref,
    step_bias_ref,
    decay_ref,
    skip_ref,
    gain_ref,
    wide_ref,
    dunited_ref,
    ext,
    back,
    dstate,
    delta_w,
    grow_w,
    tail_w,
    xs_s,
    dscan_s,
    sum_s,
    cross_s,
    gain_s,
):
    gate_ref = united_ref.at[:, GATE_C]
    conv_ref = united_ref.at[:, CONV_C]
    step_ref = united_ref.at[:, STEP_C]
    before_ref = above_ref.at[:, CONV_C]
    dgate_ref = dunited_ref.at[:, GATE_C]
    dconv_ref = dunited_ref.at[:, CONV_C]
    dstep_ref = dunited_ref.at[:, STEP_C]
    dunited_ref[:, QUERY_C] = dquery_ref[...]
    dunited_ref[:, KV_C] = dkv_ref[...]
    chunks = pl.num_programs(0)
    chunk = chunks - 1 - pl.program_id(0)
    following = jnp.minimum(chunk + 1, chunks - 1)

    @pl.when((chunk == chunks - 1) | (restart_ref[following] == 1))
    def _():
        dstate[...] = jnp.zeros_like(dstate)
        back[SPAN:, :] = jnp.zeros((HALO, XBC), F32)

    fresh = restart_ref[chunk] == 1
    ext[0:HALO, :] = jnp.where(fresh, 0.0, before_ref[...])
    ext[HALO:, :] = conv_ref[...]

    step = step_ref[...] + step_bias_ref[0:1, :]
    delta = softplus(step)
    slopes = -delta * decay_ref[0:1, :]
    lower = iota2(0) >= iota2(1)
    upper = iota2(0) <= iota2(1)
    running = dot_exact(lower.astype(F32), slopes)
    running_t = running.T
    delta_w[...] = spread(delta, wide_ref[...])
    grow_w[...] = spread(jnp.exp(running), wide_ref[...])
    tail_w[...] = spread(jnp.exp(running[SPAN - 1 :] - running), wide_ref[...])

    def convolved(cols):
        summed = filtered(ext, taps_ref, bias_ref, cols)
        ratio = sigmoid(summed)
        return summed * ratio, ratio * (1.0 + summed * (1.0 - ratio))

    vec_b, slope_b = convolved(slice(DSSM, DSSM + STATE))
    vec_c, slope_c = convolved(slice(DSSM + STATE, XBC))
    inner_t = lax.dot_general(
        vec_b, vec_c, (((1,), (1,)), ((), ())), precision=HIGH, preferred_element_type=F32
    )
    low_b = vec_b.astype(BF16)
    low_c = vec_c.astype(BF16)
    low_ct = vec_c.T.astype(BF16)
    left = iota2(1) < 64

    squares = jnp.zeros((SPAN, SPAN), F32)
    mixed = jnp.zeros((SPAN, SPAN), F32)
    for pair in range(PAIRS):
        cols = strip(pair)
        xs, slope = convolved(cols)
        xs_s[:, cols] = xs
        back[0:SPAN, cols] = slope
        gate = gate_ref[:, cols]
        ratio = sigmoid(gate)
        ssm = scan_ref[:, cols] + skip_ref[0:1, cols] * xs
        gated = ssm * (gate * ratio)
        dmamba = grad_ref[:, cols] * gain_ref[0:1, cols]
        squares = squares + gated * gated
        mixed = mixed + gated * dmamba
    scale = lax.rsqrt(jnp.sum(squares, axis=1, keepdims=True) * (1.0 / DSSM) + EPS)
    pull = scale * scale * scale * (jnp.sum(mixed, axis=1, keepdims=True) * (1.0 / DSSM))

    dinner_t = jnp.zeros((SPAN, SPAN), F32)
    dvec_b = jnp.zeros((SPAN, STATE), F32)
    dvec_c = jnp.zeros((SPAN, STATE), F32)
    for pair in range(PAIRS):
        cols = strip(pair)
        xs = xs_s[:, cols]
        gate = gate_ref[:, cols]
        ratio = sigmoid(gate)
        lit = gate * ratio
        scan = scan_ref[:, cols]
        ssm = scan + skip_ref[0:1, cols] * xs
        gated = ssm * lit
        dgated = scale * (grad_ref[:, cols] * gain_ref[0:1, cols]) - pull * gated
        dgate_ref[:, cols] = (dgated * ssm * (ratio * (1.0 + gate * (1.0 - ratio)))).astype(BF16)
        dscan = dgated * lit
        low_dy = dscan.astype(BF16)
        delta_c = delta_w[:, cols]
        xd = xs * delta_c
        low_xd = xd.astype(BF16)
        xd_both = jnp.concatenate(
            [jnp.where(left, xd, 0.0).astype(BF16), jnp.where(left, 0.0, xd).astype(BF16)], axis=0
        )
        dy_both = jnp.concatenate(
            [jnp.where(left, dscan, 0.0).astype(BF16), jnp.where(left, 0.0, dscan).astype(BF16)],
            axis=0,
        )
        dweights = dot_nt(xd_both, low_dy)
        weights = []
        for place, head in enumerate((2 * pair, 2 * pair + 1)):
            gap = running_t[head : head + 1, :] - running[:, head : head + 1]
            decays = jnp.exp(jnp.where(upper, gap, NEG))
            weights.append((inner_t * decays).astype(BF16))
            dinner_t = dinner_t + dweights[place * SPAN : (place + 1) * SPAN] * decays
        dxd_local = dot_nn(jnp.concatenate(weights, axis=1), dy_both)
        after = dstate[:, cols]
        low_after = after.astype(BF16)
        start = start_ref[0, :, cols]
        tail_c = tail_w[:, cols]
        grow_c = grow_w[:, cols]
        grow_last = grow_w[SPAN - 1 : SPAN, cols]
        dxd_state = tail_c * dot_nn(low_b, low_after)
        dxd = dxd_local + dxd_state
        dvec_b = dvec_b + dot_nt((tail_c * xd).astype(BF16), low_after)
        low_edy = (grow_c * dscan).astype(BF16)
        dvec_c = dvec_c + dot_nt(low_edy, start.astype(BF16))
        dstate[:, cols] = grow_last * after + dot_nn(low_ct, low_edy)
        wide_xd = low_xd.astype(F32)
        sum_s[:, cols] = low_dy.astype(F32) * scan - wide_xd * dxd
        cross_s[:, cols] = xs * dxd
        gain_s[0:8, cols] = jnp.broadcast_to(
            grow_last * jnp.sum(after * start, axis=0, keepdims=True)
            + jnp.sum(wide_xd * dxd_state, axis=0, keepdims=True),
            (8, 128),
        )
        dxs = skip_ref[0:1, cols] * dscan + delta_c * dxd
        back[0:SPAN, cols] = dxs * back[0:SPAN, cols]
    dvec_b = dvec_b + dot_nn(dinner_t.astype(BF16), low_c)
    dvec_c = dvec_c + dot_nn(dinner_t.T.astype(BF16), low_b)
    back[0:SPAN, DSSM : DSSM + STATE] = dvec_b * slope_b
    back[0:SPAN, DSSM + STATE :] = dvec_c * slope_c

    last = (iota2(0) == SPAN - 1).astype(F32)
    drunning = gather_heads(sum_s[...], wide_ref[...]) + last * gather_heads(
        gain_s[...], wide_ref[...]
    )[0:1, :]
    dslopes = dot_exact(upper.astype(F32), drunning)
    ddelta = gather_heads(cross_s[...], wide_ref[...]) - decay_ref[0:1, :] * dslopes
    dstep_ref[...] = (ddelta * sigmoid(step)).astype(BF16)

    for number in range(XBC // 128):
        cols = strip(number)
        total = taps_ref[0:1, cols] * back[0:SPAN, cols]
        for lag in range(1, CONV):
            total = total + taps_ref[lag : lag + 1, cols] * back[lag : lag + SPAN, cols]
        dconv_ref[:, cols] = total.astype(BF16)
    back[SPAN:, :] = back[0:HALO, :]


def spread_matrix():
    rows = jnp.arange(2 * SPAN, dtype=jnp.int32)[:, None] % SPAN
    cols = jnp.arange(DSSM, dtype=jnp.int32)[None, :] // 64
    return (rows == cols).astype(BF16)


def pad_row(value, width):
    return jnp.pad(value, (0, width - value.shape[0]))[None, :]


def fixed(shape):
    return pl.BlockSpec(shape, lambda *_: (0,) * len(shape))


def ssm_params(filter_taps, filter_bias, step_bias, decay_rate, skip_gain, state_gain):
    return (
        filter_taps,
        filter_bias[None, :],
        pad_row(step_bias, SPAN),
        pad_row(decay_rate, SPAN),
        jnp.repeat(skip_gain, 64)[None, :],
        state_gain[None, :],
        spread_matrix(),
    )


PARAM_SPECS = [
    fixed((CONV, XBC)),
    fixed((1, XBC)),
    fixed((1, SPAN)),
    fixed((1, SPAN)),
    fixed((1, DSSM)),
    fixed((1, DSSM)),
    fixed((2 * SPAN, DSSM)),
]


def mamba_forward(united, attended, restart, params):
    rows = united.shape[0]
    chunks = rows // SPAN

    def at(width):
        return pl.BlockSpec((SPAN, width), lambda i, *_: (i, 0))

    wide = pltpu.VMEM((SPAN, DSSM), F32)
    return pl.pallas_call(
        mamba_forward_kernel,
        grid_spec=pltpu.PrefetchScalarGridSpec(
            num_scalar_prefetch=1,
            grid=(chunks,),
            in_specs=[at(UNITED), at(attended.shape[1])] + PARAM_SPECS,
            out_specs=[
                at(DSSM + attended.shape[1]),
                at(DSSM),
                pl.BlockSpec((1, STATE, DSSM), lambda i, *_: (i, 0, 0)),
            ],
            scratch_shapes=[pltpu.VMEM((SPAN + HALO, XBC), F32)] + [wide] * 5,
        ),
        out_shape=[
            jax.ShapeDtypeStruct((rows, DSSM + attended.shape[1]), BF16),
            jax.ShapeDtypeStruct((rows, DSSM), F32),
            jax.ShapeDtypeStruct((chunks, STATE, DSSM), F32),
        ],
        compiler_params=pltpu.CompilerParams(
            vmem_limit_bytes=48 << 20, dimension_semantics=("arbitrary",)
        ),
        cost_estimate=pl.CostEstimate(
            flops=20 * 10**9, bytes_accessed=50 * 10**6, transcendentals=0
        ),
        name="mamba_forward",
    )(restart, united, attended, *params)


def mamba_backward(united, scan, starts, grad, dquery, dkv, restart, params):
    rows = united.shape[0]
    chunks = rows // SPAN

    def at(width):
        return pl.BlockSpec((SPAN, width), lambda i, *_: (chunks - 1 - i, 0))

    wide = pltpu.VMEM((SPAN, DSSM), F32)
    tall = pltpu.VMEM((SPAN + HALO, XBC), F32)
    return pl.pallas_call(
        mamba_backward_kernel,
        grid_spec=pltpu.PrefetchScalarGridSpec(
            num_scalar_prefetch=1,
            grid=(chunks,),
            in_specs=[
                at(UNITED),
                pl.BlockSpec(
                    (HALO, UNITED),
                    lambda i, *_: (jnp.maximum((chunks - 1 - i) * (SPAN // HALO) - 1, 0), 0),
                ),
                at(DSSM),
                pl.BlockSpec((1, STATE, DSSM), lambda i, *_: (chunks - 1 - i, 0, 0)),
                at(DSSM),
                at(dquery.shape[1]),
                at(dkv.shape[1]),
            ]
            + PARAM_SPECS,
            out_specs=[at(UNITED)],
            scratch_shapes=[tall, tall] + [wide] * 8 + [pltpu.VMEM((8, DSSM), F32)],
        ),
        out_shape=[jax.ShapeDtypeStruct((rows, UNITED), BF16)],
        compiler_params=pltpu.CompilerParams(
            vmem_limit_bytes=48 << 20, dimension_semantics=("arbitrary",)
        ),
        cost_estimate=pl.CostEstimate(
            flops=45 * 10**9, bytes_accessed=60 * 10**6, transcendentals=0
        ),
        name="mamba_backward",
    )(restart, united, united, scan, starts, grad, dquery, dkv, *params)[0]


ATT_HEADS = 8
KV_HEADS = 2
HEAD_DIM = 64
MOST_P = 4
QUERY_W = ATT_HEADS * HEAD_DIM
KEY_W = KV_HEADS * HEAD_DIM
ROPE_BASE = 100000000000.0


def lanes_of(shape):
    return lax.broadcasted_iota(jnp.int32, shape, 1)


def turn(value, cosine, sines):
    early = (lanes_of(value.shape) // 32) % 2 == 0
    other = jnp.where(early, pltpu.roll(value, 96, 1), pltpu.roll(value, 32, 1))
    return value * cosine + other * sines


def doubled(value, head):
    left = lanes_of(value.shape) < 64
    moved = pltpu.roll(value, 64, 1)
    return jnp.where(left, value, moved) if head == 0 else jnp.where(left, moved, value)


def parted(value):
    left = lanes_of(value.shape) < 64
    return jnp.concatenate([jnp.where(left, value, 0.0), jnp.where(left, 0.0, value)], axis=0)


def joined_heads(value):
    return jnp.concatenate([value[:, :128], value[:, 128:]], axis=0).T


def causal_tail(scores, blocks):
    keys = lax.broadcasted_iota(jnp.int32, (SPAN, 2 * SPAN), 0)
    asks = lax.broadcasted_iota(jnp.int32, (SPAN, 2 * SPAN), 1) % SPAN
    tail = jnp.where(keys <= asks, scores[(blocks - 1) * SPAN :], NEG)
    if blocks == 1:
        return tail
    return jnp.concatenate([scores[: (blocks - 1) * SPAN], tail], axis=0)


def attend_forward_kernel(
    first_ref, query_ref, kv_ref, cos_ref, sin_ref, out_ref, log_ref, turned_ref, kv_low_ref, keys_s, vals_s
):
    block = pl.program_id(0)
    rows = kv_ref.shape[0]

    @pl.when(block == 0)
    def _():
        keys = turn(kv_ref[:, :KEY_W], cos_ref[...], sin_ref[...]).astype(BF16).astype(F32)
        vals = kv_ref[:, KEY_W:].astype(BF16)
        kv_low_ref[:, :KEY_W] = keys.astype(BF16)
        kv_low_ref[:, KEY_W:] = vals
        for head in range(KV_HEADS):
            keys_s[head] = doubled(keys, head).astype(BF16)
        for number in range(rows // SPAN):
            span = slice(number * SPAN, (number + 1) * SPAN)
            vals_s[:, span] = kv_ref[span, KEY_W:].T.astype(BF16)

    here = pl.ds(pl.multiple_of(block * SPAN, SPAN), SPAN)
    cosine = cos_ref[here, :]
    sines = sin_ref[here, :]
    first = first_ref[block]

    def body(blocks):
        window = pl.ds(pl.multiple_of(first * SPAN, SPAN), blocks * SPAN)
        for pair in range(ATT_HEADS // 2):
            cols = strip(pair)
            group = pair // 2
            turned = turn(query_ref[:, cols], cosine, sines).astype(BF16)
            scaled = turned.astype(F32) * (HEAD_DIM**-0.5)
            turned_ref[:, cols] = scaled.astype(BF16)
            scores = dot_nt(keys_s[group, window, :], parted(scaled).astype(BF16))
            scores = causal_tail(scores, blocks)
            peak = jnp.max(scores, axis=0, keepdims=True)
            raised = jnp.exp(scores - peak)
            total = jnp.sum(raised, axis=0, keepdims=True)
            probability = (raised * (1.0 / total)).astype(BF16)
            vals_t = vals_s[group * HEAD_DIM : (group + 1) * HEAD_DIM, window]
            out_ref[:, cols] = joined_heads(dot_nn(vals_t, probability)).astype(BF16)
            logs = peak + jnp.log(total)
            log_ref[0, 2 * pair : 2 * pair + 1, :] = logs[:, :SPAN]
            log_ref[0, 2 * pair + 1 : 2 * pair + 2, :] = logs[:, SPAN:]

    for blocks in range(1, MOST_P + 1):
        pl.when(block - first == blocks - 1)(functools.partial(body, blocks))


def attend_backward_kernel(
    first_ref,
    turned_ref,
    kv_low_ref,
    grad_ref,
    log_ref,
    cos_ref,
    sin_ref,
    dquery_ref,
    dkv_ref,
    keys_s,
    vals_s,
    keys_t,
    dkeys,
    dvals,
):
    block = pl.program_id(0)
    rows = kv_low_ref.shape[0]

    @pl.when(block == 0)
    def _():
        keys = kv_low_ref[:, :KEY_W].astype(F32)
        vals = kv_low_ref[:, KEY_W:].astype(F32)
        for head in range(KV_HEADS):
            keys_s[head] = doubled(keys, head).astype(BF16)
            vals_s[head] = doubled(vals, head).astype(BF16)
        for number in range(rows // SPAN):
            span = slice(number * SPAN, (number + 1) * SPAN)
            keys_t[:, span] = kv_low_ref[span, :KEY_W].astype(F32).T.astype(BF16)
        dkeys[...] = jnp.zeros_like(dkeys)
        dvals[...] = jnp.zeros_like(dvals)

    here = pl.ds(pl.multiple_of(block * SPAN, SPAN), SPAN)
    cosine = cos_ref[here, :]
    sines = -sin_ref[here, :]
    first = first_ref[block]

    def body(blocks):
        window = pl.ds(pl.multiple_of(first * SPAN, SPAN), blocks * SPAN)
        for pair in range(ATT_HEADS // 2):
            cols = strip(pair)
            group = pair // 2
            asks = parted(turned_ref[:, cols].astype(F32)).astype(BF16)
            grads = parted(grad_ref[:, cols].astype(F32)).astype(BF16)
            scores = causal_tail(dot_nt(keys_s[group, window, :], asks), blocks)
            logs = jnp.concatenate(
                [log_ref[0, 2 * pair : 2 * pair + 1, :], log_ref[0, 2 * pair + 1 : 2 * pair + 2, :]],
                axis=1,
            )
            probability = jnp.exp(scores - logs)
            dprob = dot_nt(vals_s[group, window, :], grads)
            inner = jnp.sum(probability * dprob, axis=0, keepdims=True)
            dscore = (probability * (dprob - inner)).astype(BF16)
            keys_g = keys_t[group * HEAD_DIM : (group + 1) * HEAD_DIM, window]
            dquery = joined_heads(dot_nn(keys_g, dscore)) * (HEAD_DIM**-0.5)
            dquery_ref[:, cols] = turn(dquery, cosine, sines).astype(BF16)
            dkeys[group, window, :] += dot_nn(dscore, asks)
            dvals[group, window, :] += dot_nn(probability.astype(BF16), grads)

    for blocks in range(1, MOST_P + 1):
        pl.when(block - first == blocks - 1)(functools.partial(body, blocks))

    @pl.when(block == pl.num_programs(0) - 1)
    def _():
        left = lanes_of((rows, KEY_W)) < 64

        def folded(total):
            sums = [total[head] + pltpu.roll(total[head], 64, 1) for head in range(KV_HEADS)]
            return jnp.where(left, sums[0], sums[1])

        dkv_ref[:, :KEY_W] = turn(folded(dkeys), cos_ref[...], -sin_ref[...]).astype(BF16)
        dkv_ref[:, KEY_W:] = folded(dvals).astype(BF16)


def rotation_tables(position):
    half = HEAD_DIM // 2
    frequency = ROPE_BASE ** (-2.0 * jnp.arange(half, dtype=F32) / HEAD_DIM)
    angles = position.astype(F32)[:, None] * frequency[None, :]
    cosine, sines = jnp.cos(angles), jnp.sin(angles)
    return (
        jnp.concatenate([cosine] * 4, axis=1),
        jnp.concatenate([-sines, sines, -sines, sines], axis=1),
    )


def attend_forward(united, cosine, sines, first):
    rows = united.shape[0]
    blocks = rows // SPAN
    at = pl.BlockSpec((SPAN, QUERY_W), lambda i, *_: (i, 0))
    query_at = pl.BlockSpec((SPAN, QUERY_W), lambda i, *_: (i, QUERY_C.start // QUERY_W))
    kv_at = pl.BlockSpec((rows, 2 * KEY_W), lambda i, *_: (0, KV_C.start // (2 * KEY_W)))
    return pl.pallas_call(
        attend_forward_kernel,
        grid_spec=pltpu.PrefetchScalarGridSpec(
            num_scalar_prefetch=1,
            grid=(blocks,),
            in_specs=[query_at, kv_at, fixed((rows, 128)), fixed((rows, 128))],
            out_specs=[
                at,
                pl.BlockSpec((1, ATT_HEADS, SPAN), lambda i, *_: (i, 0, 0)),
                at,
                fixed((rows, 2 * KEY_W)),
            ],
            scratch_shapes=[
                pltpu.VMEM((KV_HEADS, rows, 128), BF16),
                pltpu.VMEM((KEY_W, rows), BF16),
            ],
        ),
        out_shape=[
            jax.ShapeDtypeStruct((rows, QUERY_W), BF16),
            jax.ShapeDtypeStruct((blocks, ATT_HEADS, SPAN), F32),
            jax.ShapeDtypeStruct((rows, QUERY_W), BF16),
            jax.ShapeDtypeStruct((rows, 2 * KEY_W), BF16),
        ],
        compiler_params=pltpu.CompilerParams(
            vmem_limit_bytes=48 << 20, dimension_semantics=("arbitrary",)
        ),
        cost_estimate=pl.CostEstimate(
            flops=15 * 10**9, bytes_accessed=6 * 10**6, transcendentals=0
        ),
        name="attend_forward",
    )(first, united, united, cosine, sines)


def attend_backward(turned, kv_low, grad, logs, cosine, sines, first):
    rows = turned.shape[0]
    blocks = rows // SPAN
    at = pl.BlockSpec((SPAN, QUERY_W), lambda i, *_: (i, 0))
    return pl.pallas_call(
        attend_backward_kernel,
        grid_spec=pltpu.PrefetchScalarGridSpec(
            num_scalar_prefetch=1,
            grid=(blocks,),
            in_specs=[
                at,
                fixed((rows, 2 * KEY_W)),
                at,
                pl.BlockSpec((1, ATT_HEADS, SPAN), lambda i, *_: (i, 0, 0)),
                fixed((rows, 128)),
                fixed((rows, 128)),
            ],
            out_specs=[at, fixed((rows, 2 * KEY_W))],
            scratch_shapes=[
                pltpu.VMEM((KV_HEADS, rows, 128), BF16),
                pltpu.VMEM((KV_HEADS, rows, 128), BF16),
                pltpu.VMEM((KEY_W, rows), BF16),
                pltpu.VMEM((KV_HEADS, rows, 128), F32),
                pltpu.VMEM((KV_HEADS, rows, 128), F32),
            ],
        ),
        out_shape=[
            jax.ShapeDtypeStruct((rows, QUERY_W), BF16),
            jax.ShapeDtypeStruct((rows, 2 * KEY_W), BF16),
        ],
        compiler_params=pltpu.CompilerParams(
            vmem_limit_bytes=48 << 20, dimension_semantics=("arbitrary",)
        ),
        cost_estimate=pl.CostEstimate(
            flops=15 * 10**9, bytes_accessed=6 * 10**6, transcendentals=0
        ),
        name="attend_backward",
    )(first, turned, kv_low, grad, logs, cosine, sines)


RANKS = 128
ROW_BLOCK = 256
D = 1024
FF = 2048
MIX = 2048
QUARTERS = 4
ADAPT_SCALE = 0.5
COLUMN_STEP = 512
MIXER = (D, UNITED, 0)
MERGE = (MIX, D, D)
EXPAND = (D, 2 * FF, D + MIX)
REDUCE = (FF, D, 2 * D + MIX)
LOWER_W = 2 * D + MIX + FF
PIECES = 3 + 2 * QUARTERS
COPIES = 3 + 3 * QUARTERS


def weight_scratch(shape):
    return [
        pltpu.VMEM((shape[0], shape[1]), BF16),
        pltpu.VMEM((RANKS, shape[1]), BF16),
        pltpu.VMEM((RANKS, shape[0]), BF16),
        pltpu.SemaphoreType.DMA((COPIES,)),
    ]


def weight_copies(info_ref, shape, pieces, scratch):
    depth, _, column = shape
    own_w, own_u, own_l = pieces[:3]
    sent = pieces[3 : 3 + QUARTERS]
    sent_l = pieces[3 + QUARTERS :]
    weight, upper, lower, sems = scratch
    side = info_ref[0]
    columns = pl.ds(column, depth)

    def rows(start, count):
        return pl.ds(pl.multiple_of(start, 16), count)

    jobs = [
        (own_w, weight.at[rows(side * (depth // 2), depth // 2), :]),
        (own_u, upper.at[rows(side * (RANKS // 2), RANKS // 2), :]),
        (own_l.at[:, columns], lower.at[rows(side * (RANKS // 2), RANKS // 2), :]),
    ]
    part = depth // 8
    for number in range(QUARTERS):
        place = info_ref[1 + number]
        base = (1 - side) * (RANKS // 2) + place * 16
        jobs += [
            (
                sent[number].at[pl.ds(0, part), :],
                weight.at[rows((1 - side) * (depth // 2) + place * part, part), :],
            ),
            (sent[number].at[pl.ds(part, 16), :], upper.at[rows(base, 16), :]),
            (sent_l[number].at[:, columns], lower.at[rows(base, 16), :]),
        ]
    return [pltpu.make_async_copy(src, dst, sems.at[i]) for i, (src, dst) in enumerate(jobs)]


def at_first(action):
    pl.when(pl.program_id(0) == 0)(action)


def start_all(copies):
    for copy in copies:
        copy.start()


def wait_all(copies):
    for copy in copies:
        copy.wait()


def halved(value):
    return (value.astype(F32) * ADAPT_SCALE).astype(BF16)


def masked(value, mask):
    return (value * mask).astype(BF16)


def norm_scale(value):
    return lax.rsqrt(jnp.sum(value * value, axis=1, keepdims=True) * (1.0 / value.shape[1]) + EPS)


def norm_back(grad, value, gain):
    scale = norm_scale(value)
    pulled = grad * gain
    inner = jnp.sum(pulled * value, axis=1, keepdims=True) * (1.0 / value.shape[1])
    return scale * pulled - value * (scale * scale * scale * inner)


def dot_tn(a, b):
    return lax.dot_general(a, b, (((0,), (0,)), ((), ())), preferred_element_type=F32)


def columns_of(width):
    return [slice(at, min(at + COLUMN_STEP, width)) for at in range(0, width, COLUMN_STEP)]


def mixer_forward_kernel(info_ref, x_ref, mask_ref, gain_ref, *rest):
    pieces = rest[:PIECES]
    united_ref, hidden_ref, mid_ref = rest[PIECES : PIECES + 3]
    scratch = rest[PIECES + 3 :]
    weight, upper, lower, _ = scratch
    copies = weight_copies(info_ref, MIXER, pieces, scratch)
    at_first(lambda: start_all(copies))
    value = x_ref[...].astype(F32)
    hidden = (value * norm_scale(value) * gain_ref[0:1, :]).astype(BF16)
    hidden_ref[...] = hidden
    at_first(lambda: wait_all(copies))
    mid = masked(dot_nt(hidden, lower[...]), mask_ref[...].astype(F32))
    mid_ref[...] = mid
    half = halved(mid)
    for cols in columns_of(UNITED):
        united_ref[:, cols] = dot_nn(hidden, weight[:, cols]) + dot_nn(half, upper[:, cols])


def block_forward_kernel(info_ref, joined_ref, x_ref, mask_ref, gain_ref, *rest):
    merge_p, expand_p, reduce_p = (rest[i * PIECES : (i + 1) * PIECES] for i in range(3))
    rest = rest[3 * PIECES :]
    mixed_ref, middle_ref, second_ref, lit_ref, up_ref, mids_ref = rest[:6]
    merge_s, expand_s, reduce_s = (rest[6 + 4 * i : 10 + 4 * i] for i in range(3))
    active_s = rest[18]
    sets = [
        weight_copies(info_ref, shape, pieces, scratch)
        for shape, pieces, scratch in (
            (MERGE, merge_p, merge_s),
            (EXPAND, expand_p, expand_s),
            (REDUCE, reduce_p, reduce_s),
        )
    ]
    at_first(lambda: start_all(sum(sets, [])))
    mask = mask_ref[...].astype(F32)

    at_first(lambda: wait_all(sets[0]))
    weight, upper, lower, _ = merge_s
    joined = joined_ref[...]
    mid = masked(dot_nt(joined, lower[...]), mask)
    mids_ref[:, 0:RANKS] = mid
    middle = x_ref[...].astype(F32) + (
        dot_nn(joined, weight[...]) + dot_nn(halved(mid), upper[...])
    )
    middle_ref[...] = middle
    second = (middle * norm_scale(middle) * gain_ref[0:1, :]).astype(BF16)
    second_ref[...] = second

    at_first(lambda: wait_all(sets[1]))
    weight, upper, lower, _ = expand_s
    mid = masked(dot_nt(second, lower[...]), mask)
    mids_ref[:, RANKS : 2 * RANKS] = mid
    half = halved(mid)
    for cols in columns_of(FF):
        beside = slice(FF + cols.start, FF + cols.stop)
        lit = dot_nn(second, weight[:, cols]) + dot_nn(half, upper[:, cols])
        up = dot_nn(second, weight[:, beside]) + dot_nn(half, upper[:, beside])
        lit_ref[:, cols] = lit
        up_ref[:, cols] = up
        active_s[:, cols] = (lit * sigmoid(lit) * up).astype(BF16)

    at_first(lambda: wait_all(sets[2]))
    weight, upper, lower, _ = reduce_s
    active = active_s[...]
    mid = masked(dot_nt(active, lower[...]), mask)
    mids_ref[:, 2 * RANKS :] = mid
    mixed_ref[...] = (
        middle_ref[...] + (dot_nn(active, weight[...]) + dot_nn(halved(mid), upper[...]))
    ).astype(BF16)


MERGE_L, MERGE_U = slice(0, MIX), slice(MIX, MIX + D)
EXPAND_L, EXPAND_U = slice(MIX + D, MIX + 2 * D), slice(MIX + 2 * D, MIX + 2 * D + 2 * FF)
REDUCE_L = slice(MIX + 2 * D + 2 * FF, MIX + 2 * D + 3 * FF)
REDUCE_U = slice(MIX + 2 * D + 3 * FF, MIX + 3 * D + 3 * FF)
GRADS_W = MIX + 3 * D + 3 * FF


def add_factor_grads(total, lower_cols, upper_cols, grad_mid, hidden, mid, grad):
    gm_t = grad_mid.astype(F32).T.astype(BF16)
    mid_t = (mid.astype(F32) * ADAPT_SCALE).T.astype(BF16)
    total[:, lower_cols] += dot_nn(gm_t, hidden)
    total[:, upper_cols] += dot_nn(mid_t, grad)


def block_backward_kernel(
    info_ref,
    grad_ref,
    joined_ref,
    middle_ref,
    second_ref,
    lit_ref,
    up_ref,
    mids_ref,
    mask_ref,
    gain_ref,
    *rest,
):
    reduce_p, expand_p, merge_p = (rest[i * PIECES : (i + 1) * PIECES] for i in range(3))
    rest = rest[3 * PIECES :]
    dmamba_ref, dattended_ref, dmiddle_ref, grads_ref = rest[:4]
    reduce_s, expand_s, merge_s = (rest[4 + 4 * i : 8 + 4 * i] for i in range(3))
    active_s, dlit_s, total = rest[16:]
    sets = [
        weight_copies(info_ref, shape, pieces, scratch)
        for shape, pieces, scratch in (
            (REDUCE, reduce_p, reduce_s),
            (EXPAND, expand_p, expand_s),
            (MERGE, merge_p, merge_s),
        )
    ]

    def begin():
        for copies in sets:
            start_all(copies)
        total[...] = jnp.zeros_like(total)

    at_first(begin)
    mask = mask_ref[...].astype(F32)

    at_first(lambda: wait_all(sets[0]))
    weight, upper, lower, _ = reduce_s
    grad = grad_ref[...]
    grad_mid = masked(ADAPT_SCALE * dot_nt(grad, upper[...]), mask)
    for cols in columns_of(FF):
        beside = slice(FF + cols.start, FF + cols.stop)
        dactive = dot_nt(grad, weight[cols, :]) + dot_nn(grad_mid, lower[:, cols])
        lit = lit_ref[:, cols]
        up = up_ref[:, cols]
        ratio = sigmoid(lit)
        glow = lit * ratio
        active_s[:, cols] = (glow * up).astype(BF16)
        dlit_s[:, cols] = (dactive * up * (ratio * (1.0 + lit * (1.0 - ratio)))).astype(BF16)
        dlit_s[:, beside] = (dactive * glow).astype(BF16)
    add_factor_grads(
        total, REDUCE_L, REDUCE_U, grad_mid, active_s[...], mids_ref[:, 2 * RANKS :], grad
    )

    at_first(lambda: wait_all(sets[1]))
    weight, upper, lower, _ = expand_s
    dexpanded = dlit_s[...]
    grad_mid = masked(ADAPT_SCALE * dot_nt(dexpanded, upper[...]), mask)
    dsecond = dot_nt(dexpanded, weight[...]) + dot_nn(grad_mid, lower[...])
    dmiddle = grad.astype(F32) + norm_back(dsecond, middle_ref[...], gain_ref[0:1, :])
    dmiddle_ref[...] = dmiddle
    add_factor_grads(
        total,
        EXPAND_L,
        EXPAND_U,
        grad_mid,
        second_ref[...],
        mids_ref[:, RANKS : 2 * RANKS],
        dexpanded,
    )

    at_first(lambda: wait_all(sets[2]))
    weight, upper, lower, _ = merge_s
    grad = dmiddle_ref[...].astype(BF16)
    grad_mid = masked(ADAPT_SCALE * dot_nt(grad, upper[...]), mask)
    for cols in columns_of(MIX):
        djoined = dot_nt(grad, weight[cols, :]) + dot_nn(grad_mid, lower[:, cols])
        if cols.start < DSSM:
            dmamba_ref[:, cols] = djoined
        else:
            dattended_ref[...] = djoined.astype(BF16)
    add_factor_grads(
        total, MERGE_L, MERGE_U, grad_mid, joined_ref[...], mids_ref[:, 0:RANKS], grad
    )

    @pl.when(pl.program_id(0) == pl.num_programs(0) - 1)
    def _():
        grads_ref[...] = total[...].astype(BF16)


MIXER_GRADS_W = D + UNITED + 128


def mixer_backward_kernel(
    info_ref, grad_ref, hidden_ref, x_ref, dmiddle_ref, mid_ref, mask_ref, gain_ref, *rest
):
    pieces = rest[:PIECES]
    out_ref, grads_ref = rest[PIECES : PIECES + 2]
    scratch = rest[PIECES + 2 : PIECES + 6]
    total = rest[PIECES + 6]
    weight, upper, lower, _ = scratch
    copies = weight_copies(info_ref, MIXER, pieces, scratch)

    def begin():
        start_all(copies)
        total[...] = jnp.zeros_like(total)

    at_first(begin)
    at_first(lambda: wait_all(copies))
    grad = grad_ref[...]
    grad_mid = masked(ADAPT_SCALE * dot_nt(grad, upper[...]), mask_ref[...].astype(F32))
    dhidden = dot_nt(grad, weight[...]) + dot_nn(grad_mid, lower[...])
    value = x_ref[...].astype(F32)
    out_ref[...] = (dmiddle_ref[...] + norm_back(dhidden, value, gain_ref[0:1, :])).astype(BF16)
    add_factor_grads(
        total,
        slice(0, D),
        slice(D, D + UNITED),
        grad_mid,
        hidden_ref[...],
        mid_ref[...],
        grad,
    )

    @pl.when(pl.program_id(0) == pl.num_programs(0) - 1)
    def _():
        grads_ref[...] = total[...].astype(BF16)


def row_call(kernel, rows, ins, fixed_ins, raw, outs, fixed_outs, scratch, info, name, flops, moved):
    def at(width):
        return pl.BlockSpec((ROW_BLOCK, width), lambda i, *_: (i, 0))

    return pl.pallas_call(
        kernel,
        grid_spec=pltpu.PrefetchScalarGridSpec(
            num_scalar_prefetch=1,
            grid=(rows // ROW_BLOCK,),
            in_specs=[at(v.shape[1]) for v in ins]
            + [fixed(v.shape) for v in fixed_ins]
            + [pl.BlockSpec(memory_space=pl.ANY)] * len(raw),
            out_specs=[at(width) for width, _ in outs] + [fixed(shape) for shape in fixed_outs],
            scratch_shapes=scratch,
        ),
        out_shape=[jax.ShapeDtypeStruct((rows, width), kind) for width, kind in outs]
        + [jax.ShapeDtypeStruct(shape, BF16) for shape in fixed_outs],
        compiler_params=pltpu.CompilerParams(
            vmem_limit_bytes=60 << 20, dimension_semantics=("arbitrary",)
        ),
        cost_estimate=pl.CostEstimate(flops=flops, bytes_accessed=moved, transcendentals=0),
        name=name,
    )(info, *ins, *fixed_ins, *raw)


def mixer_forward(info, x, mask, gain, pieces):
    rows = x.shape[0]
    return row_call(
        mixer_forward_kernel,
        rows,
        [x, mask],
        [gain[None, :]],
        pieces,
        [(UNITED, F32), (D, BF16), (RANKS, BF16)],
        [],
        weight_scratch(MIXER),
        info,
        "mixer_forward",
        2 * rows * D * UNITED,
        2 * D * UNITED + 4 * rows * UNITED,
    )


def block_forward(info, joined, x, mask, gain, merge_p, expand_p, reduce_p):
    rows = x.shape[0]
    return row_call(
        block_forward_kernel,
        rows,
        [joined, x, mask],
        [gain[None, :]],
        [*merge_p, *expand_p, *reduce_p],
        [(D, BF16), (D, F32), (D, BF16), (FF, F32), (FF, F32), (3 * RANKS, BF16)],
        [],
        weight_scratch(MERGE)
        + weight_scratch(EXPAND)
        + weight_scratch(REDUCE)
        + [pltpu.VMEM((ROW_BLOCK, FF), BF16)],
        info,
        "block_forward",
        2 * rows * D * (MIX + 3 * FF),
        2 * D * (MIX + 3 * FF) + 12 * rows * FF,
    )


def block_backward(info, grad, joined, middle, second, lit, up, mids, mask, gain, merge_p, expand_p, reduce_p):
    rows = grad.shape[0]
    return row_call(
        block_backward_kernel,
        rows,
        [grad, joined, middle, second, lit, up, mids, mask],
        [gain[None, :]],
        [*reduce_p, *expand_p, *merge_p],
        [(DSSM, F32), (MIX - DSSM, BF16), (D, F32)],
        [(RANKS, GRADS_W)],
        weight_scratch(REDUCE)
        + weight_scratch(EXPAND)
        + weight_scratch(MERGE)
        + [
            pltpu.VMEM((ROW_BLOCK, FF), BF16),
            pltpu.VMEM((ROW_BLOCK, 2 * FF), BF16),
            pltpu.VMEM((RANKS, GRADS_W), F32),
        ],
        info,
        "block_backward",
        2 * rows * D * (MIX + 3 * FF),
        2 * D * (MIX + 3 * FF) + 12 * rows * FF,
    )


def mixer_backward(info, grad, hidden, x, dmiddle, mid, mask, gain, pieces):
    rows = x.shape[0]
    return row_call(
        mixer_backward_kernel,
        rows,
        [grad, hidden, x, dmiddle, mid, mask],
        [gain[None, :]],
        pieces,
        [(D, BF16)],
        [(RANKS, MIXER_GRADS_W)],
        weight_scratch(MIXER) + [pltpu.VMEM((RANKS, MIXER_GRADS_W), F32)],
        info,
        "mixer_backward",
        2 * rows * D * UNITED,
        2 * D * UNITED + 8 * rows * D,
    )


SEQ_SLOTS = 3
RANK = 16
STEP_W = 24


def swap_pairs(count, bit):
    return [(i, i ^ bit) for i in range(count)]


def send_quarter(weight, upper, quarter):
    part, own = weight.shape[0] // QUARTERS, upper.shape[0] // QUARTERS
    return jnp.concatenate(
        [
            lax.dynamic_slice_in_dim(weight, quarter * part, part, 0),
            lax.dynamic_slice_in_dim(upper, quarter * own, own, 0),
        ],
        axis=0,
    )


def across(value):
    return lax.ppermute(value, "shard", swap_pairs(2, 1))


def beside(value, bit):
    return lax.ppermute(value, "rep", swap_pairs(lax.axis_size("rep"), bit))


def spread_quarter(first):
    second = beside(first, 2)
    return (first, second, beside(first, 1), beside(second, 1))


def aligned_columns(value):
    gate, conv = value[:, :DSSM], value[:, DSSM : DSSM + XBC]
    step = value[:, DSSM + XBC : DSSM + XBC + STEP_W]
    attention = value[:, DSSM + XBC + STEP_W :]
    padding = jnp.zeros((value.shape[0], SPAN - STEP_W), value.dtype)
    return jnp.concatenate([gate, attention, conv, step, padding], axis=1)


def given_columns(value):
    conv_at = CONV_C.start
    return jnp.concatenate(
        [
            value[:, :DSSM],
            value[:, conv_at : conv_at + XBC],
            value[:, STEP_C.start : STEP_C.start + STEP_W],
            value[:, DSSM:conv_at],
        ],
        axis=1,
    )


def after(value, *others):
    return lax.optimization_barrier((value, *others))[0]


def reduce_factors(grads):
    rows, width = grads.shape
    half, mine = width // 2, rows // 2
    rep = lax.axis_index("rep")
    side = lax.axis_index("shard")
    core = rep % 2
    count = lax.axis_size("rep") // 2
    groups = [[2 * i + place for i in range(count)] for place in range(2)]
    kept = lax.dynamic_slice_in_dim(grads, core * half, half, 1)
    sent = lax.dynamic_slice_in_dim(grads, (1 - core) * half, half, 1)
    total = kept.astype(F32) + beside(sent, 1).astype(F32)
    kept = lax.dynamic_slice_in_dim(total, side * mine, mine, 0)
    sent = lax.dynamic_slice_in_dim(total, (1 - side) * mine, mine, 0).astype(BF16)
    total = (kept + across(sent).astype(F32)).astype(BF16)
    parts = lax.all_to_all(
        total.reshape(count, mine // count, half),
        "rep",
        split_axis=0,
        concat_axis=0,
        axis_index_groups=groups,
        tiled=True,
    )
    own = jnp.sum(parts.astype(F32), axis=0, keepdims=True).astype(BF16)
    whole = lax.all_to_all(
        jnp.broadcast_to(own, (count, *own.shape[1:])),
        "rep",
        split_axis=0,
        concat_axis=0,
        axis_index_groups=groups,
        tiled=True,
    ).reshape(mine, half)
    other = beside(whole, 1)
    return jnp.where(
        core == 0,
        jnp.concatenate([whole, other], axis=1),
        jnp.concatenate([other, whole], axis=1),
    ).astype(F32)


def row_orders(assignment, stripe, groups):
    units = assignment.shape[0]
    per = units // groups
    total = stripe * units
    sending = jnp.arange(total, dtype=jnp.int32)
    group, row, piece = sending // (stripe * per), sending // per % stripe, sending % per
    source = row * units + jnp.take(assignment, group * per + piece)
    columns = jnp.arange(total, dtype=jnp.int32)
    pick = (source[:, None] == columns[None, :]).astype(BF16)
    working = jnp.arange(total, dtype=jnp.int32)
    piece, group, row = working // (groups * stripe), working // stripe % groups, working % stripe
    received = (group * stripe + row) * per + piece
    place = (received[:, None] == columns[None, :]).astype(BF16)
    return pick, place


def exchange(value):
    return lax.all_to_all(value, ("rep", "shard"), split_axis=0, concat_axis=0, tiled=True)


def on_device(
    tokens,
    cotangent,
    lengths,
    adapter_index,
    assignment,
    first_gain,
    mixer_weight,
    mixer_down,
    mixer_up,
    filter_taps,
    filter_bias,
    step_bias,
    decay_rate,
    skip_gain,
    state_gain,
    merge_weight,
    merge_down,
    merge_up,
    second_gain,
    expand_weight,
    expand_down,
    expand_up,
    reduce_weight,
    reduce_down,
    reduce_up,
):
    stripe, units, width = tokens.shape
    groups = lax.axis_size("rep") * lax.axis_size("shard")
    rows = stripe * units
    rep = lax.axis_index("rep")
    side = lax.axis_index("shard")
    quarter = rep % QUARTERS
    info = jnp.stack([side, quarter, quarter ^ 2, quarter ^ 1, quarter ^ 3]).astype(jnp.int32)

    pick, place = row_orders(assignment, stripe, groups)

    def send_rows(value):
        return dot_nn(pick, value.reshape(rows, width)).astype(BF16)

    def work_rows(value):
        return dot_nn(place, value).astype(BF16)

    token_rows = exchange(send_rows(tokens))

    lower_own = jnp.concatenate([mixer_down, merge_down, expand_down, reduce_down], axis=1)
    lower_sent = lax.dynamic_slice_in_dim(lower_own, quarter * RANK, RANK, 0)
    mixer_sent = aligned_columns(send_quarter(mixer_weight, mixer_up, quarter))
    mixer_own = (aligned_columns(mixer_weight), aligned_columns(mixer_up))
    lower_in = across(lower_sent)
    mixer_in = across(mixer_sent)
    merge_in = across(after(send_quarter(merge_weight, merge_up, quarter), mixer_in))
    expand_in = across(after(send_quarter(expand_weight, expand_up, quarter), merge_in))
    reduce_in = across(after(send_quarter(reduce_weight, reduce_up, quarter), expand_in))
    lowers = spread_quarter(lower_in)
    mixer_p = (*mixer_own, lower_own, *spread_quarter(mixer_in), *lowers)
    merge_p = (merge_weight, merge_up, lower_own, *spread_quarter(merge_in), *lowers)
    expand_p = (expand_weight, expand_up, lower_own, *spread_quarter(expand_in), *lowers)
    reduce_p = (reduce_weight, reduce_up, lower_own, *spread_quarter(reduce_in), *lowers)

    finish = jnp.cumsum(lengths[0])
    begin = finish - lengths[0]
    blocks = jnp.arange(rows // SPAN, dtype=jnp.int32)
    member = (blocks[:, None] >= begin[None, :]) & (blocks[:, None] < finish[None, :])
    first = jnp.sum(jnp.where(member, begin[None, :], 0), axis=1).astype(jnp.int32)
    owner = jnp.sum(jnp.where(member, adapter_index[None, :], 0), axis=1)
    restart = (first == blocks).astype(jnp.int32)
    position = jnp.arange(rows, dtype=jnp.int32) - jnp.repeat(first * SPAN, SPAN)
    mask = (
        jnp.repeat(owner, SPAN)[:, None] == jnp.arange(RANKS, dtype=jnp.int32)[None, :] // RANK
    ).astype(BF16)
    cosine, sines = rotation_tables(position)
    params = ssm_params(filter_taps, filter_bias, step_bias, decay_rate, skip_gain, state_gain)

    x = work_rows(token_rows)
    grad_rows = exchange(after(send_rows(cotangent), token_rows))
    united, hidden, mixer_mid = mixer_forward(info, x, mask, first_gain, mixer_p)
    attended, logs, turned, kv_low = attend_forward(united, cosine, sines, first)
    joined, scan, starts = mamba_forward(united, attended, restart, params)
    mixed, middle, second, lit, up, mids = block_forward(
        info, joined, x, mask, second_gain, merge_p, expand_p, reduce_p
    )

    def leave_rows(value):
        return exchange(lax.dot_general(
            place, value, (((0,), (0,)), ((), ())), preferred_element_type=F32
        ).astype(BF16))

    def input_rows(value, kind):
        return (
            lax.dot_general(pick, value, (((0,), (0,)), ((), ())), preferred_element_type=F32)
            .astype(kind)
            .reshape(stripe, units, width)
        )

    mixed_rows = leave_rows(mixed)

    grad_top = work_rows(grad_rows)
    dmamba, dattended, dmiddle, block_grads = block_backward(
        info, grad_top, joined, middle, second, lit, up, mids, mask, second_gain,
        merge_p, expand_p, reduce_p,
    )
    block_final = reduce_factors(block_grads)
    dquery, dkv = attend_backward(turned, kv_low, dattended, logs, cosine, sines, first)
    dunited = mamba_backward(united, scan, starts, dmamba, dquery, dkv, restart, params)
    work_grad, mixer_grads = mixer_backward(
        info, dunited, hidden, x, dmiddle, mixer_mid, mask, first_gain, mixer_p
    )
    token_grads = leave_rows(work_grad)
    mixer_final = reduce_factors(mixer_grads)
    return (
        input_rows(mixed_rows, BF16),
        input_rows(token_grads, F32),
        mixer_final[:, :D],
        given_columns(mixer_final[:, D : D + UNITED]),
        block_final[:, MERGE_L],
        block_final[:, MERGE_U],
        block_final[:, EXPAND_L],
        block_final[:, EXPAND_U],
        block_final[:, REDUCE_L],
        block_final[:, REDUCE_U],
    )


def solution(mesh):
    split = ("rep", "shard")
    sharded = P("shard", None)
    placed = (
        P(split, None, None),
        P(split, None, None),
        P(split, None),
        P(split),
        P(),
        P(),
        sharded,
        sharded,
        sharded,
        P(),
        P(),
        P(),
        P(),
        P(),
        P(),
        sharded,
        sharded,
        sharded,
        P(),
        sharded,
        sharded,
        sharded,
        sharded,
        sharded,
        sharded,
    )
    return jax.shard_map(
        on_device,
        mesh=mesh,
        in_specs=placed,
        out_specs=(P(split, None, None), P(split, None, None)) + (sharded,) * 8,
        check_vma=False,
    )
```

time: 1800 us -> 654 us (0.36); the launches traced: 1770 us -> 649 us
  local copies, waits for them, and re-layouts: 570 us -> 62.1 us
  matrix products: 539 us -> 37 us
  Pallas kernels: 0 us -> 263 us
  other arithmetic: 271 us -> 13.7 us
  blocking collectives: 191 us -> 0 us
  waiting for transfers between devices: 154 us -> 220 us
  starting transfers between devices: 23.3 us -> 51.5 us
    dot_general x156 -> x8, matrix products: 539 us -> 37 us  [the longest x4 18 us: dot_nn(): lax.dot_general(a, b, (((1,), (0,)), ((), ())), preferred_element_type=F32)]
    dynamic_update_slice x88 -> x0, local copies, waits for them, and re-layouts: 368 us -> none  [state_scan(): lax.scan(advance, initial, (inputs_x, vector_b, vector_c, delta, restart))]
    pallas_call x0 -> x8, Pallas kernels: none -> 263 us  [the longest x4 161 us: row_call(): pl.pallas_call(kernel, grid_spec=pltpu.PrefetchScalarGridSpec(num_scalar_...]
    ppermute x0 -> x26, waiting for transfers between devices: none -> 110 us  [the longest x7 80.4 us: across(): return lax.ppermute(value, 'shard', swap_pairs(2, 1))]
    all_to_all x4 -> x8, waiting for transfers between devices: 7.35 us -> 110 us  [the longest x4 58.9 us: exchange(): lax.all_to_all(value, ('rep', 'shard'), split_axis=0, concat_axis=0, tile...]
    psum x1 -> x0, blocking collectives: 98.3 us -> none  [settle_all(): lax.psum((owned[0], owned[1], owned[2], owned[3], owned[4], owned[5], own...]
    all_gather x6 -> x0, blocking collectives: 92.8 us -> none  [the longest x4 57.3 us: fetch(): lax.all_gather(lower, 'shard', axis=0, tiled=True)]
    all_gather x6 -> x0, waiting for transfers between devices: 78 us -> none  [the longest x4 78 us: fetch(): lax.all_gather(weight, 'shard', axis=0, tiled=True)]
  transfers between devices with their start and end apart: 18 -> 34, of which waited for: 5 -> 12; matrix products, arithmetic and copies ran while one was open for 70% -> 13% of each run, Pallas kernels for 0% -> 17%
where the time goes in v1:
time: 654 us; the launch traced here: 649 us
  Pallas kernels  263 us (40%)
  waiting for transfers between devices  220 us (34%)
  local copies, waits for them, and re-layouts  62.1 us (9%)
  starting transfers between devices  51.5 us (8%)
  matrix products  37 us (6%)
  other arithmetic  13.7 us (2%)
    pallas_call x4, Pallas kernels, row_call(): pl.pallas_call(kernel, grid_spec=pltpu.PrefetchScalarGridSpec(num_scalar_...  161 us
    ppermute x7, waiting for transfers between devices, across(): return lax.ppermute(value, 'shard', swap_pairs(2, 1))  80.4 us
    all_to_all x4, waiting for transfers between devices, exchange(): lax.all_to_all(value, ('rep', 'shard'), split_axis=0, concat_axis=0, tile...  58.9 us
    pallas_call x1, Pallas kernels, mamba_backward(): pl.pallas_call(mamba_backward_kernel, grid_spec=pltpu.PrefetchScalarGridS...  49.1 us
    ppermute x19, waiting for transfers between devices, beside(): return lax.ppermute(value, 'rep', swap_pairs(lax.axis_size('rep'), bit))  29.3 us
    all_to_all x2, waiting for transfers between devices, reduce_factors(): lax.all_to_all(total.reshape(count, mine // count, half), 'rep', split_ax...  27.4 us
    all_to_all x2, waiting for transfers between devices, reduce_factors(): lax.all_to_all(jnp.broadcast_to(own, (count, *own.shape[1:])), 'rep', spl...  24 us
    pallas_call x1, Pallas kernels, mamba_forward(): pl.pallas_call(mamba_forward_kernel, grid_spec=pltpu.PrefetchScalarGridSp...  22.1 us
  transfers between devices with their start and end apart: 34, of which 12 were waited for; matrix products, arithmetic and copies ran while one was open for 13% of the time, Pallas kernels for 17%

profile of v1, /device:TPU:0, one launch (start us, length us, event | category | flops | bytes accessed | tf_op | source)
XLA Modules:
  0.0 649.0 jit_solution(15135468739927925686)
XLA Ops:
  1.5 6.8 %gather_fusion = s32[1024]{0:T(1024)S(1)} fusion(s32[256]{0:T(256)S(1)} %copy-done.5, s32[1024]{0:T(1024)S(1)} %broadcast_clamp_fusion), kind=kCustom, calls=%fused_computation | custom fusion | bytes 12288 | tf_op jit(solution)/shard_map/jit(_take)/gather | solution.py:1233
  8.4 3.7 fusion.18
  12.1 8.0 %all-to-all-start = ((bf16[32,32,1024]{2,1,0:T(8,128)(2,1)}), bf16[32,32,1024]{2,1,0:T(8,128)(2,1)}, u32[]{:S(2)}, u32[]{:S(2)}) async-start(bf16[32,32,1024]{2,1,0:T(8,128)(2,1)} %bitcast.56), calls=%async_computation | async-start | bytes 4194304 | tf_op jit(solution)/shard_map/all_to_all | solution.py:1244
  24.2 1.9 collective-permute-start
  35.9 36.0 %collective-permute-done.rest_3_ = bf16[144,4224]{1,0:T(8,128)(2,1)} collective-permute-done((bf16[144,4224]{1,0:T(8,128)(2,1)S(1)}, bf16[144,4224]{1,0:T(8,128)(2,1)}, u32[]{:S(2)}, u32[]{:S(2)}) %collective-permute-start) | collective-permute-done | bytes 1216544 | tf_op jit(solution)/shard_map/ppermute | solution.py:1151
  74.9 12.6 %collective-permute-done.8.rest_3_.rest_25_ = bf16[272,1024]{1,0:T(8,128)(2,1)} collective-permute-done((bf16[272,1024]{1,0:T(8,128)(2,1)S(1)}, bf16[272,1024]{1,0:T(8,128)(2,1)}, u32[]{:S(2)}, u32[]{:S(2)}) %collective-permute-start.8) | collective-permute-done | bytes 557088 | tf_op jit(solution)/shard_map/ppermute | solution.py:1151
  88.7 3.8 fusion.20
  92.5 7.8 %collective-permute-done.1.rest_4_ = bf16[144,4224]{1,0:T(8,128)(2,1)} collective-permute-done((bf16[144,4224]{1,0:T(8,128)(2,1)}, bf16[144,4224]{1,0:T(8,128)(2,1)}, u32[]{:S(2)}, u32[]{:S(2)}) %collective-permute-start.1) | collective-permute-done | bytes 1216544 | tf_op jit(solution)/shard_map/ppermute | solution.py:1155
  104.1 11.0 %collective-permute-done.12.rest_14_ = bf16[144,4096]{1,0:T(8,128)(2,1)} collective-permute-done((bf16[144,4096]{1,0:T(8,128)(2,1)S(1)}, bf16[144,4096]{1,0:T(8,128)(2,1)}, u32[]{:S(2)}, u32[]{:S(2)}) %collective-permute-start.12) | collective-permute-done | bytes 1179680 | tf_op jit(solution)/shard_map/ppermute | solution.py:1151
  117.6 2.1 slice.71
  119.7 3.0 slice.72
  126.4 2.3 copy.53
  128.7 4.0 copy.54
  133.5 7.4 %concatenate.47.rest_0_ = bf16[512,4224]{1,0:T(8,128)(2,1)} concatenate(bf16[512,1536]{1,0:T(8,128)(2,1)S(1)} %copy-done.6, bf16[512,768]{1,0:T(8,128)(2,1)} %copy.53, bf16[512,1816]{1,0:T(8,128)(2,1)} %copy.54, bf16[512,104]{1,0:T(8,128)(2,1)} %broadcast_in_dim.92), dimensions={1} | concatenate | bytes 8650752 | tf_op jit(solution)/shard_map/concatenate | solution.py:1168
  143.5 5.3 fusion.21.x_ref
  148.7 5.0 all-to-all-start.2
  156.5 22.6 %mixer_forward.1 = (f32[1024,4224]{1,0:T(8,128)}, bf16[1024,1024]{1,0:T(8,128)(2,1)}, bf16[1024,128]{1,0:T(8,128)(2,1)}) custom-call(s32[5]{0:T(128)} %stack.23.info_ref, bf16[1024,1024]{1,0:T(8,128)(2,1)} %fusion.21.x_ref, bf16[1024,128]{1,0:T(8,128)(2,1)} %compare_convert_fusion.1.mask_ref, f32[1,1024]{1,0:T(1,128)} %bitcast.66, ...), custom_call_target="tpu_custom_call" | custom-call | flops 8858370048 | bytes 25952256 | tf_op jit(solution)/shard_map/mixer_forward/pallas_call | solution.py:1027
  179.0 15.4 %attend_forward.1 = (bf16[1024,512]{1,0:T(8,128)(2,1)S(1)}, f32[8,8,128]{2,1,0:T(8,128)S(1)}, bf16[1024,512]{1,0:T(8,128)(2,1)S(1)}, bf16[1024,256]{1,0:T(8,128)(2,1)S(1)}) custom-call(s32[8]{0:T(128)S(1)} %get-tuple-element.67.first_ref, f32[1024,4224]{1,0:T(8,128)} %get-tuple-element.38.query_ref.kv_ref.united_ref.above_ref, ...), custom_call_target="tpu_custom_call" | custom-call | flops 15000000512 | bytes 6000000 | tf_op jit(solution)/shard_map/attend_forward/pallas_call | solution.py:639
  194.8 21.5 %collective-permute-done.17.rest_26_.rest_4_ = bf16[272,1024]{1,0:T(8,128)(2,1)} collective-permute-done((bf16[272,1024]{1,0:T(8,128)(2,1)}, bf16[272,1024]{1,0:T(8,128)(2,1)}, u32[]{:S(2)}, u32[]{:S(2)}) %collective-permute-start.17) | collective-permute-done | bytes 557088 | tf_op jit(solution)/shard_map/ppermute | solution.py:1155
  216.8 22.1 %mamba_forward.1 = (bf16[1024,2048]{1,0:T(8,128)(2,1)S(1)}, f32[1024,1536]{1,0:T(8,128)}, f32[8,128,1536]{2,1,0:T(8,128)}) custom-call(s32[8]{0:T(128)S(1)} %compare_convert_fusion.2.restart_ref, f32[1024,4224]{1,0:T(8,128)} %get-tuple-element.38.query_ref.kv_ref.united_ref.above_ref, bf16[1024,512]{1,0:T(8,128)(2,1)S(1)} %get-tuple-element.39.attended_ref, ...), custom_call_target="tpu_custom_call" | custom-call | flops 20000000000 | bytes 50000000 | tf_op jit(solution)/shard_map/mamba_forward/pallas_call | solution.py:389
  239.0 2.0 copy-done.3
  241.0 48.2 %block_forward.1 = (bf16[1024,1024]{1,0:T(8,128)(2,1)}, f32[1024,1024]{1,0:T(8,128)}, bf16[1024,1024]{1,0:T(8,128)(2,1)}, f32[1024,2048]{1,0:T(8,128)}, f32[1024,2048]{1,0:T(8,128)}, /*index=5*/bf16[1024,384]{1,0:T(8,128)(2,1)}) custom-call(s32[5]{0:T(128)} %stack.23.info_ref, bf16[1024,2048]{1,0:T(8,128)(2,1)} %copy-done.3, ...), custom_call_target="tpu_custom_call" | custom-call | flops 17179869184 | bytes 41943040 | tf_op jit(solution)/shard_map/block_forward/pallas_call | solution.py:1027
  289.3 5.3 fusion.23.grad_ref
  294.5 65.1 %block_backward.1 = (f32[1024,1536]{1,0:T(8,128)}, bf16[1024,512]{1,0:T(8,128)(2,1)}, f32[1024,1024]{1,0:T(8,128)}, bf16[128,11264]{1,0:T(8,128)(2,1)}) custom-call(s32[5]{0:T(128)} %stack.23.info_ref, bf16[1024,1024]{1,0:T(8,128)(2,1)} %fusion.23.grad_ref, bf16[1024,2048]{1,0:T(8,128)(2,1)} %copy-done.3, f32[1024,1024]{1,0:T(8,128)} %get-tuple-element.48.middle_ref, ...), custom_call_target="tpu_custom_call" | custom-call | flops 17179869184 | bytes 41943040 | tf_op jit(solution)/shard_map/block_backward/pallas_call | solution.py:1027
  360.9 15.9 %attend_backward.1 = (bf16[1024,512]{1,0:T(8,128)(2,1)S(1)}, bf16[1024,256]{1,0:T(8,128)(2,1)S(1)}) custom-call(s32[8]{0:T(128)S(1)} %get-tuple-element.67.first_ref, bf16[1024,512]{1,0:T(8,128)(2,1)S(1)} %get-tuple-element.54.turned_ref, bf16[1024,256]{1,0:T(8,128)(2,1)S(1)} %get-tuple-element.55.kv_low_ref, bf16[1024,512]{1,0:T(8,128)(2,1)S(1)} %copy-done.4, ...), custom_call_target="tpu_custom_call" | custom-call | flops 15000000512 | bytes 6000000 | tf_op jit(solution)/shard_map/attend_backward/pallas_call | solution.py:676
  376.8 49.1 %mamba_backward.1.grad_ref = bf16[1024,4224]{1,0:T(8,128)(2,1)} custom-call(s32[8]{0:T(128)S(1)} %compare_convert_fusion.2.restart_ref, f32[1024,4224]{1,0:T(8,128)} %get-tuple-element.38.query_ref.kv_ref.united_ref.above_ref, f32[1024,4224]{1,0:T(8,128)} %get-tuple-element.38.query_ref.kv_ref.united_ref.above_ref, f32[1024,1536]{1,0:T(8,128)} %get-tuple-element.45.scan_ref, ...), custom_call_target="tpu_custom_call" | custom-call | flops 44999999488 | bytes 60000000 | tf_op jit(solution)/shard_map/mamba_backward/pallas_call | solution.py:426
  425.9 24.6 %mixer_backward.1 = (bf16[1024,1024]{1,0:T(8,128)(2,1)}, bf16[128,5376]{1,0:T(8,128)(2,1)}) custom-call(s32[5]{0:T(128)} %stack.23.info_ref, bf16[1024,4224]{1,0:T(8,128)(2,1)} %mamba_backward.1.grad_ref, bf16[1024,1024]{1,0:T(8,128)(2,1)} %get-tuple-element.60.hidden_ref, bf16[1024,1024]{1,0:T(8,128)(2,1)} %fusion.21.x_ref, ...), custom_call_target="tpu_custom_call" | custom-call | flops 8858370048 | bytes 17039360 | tf_op jit(solution)/shard_map/mixer_backward/pallas_call | solution.py:1027
  450.5 2.1 constant_dynamic-slice_fusion.1
  454.4 3.8 fusion.22
  458.2 4.9 all-to-all-start.1
  465.9 2.2 convert_add_fusion
  469.4 20.8 %collective-permute-done.21 = bf16[64,2688]{1,0:T(8,128)(2,1)S(1)} collective-permute-done((bf16[64,2688]{1,0:T(8,128)(2,1)}, bf16[64,2688]{1,0:T(8,128)(2,1)S(1)}, u32[]{:S(2)}, u32[]{:S(2)}) %collective-permute-start.21) | collective-permute-done | bytes 344096 | tf_op jit(solution)/shard_map/ppermute | solution.py:1151
  492.0 19.8 %all-to-all-done.1 = bf16[32,32,1024]{2,1,0:T(8,128)(2,1)} async-done(((bf16[32,32,1024]{2,1,0:T(8,128)(2,1)}), bf16[32,32,1024]{2,1,0:T(8,128)(2,1)}, u32[]{:S(2)}, u32[]{:S(2)}) %all-to-all-start.1) | async-done | bytes 2097184 | tf_op jit(solution)/shard_map/all_to_all | solution.py:1244
  511.9 3.8 all-to-all-start.4
  515.6 2.1 fusion.26
  517.7 8.8 %all-to-all-done.4 = bf16[8,8,2688]{2,1,0:T(8,128)(2,1)S(1)} async-done(((bf16[8,8,2688]{2,1,0:T(8,128)(2,1)}), bf16[8,8,2688]{2,1,0:T(8,128)(2,1)S(1)}, u32[]{:S(2)}, u32[]{:S(2)}) %all-to-all-start.4) | async-done | bytes 344096 | tf_op jit(solution)/shard_map/all_to_all | solution.py:1202
  526.5 3.6 all-to-all-start.6
  530.2 18.7 %all-to-all-done.6 = bf16[8,8,5632]{2,1,0:T(8,128)(2,1)S(1)} async-done(((bf16[8,8,5632]{2,1,0:T(8,128)(2,1)}), bf16[8,8,5632]{2,1,0:T(8,128)(2,1)S(1)}, u32[]{:S(2)}, u32[]{:S(2)}) %all-to-all-start.6) | async-done | bytes 720928 | tf_op jit(solution)/shard_map/all_to_all | solution.py:1202
  549.6 3.6 all-to-all-start.5
  553.3 10.7 %all-to-all-done.5 = bf16[8,8,2688]{2,1,0:T(8,128)(2,1)S(1)} async-done(((bf16[8,8,2688]{2,1,0:T(8,128)(2,1)}), bf16[8,8,2688]{2,1,0:T(8,128)(2,1)S(1)}, u32[]{:S(2)}, u32[]{:S(2)}) %all-to-all-start.5) | async-done | bytes 344096 | tf_op jit(solution)/shard_map/all_to_all | solution.py:1211
  564.9 3.6 all-to-all-start.7
  568.6 5.4 fusion.24
  574.0 13.3 %all-to-all-done.7 = bf16[8,8,5632]{2,1,0:T(8,128)(2,1)S(1)} async-done(((bf16[8,8,5632]{2,1,0:T(8,128)(2,1)}), bf16[8,8,5632]{2,1,0:T(8,128)(2,1)S(1)}, u32[]{:S(2)}, u32[]{:S(2)}) %all-to-all-start.7) | async-done | bytes 720928 | tf_op jit(solution)/shard_map/all_to_all | solution.py:1211
  587.3 3.7 all-to-all-start.3
  591.5 5.4 fusion.19
  598.7 2.0 concatenate.59
  600.7 39.0 %all-to-all-done.3 = bf16[32,32,1024]{2,1,0:T(8,128)(2,1)S(1)} async-done(((bf16[32,32,1024]{2,1,0:T(8,128)(2,1)}), bf16[32,32,1024]{2,1,0:T(8,128)(2,1)S(1)}, u32[]{:S(2)}, u32[]{:S(2)}) %all-to-all-start.3) | async-done | bytes 2097184 | tf_op jit(solution)/shard_map/all_to_all | solution.py:1244
  639.7 4.4 fusion.7
  (177 shorter events, 53.2 us)
Async XLA Ops:
  0.6 7.7 %copy-start = (bf16[4,256,1024]{2,1,0:T(8,128)(2,1)S(1)}, bf16[4,256,1024]{2,1,0:T(8,128)(2,1)}, u32[]{:S(2)}) copy-start(bf16[4,256,1024]{2,1,0:T(8,128)(2,1)} %param.25) | copy-start | bytes 6291460
  8.3 80.4 %copy-start.16 = (s32[1024]{0:T(1024)}, s32[1024]{0:T(1024)S(1)}, u32[]{:S(2)}) copy-start(s32[1024]{0:T(1024)S(1)} %fusion.50) | copy-start | bytes 12292
  12.1 131.4 %all-to-all-start = ((bf16[32,32,1024]{2,1,0:T(8,128)(2,1)}), bf16[32,32,1024]{2,1,0:T(8,128)(2,1)}, u32[]{:S(2)}, u32[]{:S(2)}) async-start(bf16[32,32,1024]{2,1,0:T(8,128)(2,1)} %bitcast.56), calls=%async_computation | async-start | bytes 4194304 | tf_op jit(solution)/shard_map/all_to_all | solution.py:1244
  23.7 4.6 copy-start.26
  23.8 4.7 copy-start.18
  24.2 47.7 %collective-permute-start = (bf16[144,4224]{1,0:T(8,128)(2,1)S(1)}, bf16[144,4224]{1,0:T(8,128)(2,1)}, u32[]{:S(2)}, u32[]{:S(2)}) collective-permute-start(bf16[144,4224]{1,0:T(8,128)(2,1)S(1)} %concatenate.51), channel_id=1, source_target_pairs={{0,1},{1,0},{2,3},{3,2},{4,5},{5,4},{6,7},{7,6},{8,9},{9,8},{10,11... | collective-permute-start | bytes 3649544 | tf_op jit(solution)/shard_map/ppermute | solution.py:1151
  28.0 6.3 copy-start.13
  28.1 73.3 %collective-permute-start.4 = (bf16[16,6144]{1,0:T(8,128)(2,1)S(1)}, bf16[16,6144]{1,0:T(8,128)(2,1)}, u32[]{:S(2)}, u32[]{:S(2)}) collective-permute-start(bf16[16,6144]{1,0:T(8,128)(2,1)S(1)} %constant_dynamic-slice_fusion.8), channel_id=1, source_target_pairs={{0,1},{1,0},{2,3},{3,2},{4,5},{5,4},{6,7},{7,6},{8,9},{9,8},{10,11... | collective-permute-start | bytes 589832 | tf_op jit(solution)/shard_map/ppermute | solution.py:1151
  71.9 15.6 %collective-permute-start.8 = (bf16[272,1024]{1,0:T(8,128)(2,1)S(1)}, bf16[272,1024]{1,0:T(8,128)(2,1)}, u32[]{:S(2)}, u32[]{:S(2)}) collective-permute-start(bf16[272,1024]{1,0:T(8,128)(2,1)S(1)} %pad_maximum_fusion.1), channel_id=1, source_target_pairs={{0,1},{1,0},{2,3},{3,2},{4,5},{5,4},{6,7},{7,6},{8,9},{9,8},{10,11... | collective-permute-start | bytes 1671176 | tf_op jit(solution)/shard_map/ppermute | solution.py:1151
  72.1 28.2 %collective-permute-start.1 = (bf16[144,4224]{1,0:T(8,128)(2,1)}, bf16[144,4224]{1,0:T(8,128)(2,1)}, u32[]{:S(2)}, u32[]{:S(2)}) collective-permute-start(bf16[144,4224]{1,0:T(8,128)(2,1)} %collective-permute-done.rest_3_), channel_id=1, source_target_pairs={{0,4},{2,6},{4,0},{6,2},{8,12},{10,14},{12,8},{14,10},{16,20},{18,... | collective-permute-start | bytes 3649544 | tf_op jit(solution)/shard_map/ppermute | solution.py:1155
  73.9 14.8 %copy-start.22 = (bf16[4,256,1024]{2,1,0:T(8,128)(2,1)S(1)}, bf16[4,256,1024]{2,1,0:T(8,128)(2,1)}, u32[]{:S(2)}) copy-start(bf16[4,256,1024]{2,1,0:T(8,128)(2,1)} %param.26) | copy-start | bytes 6291460
  87.5 27.6 %collective-permute-start.12 = (bf16[144,4096]{1,0:T(8,128)(2,1)S(1)}, bf16[144,4096]{1,0:T(8,128)(2,1)}, u32[]{:S(2)}, u32[]{:S(2)}) collective-permute-start(bf16[144,4096]{1,0:T(8,128)(2,1)S(1)} %pad_maximum_fusion), channel_id=1, source_target_pairs={{0,1},{1,0},{2,3},{3,2},{4,5},{5,4},{6,7},{7,6},{8,9},{9,8},{10,11... | collective-permute-start | bytes 3538952 | tf_op jit(solution)/shard_map/ppermute | solution.py:1151
  92.5 24.8 %copy-start.20 = (f32[24]{0:T(128)S(1)}, f32[24]{0:T(128)}, u32[]{:S(2)}) copy-start(f32[24]{0:T(128)} %param.37) | copy-start | bytes 292
  92.5 24.8 %copy-start.21 = (f32[24]{0:T(128)S(1)}, f32[24]{0:T(128)}, u32[]{:S(2)}) copy-start(f32[24]{0:T(128)} %param.36) | copy-start | bytes 292
  92.5 61.9 %collective-permute-start.2 = (bf16[144,4224]{1,0:T(8,128)(2,1)}, bf16[144,4224]{1,0:T(8,128)(2,1)}, u32[]{:S(2)}, u32[]{:S(2)}) collective-permute-start(bf16[144,4224]{1,0:T(8,128)(2,1)} %collective-permute-done.rest_3_), channel_id=1, source_target_pairs={{0,2},{2,0},{4,6},{6,4},{8,10},{10,8},{12,14},{14,12},{16,18},{18,... | collective-permute-start | bytes 3649544 | tf_op jit(solution)/shard_map/ppermute | solution.py:1155
  100.3 56.0 %collective-permute-start.3 = (bf16[144,4224]{1,0:T(8,128)(2,1)}, bf16[144,4224]{1,0:T(8,128)(2,1)}, u32[]{:S(2)}, u32[]{:S(2)}) collective-permute-start(bf16[144,4224]{1,0:T(8,128)(2,1)} %collective-permute-done.1.rest_4_), channel_id=1, source_target_pairs={{0,2},{2,0},{4,6},{6,4},{8,10},{10,8},{12,14},{14,12},{16,18},{18,... | collective-permute-start | bytes 3649544 | tf_op jit(solution)/shard_map/ppermute | solution.py:1155
  101.4 15.5 %collective-permute-start.5 = (bf16[16,6144]{1,0:T(8,128)(2,1)}, bf16[16,6144]{1,0:T(8,128)(2,1)S(1)}, u32[]{:S(2)}, u32[]{:S(2)}) collective-permute-start(bf16[16,6144]{1,0:T(8,128)(2,1)} %collective-permute-done.4.rest_7_.rest_18_.rest_29_), channel_id=1, source_target_pairs={{0,4},{2,6},{4,0},{6,2},{8,12},{10,14},{12,8},{14,10},{16,20},{18,... | collective-permute-start | bytes 589832 | tf_op jit(solution)/shard_map/ppermute | solution.py:1155
  103.8 39.6 %collective-permute-start.6 = (bf16[16,6144]{1,0:T(8,128)(2,1)}, bf16[16,6144]{1,0:T(8,128)(2,1)}, u32[]{:S(2)}, u32[]{:S(2)}) collective-permute-start(bf16[16,6144]{1,0:T(8,128)(2,1)} %collective-permute-done.4.rest_7_.rest_18_.rest_29_), channel_id=1, source_target_pairs={{0,2},{2,0},{4,6},{6,4},{8,10},{10,8},{12,14},{14,12},{16,18},{18,... | collective-permute-start | bytes 589832 | tf_op jit(solution)/shard_map/ppermute | solution.py:1155
  115.1 39.1 %collective-permute-start.9 = (bf16[272,1024]{1,0:T(8,128)(2,1)}, bf16[272,1024]{1,0:T(8,128)(2,1)}, u32[]{:S(2)}, u32[]{:S(2)}) collective-permute-start(bf16[272,1024]{1,0:T(8,128)(2,1)} %collective-permute-done.8.rest_3_.rest_25_), channel_id=1, source_target_pairs={{0,4},{2,6},{4,0},{6,2},{8,12},{10,14},{12,8},{14,10},{16,20},{18,... | collective-permute-start | bytes 1671176 | tf_op jit(solution)/shard_map/ppermute | solution.py:1155
  116.9 39.3 %collective-permute-start.16 = (bf16[272,1024]{1,0:T(8,128)(2,1)}, bf16[272,1024]{1,0:T(8,128)(2,1)}, u32[]{:S(2)}, u32[]{:S(2)}) collective-permute-start(bf16[272,1024]{1,0:T(8,128)(2,1)} %pad_maximum_fusion.2), channel_id=1, source_target_pairs={{0,1},{1,0},{2,3},{3,2},{4,5},{5,4},{6,7},{7,6},{8,9},{9,8},{10,11... | collective-permute-start | bytes 1671176 | tf_op jit(solution)/shard_map/ppermute | solution.py:1151
  119.7 5.1 slice-start
  128.7 4.9 copy-start.6
  143.4 10.3 %collective-permute-start.7 = (bf16[16,6144]{1,0:T(8,128)(2,1)}, bf16[16,6144]{1,0:T(8,128)(2,1)S(1)}, u32[]{:S(2)}, u32[]{:S(2)}) collective-permute-start(bf16[16,6144]{1,0:T(8,128)(2,1)} %copy-done.24), channel_id=1, source_target_pairs={{0,2},{2,0},{4,6},{6,4},{8,10},{10,8},{12,14},{14,12},{16,18},{18,... | collective-permute-start | bytes 589832 | tf_op jit(solution)/shard_map/ppermute | solution.py:1155
  148.7 140.5 %all-to-all-start.2 = ((bf16[32,32,1024]{2,1,0:T(8,128)(2,1)}), bf16[32,32,1024]{2,1,0:T(8,128)(2,1)}, u32[]{:S(2)}, u32[]{:S(2)}) async-start(bf16[32,32,1024]{2,1,0:T(8,128)(2,1)} %bitcast.57), calls=%async_computation.2 | async-start | bytes 4194304 | tf_op jit(solution)/shard_map/all_to_all | solution.py:1244
  153.8 40.7 %collective-permute-start.10 = (bf16[272,1024]{1,0:T(8,128)(2,1)}, bf16[272,1024]{1,0:T(8,128)(2,1)S(1)}, u32[]{:S(2)}, u32[]{:S(2)}) collective-permute-start(bf16[272,1024]{1,0:T(8,128)(2,1)} %collective-permute-done.8.rest_3_.rest_25_), channel_id=1, source_target_pairs={{0,2},{2,0},{4,6},{6,4},{8,10},{10,8},{12,14},{14,12},{16,18},{18,... | collective-permute-start | bytes 1671176 | tf_op jit(solution)/shard_map/ppermute | solution.py:1155
  154.2 86.8 %collective-permute-start.11 = (bf16[272,1024]{1,0:T(8,128)(2,1)}, bf16[272,1024]{1,0:T(8,128)(2,1)}, u32[]{:S(2)}, u32[]{:S(2)}) collective-permute-start(bf16[272,1024]{1,0:T(8,128)(2,1)} %collective-permute-done.9.rest_4_.rest_26_), channel_id=1, source_target_pairs={{0,2},{2,0},{4,6},{6,4},{8,10},{10,8},{12,14},{14,12},{16,18},{18,... | collective-permute-start | bytes 1671176 | tf_op jit(solution)/shard_map/ppermute | solution.py:1155
  154.3 62.0 %collective-permute-start.13 = (bf16[144,4096]{1,0:T(8,128)(2,1)}, bf16[144,4096]{1,0:T(8,128)(2,1)}, u32[]{:S(2)}, u32[]{:S(2)}) collective-permute-start(bf16[144,4096]{1,0:T(8,128)(2,1)} %collective-permute-done.12.rest_14_), channel_id=1, source_target_pairs={{0,4},{2,6},{4,0},{6,2},{8,12},{10,14},{12,8},{14,10},{16,20},{18,... | collective-permute-start | bytes 3538952 | tf_op jit(solution)/shard_map/ppermute | solution.py:1155
  156.2 84.8 %collective-permute-start.14 = (bf16[144,4096]{1,0:T(8,128)(2,1)}, bf16[144,4096]{1,0:T(8,128)(2,1)}, u32[]{:S(2)}, u32[]{:S(2)}) collective-permute-start(bf16[144,4096]{1,0:T(8,128)(2,1)} %collective-permute-done.12.rest_14_), channel_id=1, source_target_pairs={{0,2},{2,0},{4,6},{6,4},{8,10},{10,8},{12,14},{14,12},{16,18},{18,... | collective-permute-start | bytes 3538952 | tf_op jit(solution)/shard_map/ppermute | solution.py:1155
  156.2 60.1 %collective-permute-start.17 = (bf16[272,1024]{1,0:T(8,128)(2,1)}, bf16[272,1024]{1,0:T(8,128)(2,1)}, u32[]{:S(2)}, u32[]{:S(2)}) collective-permute-start(bf16[272,1024]{1,0:T(8,128)(2,1)} %collective-permute-done.16.rest_25_.rest_3_), channel_id=1, source_target_pairs={{0,4},{2,6},{4,0},{6,2},{8,12},{10,14},{12,8},{14,10},{16,20},{18,... | collective-permute-start | bytes 1671176 | tf_op jit(solution)/shard_map/ppermute | solution.py:1155
  179.0 37.8 %copy-start.2 = (f32[4,1792]{1,0:T(4,128)S(1)}, f32[4,1792]{1,0:T(4,128)}, u32[]{:S(2)}) copy-start(f32[4,1792]{1,0:T(4,128)} %taps_ref.3) | copy-start | bytes 86020
  194.5 44.5 %copy-start.23 = (bf16[272,1024]{1,0:T(8,128)(2,1)}, bf16[272,1024]{1,0:T(8,128)(2,1)S(1)}, u32[]{:S(2)}) copy-start(bf16[272,1024]{1,0:T(8,128)(2,1)S(1)} %collective-permute-done.10.rest_5_.rest_27_) | copy-start | bytes 1671172
  194.5 46.5 %collective-permute-start.18 = (bf16[272,1024]{1,0:T(8,128)(2,1)}, bf16[272,1024]{1,0:T(8,128)(2,1)}, u32[]{:S(2)}, u32[]{:S(2)}) collective-permute-start(bf16[272,1024]{1,0:T(8,128)(2,1)} %collective-permute-done.16.rest_25_.rest_3_), channel_id=1, source_target_pairs={{0,2},{2,0},{4,6},{6,4},{8,10},{10,8},{12,14},{14,12},{16,18},{18,... | collective-permute-start | bytes 1671176 | tf_op jit(solution)/shard_map/ppermute | solution.py:1155
  216.3 24.7 %collective-permute-start.19 = (bf16[272,1024]{1,0:T(8,128)(2,1)}, bf16[272,1024]{1,0:T(8,128)(2,1)}, u32[]{:S(2)}, u32[]{:S(2)}) collective-permute-start(bf16[272,1024]{1,0:T(8,128)(2,1)} %collective-permute-done.17.rest_26_.rest_4_), channel_id=1, source_target_pairs={{0,2},{2,0},{4,6},{6,4},{8,10},{10,8},{12,14},{14,12},{16,18},{18,... | collective-permute-start | bytes 1671176 | tf_op jit(solution)/shard_map/ppermute | solution.py:1155
  216.3 24.7 %collective-permute-start.15 = (bf16[144,4096]{1,0:T(8,128)(2,1)}, bf16[144,4096]{1,0:T(8,128)(2,1)}, u32[]{:S(2)}, u32[]{:S(2)}) collective-permute-start(bf16[144,4096]{1,0:T(8,128)(2,1)} %collective-permute-done.13.rest_15_), channel_id=1, source_target_pairs={{0,2},{2,0},{4,6},{6,4},{8,10},{10,8},{12,14},{14,12},{16,18},{18,... | collective-permute-start | bytes 3538952 | tf_op jit(solution)/shard_map/ppermute | solution.py:1155
  425.9 26.8 %copy-start.8 = (bf16[128,11264]{1,0:T(8,128)(2,1)S(1)}, bf16[128,11264]{1,0:T(8,128)(2,1)}, u32[]{:S(2)}) copy-start(bf16[128,11264]{1,0:T(8,128)(2,1)} %get-tuple-element.65) | copy-start | bytes 8650756
  452.7 10.5 %collective-permute-start.20 = (bf16[128,2688]{1,0:T(8,128)(2,1)}, bf16[128,2688]{1,0:T(8,128)(2,1)S(1)}, u32[]{:S(2)}, u32[]{:S(2)}) collective-permute-start(bf16[128,2688]{1,0:T(8,128)(2,1)} %constant_dynamic-slice_fusion.1), channel_id=1, source_target_pairs={{0,2},{2,0},{4,6},{6,4},{8,10},{10,8},{12,14},{14,12},{16,18},{18,... | collective-permute-start | bytes 2064392 | tf_op jit(solution)/shard_map/ppermute | solution.py:1155
  453.9 12.0 %collective-permute-start.23 = (bf16[128,5632]{1,0:T(8,128)(2,1)}, bf16[128,5632]{1,0:T(8,128)(2,1)}, u32[]{:S(2)}, u32[]{:S(2)}) collective-permute-start(bf16[128,5632]{1,0:T(8,128)(2,1)} %constant_dynamic-slice_fusion), channel_id=1, source_target_pairs={{0,2},{2,0},{4,6},{6,4},{8,10},{10,8},{12,14},{14,12},{16,18},{18,... | collective-permute-start | bytes 4325384 | tf_op jit(solution)/shard_map/ppermute | solution.py:1155
  458.2 5.0 copy-start.9
  458.2 53.6 %all-to-all-start.1 = ((bf16[32,32,1024]{2,1,0:T(8,128)(2,1)}), bf16[32,32,1024]{2,1,0:T(8,128)(2,1)}, u32[]{:S(2)}, u32[]{:S(2)}) async-start(bf16[32,32,1024]{2,1,0:T(8,128)(2,1)} %bitcast.19), calls=%async_computation.1 | async-start | bytes 4194304 | tf_op jit(solution)/shard_map/all_to_all | solution.py:1244
  464.2 25.9 %collective-permute-start.21 = (bf16[64,2688]{1,0:T(8,128)(2,1)}, bf16[64,2688]{1,0:T(8,128)(2,1)S(1)}, u32[]{:S(2)}, u32[]{:S(2)}) collective-permute-start(bf16[64,2688]{1,0:T(8,128)(2,1)} %dynamic-slice_convert_fusion.1), channel_id=1, source_target_pairs={{0,1},{1,0},{2,3},{3,2},{4,5},{5,4},{6,7},{7,6},{8,9},{9,8},{10,11... | collective-permute-start | bytes 1032200 | tf_op jit(solution)/shard_map/ppermute | solution.py:1151
  469.0 46.6 %collective-permute-start.24 = (bf16[64,5632]{1,0:T(8,128)(2,1)}, bf16[64,5632]{1,0:T(8,128)(2,1)}, u32[]{:S(2)}, u32[]{:S(2)}) collective-permute-start(bf16[64,5632]{1,0:T(8,128)(2,1)} %dynamic-slice_convert_fusion), channel_id=1, source_target_pairs={{0,1},{1,0},{2,3},{3,2},{4,5},{5,4},{6,7},{7,6},{8,9},{9,8},{10,11... | collective-permute-start | bytes 2162696 | tf_op jit(solution)/shard_map/ppermute | solution.py:1151
  511.9 14.6 %all-to-all-start.4 = ((bf16[8,8,2688]{2,1,0:T(8,128)(2,1)}), bf16[8,8,2688]{2,1,0:T(8,128)(2,1)S(1)}, u32[]{:S(2)}, u32[]{:S(2)}) async-start(bf16[8,8,2688]{2,1,0:T(8,128)(2,1)} %fusion.29), calls=%async_computation.4 | async-start | bytes 688128 | tf_op jit(solution)/shard_map/all_to_all | solution.py:1202
  526.5 22.4 %all-to-all-start.6 = ((bf16[8,8,5632]{2,1,0:T(8,128)(2,1)}), bf16[8,8,5632]{2,1,0:T(8,128)(2,1)S(1)}, u32[]{:S(2)}, u32[]{:S(2)}) async-start(bf16[8,8,5632]{2,1,0:T(8,128)(2,1)} %fusion.26), calls=%async_computation.6 | async-start | bytes 1441792 | tf_op jit(solution)/shard_map/all_to_all | solution.py:1202
  549.6 14.4 %all-to-all-start.5 = ((bf16[8,8,2688]{2,1,0:T(8,128)(2,1)}), bf16[8,8,2688]{2,1,0:T(8,128)(2,1)S(1)}, u32[]{:S(2)}, u32[]{:S(2)}) async-start(bf16[8,8,2688]{2,1,0:T(8,128)(2,1)} %broadcast_in_dim.102), calls=%async_computation.5 | async-start | bytes 688128 | tf_op jit(solution)/shard_map/all_to_all | solution.py:1211
  564.9 22.3 %all-to-all-start.7 = ((bf16[8,8,5632]{2,1,0:T(8,128)(2,1)}), bf16[8,8,5632]{2,1,0:T(8,128)(2,1)S(1)}, u32[]{:S(2)}, u32[]{:S(2)}) async-start(bf16[8,8,5632]{2,1,0:T(8,128)(2,1)} %broadcast_in_dim.103), calls=%async_computation.7 | async-start | bytes 1441792 | tf_op jit(solution)/shard_map/all_to_all | solution.py:1211
  587.3 52.4 %all-to-all-start.3 = ((bf16[32,32,1024]{2,1,0:T(8,128)(2,1)}), bf16[32,32,1024]{2,1,0:T(8,128)(2,1)S(1)}, u32[]{:S(2)}, u32[]{:S(2)}) async-start(bf16[32,32,1024]{2,1,0:T(8,128)(2,1)} %bitcast.25), calls=%async_computation.3 | async-start | bytes 4194304 | tf_op jit(solution)/shard_map/all_to_all | solution.py:1244
  591.0 6.0 collective-permute-start.22
  596.8 47.3 %collective-permute-start.25 = (bf16[64,5632]{1,0:T(8,128)(2,1)S(1)}, bf16[64,5632]{1,0:T(8,128)(2,1)}, u32[]{:S(2)}, u32[]{:S(2)}) collective-permute-start(bf16[64,5632]{1,0:T(8,128)(2,1)S(1)} %bitcast.54), channel_id=1, source_target_pairs={{0,2},{2,0},{4,6},{6,4},{8,10},{10,8},{12,14},{14,12},{16,18},{18,... | collective-permute-start | bytes 2162696 | tf_op jit(solution)/shard_map/ppermute | solution.py:1155
  (15 other events, 43.9 us)

commit v2 on v1

--- a/solution.py
+++ b/solution.py
@@ -26,6 +26,9 @@
 CONV_C = slice(2304, 4096)
 STEP_C = slice(4096, 4224)
 UNITED = 4224
+GIVEN = 4120
+TAIL_AT = DSSM + XBC
+STEP_W = 24
 
 
 def dot_nn(a, b):
@@ -63,7 +66,7 @@
 
 
 def sigmoid(value):
-    return 1.0 / (1.0 + jnp.exp(-value))
+    return 0.5 * jnp.tanh(0.5 * value) + 0.5
 
 
 def iota2(dim):
@@ -202,11 +205,8 @@
     conv_ref = united_ref.at[:, CONV_C]
     step_ref = united_ref.at[:, STEP_C]
     before_ref = above_ref.at[:, CONV_C]
-    dgate_ref = dunited_ref.at[:, GATE_C]
-    dconv_ref = dunited_ref.at[:, CONV_C]
-    dstep_ref = dunited_ref.at[:, STEP_C]
-    dunited_ref[:, QUERY_C] = dquery_ref[...]
-    dunited_ref[:, KV_C] = dkv_ref[...]
+    dgate_ref = dunited_ref.at[:, :DSSM]
+    dconv_ref = dunited_ref.at[:, DSSM:TAIL_AT]
     chunks = pl.num_programs(0)
     chunk = chunks - 1 - pl.program_id(0)
     following = jnp.minimum(chunk + 1, chunks - 1)
@@ -330,7 +330,13 @@
     )[0:1, :]
     dslopes = dot_exact(upper.astype(F32), drunning)
     ddelta = gather_heads(cross_s[...], wide_ref[...]) - decay_ref[0:1, :] * dslopes
-    dstep_ref[...] = (ddelta * sigmoid(step)).astype(BF16)
+    dstep = ddelta * sigmoid(step)
+    attention = jnp.concatenate(
+        [dquery_ref[...].astype(F32), dkv_ref[...].astype(F32), jnp.zeros((SPAN, SPAN), F32)], axis=1
+    )
+    attention = pltpu.roll(attention, STEP_W, 1)
+    dunited_ref[:, TAIL_AT : TAIL_AT + SPAN] = (attention[:, :SPAN] + dstep).astype(BF16)
+    dunited_ref[:, TAIL_AT + SPAN :] = attention[:, SPAN:].astype(BF16)
 
     for number in range(XBC // 128):
         cols = strip(number)
@@ -717,54 +723,115 @@
 QUARTERS = 4
 ADAPT_SCALE = 0.5
 COLUMN_STEP = 512
-MIXER = (D, UNITED, 0)
-MERGE = (MIX, D, D)
-EXPAND = (D, 2 * FF, D + MIX)
-REDUCE = (FF, D, 2 * D + MIX)
+MERGE = (MIX, D, D, 4)
+EXPAND = (D, 2 * FF, D + MIX, 4)
+REDUCE = (FF, D, 2 * D + MIX, 2)
+MIXER_CHUNKS = (slice(0, 2048), slice(2048, 4128))
+OWN_ROWS = 4112
 LOWER_W = 2 * D + MIX + FF
-PIECES = 3 + 2 * QUARTERS
-COPIES = 3 + 3 * QUARTERS
+FACTORS_W = LOWER_W + UNITED
+
+
+def piece_count(shape):
+    return 3 + QUARTERS + shape[3]
+
+
+def copy_count(shape):
+    return 3 + QUARTERS + 2 * shape[3]
+
+
+MIXER_PIECES = 3 + QUARTERS + QUARTERS * len(MIXER_CHUNKS)
+MIXER_COPIES = 4 + 2 * QUARTERS + QUARTERS * len(MIXER_CHUNKS)
+
+
+def taken(rest, *counts):
+    sets = []
+    for count in counts:
+        sets.append(rest[:count])
+        rest = rest[count:]
+    return (*sets, rest)
 
 
 def weight_scratch(shape):
     return [
-        pltpu.VMEM((shape[0], shape[1]), BF16),
-        pltpu.VMEM((RANKS, shape[1]), BF16),
+        pltpu.VMEM((shape[0] + RANKS, shape[1]), BF16),
         pltpu.VMEM((RANKS, shape[0]), BF16),
-        pltpu.SemaphoreType.DMA((COPIES,)),
+        pltpu.SemaphoreType.DMA((copy_count(shape),)),
     ]
 
 
+def mixer_scratch():
+    return [
+        pltpu.VMEM((UNITED, D), BF16),
+        pltpu.VMEM((RANKS, UNITED), BF16),
+        pltpu.VMEM((RANKS, D), BF16),
+        pltpu.SemaphoreType.DMA((MIXER_COPIES,)),
+    ]
+
+
+def rows_at(start, count):
+    return pl.ds(pl.multiple_of(start, 16), count)
+
+
+def with_sems(jobs, sems):
+    return [pltpu.make_async_copy(src, dst, sems.at[i]) for i, (src, dst) in enumerate(jobs)]
+
+
+def factor_jobs(info_ref, own, sent, source, target):
+    side = info_ref[0]
+    half = RANKS // 2
+    jobs = [(own.at[:, source], target.at[rows_at(side * half, half), :])]
+    for number, piece in enumerate(sent):
+        base = (1 - side) * half + info_ref[1 + number] * 16
+        jobs.append((piece.at[:, source], target.at[rows_at(base, 16), :]))
+    return jobs
+
+
 def weight_copies(info_ref, shape, pieces, scratch):
-    depth, _, column = shape
-    own_w, own_u, own_l = pieces[:3]
-    sent = pieces[3 : 3 + QUARTERS]
-    sent_l = pieces[3 + QUARTERS :]
+    depth, _, column, parts = shape
+    own_l, *sent_l = pieces[: 1 + QUARTERS]
+    own_w, own_u, *sent_w = pieces[1 + QUARTERS :]
+    weight, lower, sems = scratch
+    side = info_ref[0]
+    half, part, few = depth // 2, depth // 2 // parts, RANKS // 2 // parts
+    jobs = factor_jobs(info_ref, own_l, sent_l, pl.ds(column, depth), lower)
+    jobs.append((own_w, weight.at[rows_at(side * half, half), :]))
+    jobs.append((own_u, weight.at[rows_at(depth + side * (RANKS // 2), RANKS // 2), :]))
+    for number, sent in enumerate(sent_w):
+        place = info_ref[(1 if parts == QUARTERS else 1 + QUARTERS) + number]
+        start = (1 - side) * half + place * part
+        base = depth + (1 - side) * (RANKS // 2) + place * few
+        jobs.append((sent.at[pl.ds(0, part), :], weight.at[rows_at(start, part), :]))
+        jobs.append((sent.at[pl.ds(part, few), :], weight.at[rows_at(base, few), :]))
+    return with_sems(jobs, sems)
+
+
+def mixer_copies(info_ref, pieces, scratch):
+    own_l, *sent_l = pieces[: 1 + QUARTERS]
+    own_w, own_end, *sent_w = pieces[1 + QUARTERS :]
     weight, upper, lower, sems = scratch
     side = info_ref[0]
-    columns = pl.ds(column, depth)
-
-    def rows(start, count):
-        return pl.ds(pl.multiple_of(start, 16), count)
-
-    jobs = [
-        (own_w, weight.at[rows(side * (depth // 2), depth // 2), :]),
-        (own_u, upper.at[rows(side * (RANKS // 2), RANKS // 2), :]),
-        (own_l.at[:, columns], lower.at[rows(side * (RANKS // 2), RANKS // 2), :]),
-    ]
-    part = depth // 8
+    half, part = D // 2, D // 2 // QUARTERS
+
+    def lanes_at(start, count):
+        return pl.ds(pl.multiple_of(start, 128), count)
+
+    jobs = factor_jobs(info_ref, own_l, sent_l, pl.ds(0, D), lower)
+    jobs += factor_jobs(info_ref, own_l, sent_l, pl.ds(LOWER_W, UNITED), upper)
+    mine = lanes_at(side * half, half)
+    jobs.append((own_w.at[pl.ds(0, OWN_ROWS), :], weight.at[pl.ds(0, OWN_ROWS), mine]))
+    jobs.append((own_end, weight.at[pl.ds(OWN_ROWS, 16), mine]))
     for number in range(QUARTERS):
-        place = info_ref[1 + number]
-        base = (1 - side) * (RANKS // 2) + place * 16
-        jobs += [
-            (
-                sent[number].at[pl.ds(0, part), :],
-                weight.at[rows((1 - side) * (depth // 2) + place * part, part), :],
-            ),
-            (sent[number].at[pl.ds(part, 16), :], upper.at[rows(base, 16), :]),
-            (sent_l[number].at[:, columns], lower.at[rows(base, 16), :]),
-        ]
-    return [pltpu.make_async_copy(src, dst, sems.at[i]) for i, (src, dst) in enumerate(jobs)]
+        theirs = lanes_at((1 - side) * half + info_ref[1 + number] * part, part)
+        for chunk, cols in enumerate(MIXER_CHUNKS):
+            jobs.append((sent_w[chunk * QUARTERS + number], weight.at[cols, theirs]))
+    return with_sems(jobs, sems)
+
+
+def start_mixer(copies, weight):
+    start_all(copies)
+    end = MIXER_CHUNKS[-1].stop
+    weight[end:, :] = jnp.zeros((UNITED - end, D), BF16)
 
 
 def at_first(action):
@@ -808,13 +875,17 @@
     return [slice(at, min(at + COLUMN_STEP, width)) for at in range(0, width, COLUMN_STEP)]
 
 
+def beside_half(hidden, mid):
+    return jnp.concatenate([hidden, halved(mid)], axis=1)
+
+
 def mixer_forward_kernel(info_ref, x_ref, mask_ref, gain_ref, *rest):
-    pieces = rest[:PIECES]
-    united_ref, hidden_ref, mid_ref = rest[PIECES : PIECES + 3]
-    scratch = rest[PIECES + 3 :]
+    pieces, rest = taken(rest, MIXER_PIECES)
+    united_ref, hidden_ref, mid_ref = rest[:3]
+    scratch = rest[3:]
     weight, upper, lower, _ = scratch
-    copies = weight_copies(info_ref, MIXER, pieces, scratch)
-    at_first(lambda: start_all(copies))
+    copies = mixer_copies(info_ref, pieces, scratch)
+    at_first(lambda: start_mixer(copies, weight))
     value = x_ref[...].astype(F32)
     hidden = (value * norm_scale(value) * gain_ref[0:1, :]).astype(BF16)
     hidden_ref[...] = hidden
@@ -822,16 +893,42 @@
     mid = masked(dot_nt(hidden, lower[...]), mask_ref[...].astype(F32))
     mid_ref[...] = mid
     half = halved(mid)
-    for cols in columns_of(UNITED):
-        united_ref[:, cols] = dot_nn(hidden, weight[:, cols]) + dot_nn(half, upper[:, cols])
-
-
-def block_forward_kernel(info_ref, joined_ref, x_ref, mask_ref, gain_ref, *rest):
-    merge_p, expand_p, reduce_p = (rest[i * PIECES : (i + 1) * PIECES] for i in range(3))
-    rest = rest[3 * PIECES :]
-    mixed_ref, middle_ref, second_ref, lit_ref, up_ref, mids_ref = rest[:6]
-    merge_s, expand_s, reduce_s = (rest[6 + 4 * i : 10 + 4 * i] for i in range(3))
-    active_s = rest[18]
+
+    def projected(cols):
+        return dot_nt(hidden, weight[cols, :]) + dot_nn(half, upper[:, cols])
+
+    for start, end, shift in ((0, DSSM, 0), (DSSM, TAIL_AT, CONV_C.start - DSSM)):
+        for at in range(start, end, COLUMN_STEP):
+            cols = slice(at, min(at + COLUMN_STEP, end))
+            united_ref[:, cols.start + shift : cols.stop + shift] = projected(cols)
+    tail = projected(slice(TAIL_AT, UNITED))
+    width = tail.shape[1]
+    united_ref[:, DSSM : CONV_C.start] = pltpu.roll(tail, width - STEP_W, 1)[
+        :, : CONV_C.start - DSSM
+    ]
+    steps = tail[:, :SPAN]
+    united_ref[:, STEP_C] = jnp.where(lanes_of(steps.shape) < STEP_W, steps, 0.0)
+
+
+MERGE_L, MERGE_U = slice(0, MIX), slice(MIX, MIX + D)
+EXPAND_L, EXPAND_U = slice(MIX + D, MIX + 2 * D), slice(MIX + 2 * D, MIX + 2 * D + 2 * FF)
+REDUCE_L = slice(MIX + 2 * D + 2 * FF, MIX + 2 * D + 3 * FF)
+REDUCE_U = slice(MIX + 2 * D + 3 * FF, MIX + 3 * D + 3 * FF)
+GRADS_W = MIX + 3 * D + 3 * FF
+
+
+def add_factor_grads(total, lower_cols, upper_cols, grad_mid, hidden, mid, grad):
+    gm_t = grad_mid.astype(F32).T.astype(BF16)
+    mid_t = (mid.astype(F32) * ADAPT_SCALE).T.astype(BF16)
+    total[:, lower_cols] += dot_nn(gm_t, hidden)
+    total[:, upper_cols] += dot_nn(mid_t, grad)
+
+
+def block_kernel(info_ref, joined_ref, x_ref, grad_ref, mask_ref, gain_ref, *rest):
+    merge_p, expand_p, reduce_p, rest = taken(rest, *map(piece_count, (MERGE, EXPAND, REDUCE)))
+    mixed_ref, dmamba_ref, dattended_ref, dmiddle_ref, grads_ref = rest[:5]
+    merge_s, expand_s, reduce_s = (rest[5 + 3 * i : 8 + 3 * i] for i in range(3))
+    lit_s, up_s, active_s, dexpanded_s, total = rest[14:]
     sets = [
         weight_copies(info_ref, shape, pieces, scratch)
         for shape, pieces, scratch in (
@@ -840,84 +937,6 @@
             (REDUCE, reduce_p, reduce_s),
         )
     ]
-    at_first(lambda: start_all(sum(sets, [])))
-    mask = mask_ref[...].astype(F32)
-
-    at_first(lambda: wait_all(sets[0]))
-    weight, upper, lower, _ = merge_s
-    joined = joined_ref[...]
-    mid = masked(dot_nt(joined, lower[...]), mask)
-    mids_ref[:, 0:RANKS] = mid
-    middle = x_ref[...].astype(F32) + (
-        dot_nn(joined, weight[...]) + dot_nn(halved(mid), upper[...])
-    )
-    middle_ref[...] = middle
-    second = (middle * norm_scale(middle) * gain_ref[0:1, :]).astype(BF16)
-    second_ref[...] = second
-
-    at_first(lambda: wait_all(sets[1]))
-    weight, upper, lower, _ = expand_s
-    mid = masked(dot_nt(second, lower[...]), mask)
-    mids_ref[:, RANKS : 2 * RANKS] = mid
-    half = halved(mid)
-    for cols in columns_of(FF):
-        beside = slice(FF + cols.start, FF + cols.stop)
-        lit = dot_nn(second, weight[:, cols]) + dot_nn(half, upper[:, cols])
-        up = dot_nn(second, weight[:, beside]) + dot_nn(half, upper[:, beside])
-        lit_ref[:, cols] = lit
-        up_ref[:, cols] = up
-        active_s[:, cols] = (lit * sigmoid(lit) * up).astype(BF16)
-
-    at_first(lambda: wait_all(sets[2]))
-    weight, upper, lower, _ = reduce_s
-    active = active_s[...]
-    mid = masked(dot_nt(active, lower[...]), mask)
-    mids_ref[:, 2 * RANKS :] = mid
-    mixed_ref[...] = (
-        middle_ref[...] + (dot_nn(active, weight[...]) + dot_nn(halved(mid), upper[...]))
-    ).astype(BF16)
-
-
-MERGE_L, MERGE_U = slice(0, MIX), slice(MIX, MIX + D)
-EXPAND_L, EXPAND_U = slice(MIX + D, MIX + 2 * D), slice(MIX + 2 * D, MIX + 2 * D + 2 * FF)
-REDUCE_L = slice(MIX + 2 * D + 2 * FF, MIX + 2 * D + 3 * FF)
-REDUCE_U = slice(MIX + 2 * D + 3 * FF, MIX + 3 * D + 3 * FF)
-GRADS_W = MIX + 3 * D + 3 * FF
-
-
-def add_factor_grads(total, lower_cols, upper_cols, grad_mid, hidden, mid, grad):
-    gm_t = grad_mid.astype(F32).T.astype(BF16)
-    mid_t = (mid.astype(F32) * ADAPT_SCALE).T.astype(BF16)
-    total[:, lower_cols] += dot_nn(gm_t, hidden)
-    total[:, upper_cols] += dot_nn(mid_t, grad)
-
-
-def block_backward_kernel(
-    info_ref,
-    grad_ref,
-    joined_ref,
-    middle_ref,
-    second_ref,
-    lit_ref,
-    up_ref,
-    mids_ref,
-    mask_ref,
-    gain_ref,
-    *rest,
-):
-    reduce_p, expand_p, merge_p = (rest[i * PIECES : (i + 1) * PIECES] for i in range(3))
-    rest = rest[3 * PIECES :]
-    dmamba_ref, dattended_ref, dmiddle_ref, grads_ref = rest[:4]
-    reduce_s, expand_s, merge_s = (rest[4 + 4 * i : 8 + 4 * i] for i in range(3))
-    active_s, dlit_s, total = rest[16:]
-    sets = [
-        weight_copies(info_ref, shape, pieces, scratch)
-        for shape, pieces, scratch in (
-            (REDUCE, reduce_p, reduce_s),
-            (EXPAND, expand_p, expand_s),
-            (MERGE, merge_p, merge_s),
-        )
-    ]
 
     def begin():
         for copies in sets:
@@ -926,59 +945,68 @@
 
     at_first(begin)
     mask = mask_ref[...].astype(F32)
+    gain = gain_ref[0:1, :]
 
     at_first(lambda: wait_all(sets[0]))
-    weight, upper, lower, _ = reduce_s
+    weight, lower, _ = merge_s
+    joined = joined_ref[...]
+    merge_mid = masked(dot_nt(joined, lower[...]), mask)
+    middle = x_ref[...].astype(F32) + dot_nn(beside_half(joined, merge_mid), weight[...])
+    second = (middle * norm_scale(middle) * gain).astype(BF16)
+
+    at_first(lambda: wait_all(sets[1]))
+    weight, lower, _ = expand_s
+    expand_mid = masked(dot_nt(second, lower[...]), mask)
+    both = beside_half(second, expand_mid)
+    for cols in columns_of(FF):
+        lit = dot_nn(both, weight[:, cols])
+        up = dot_nn(both, weight[:, FF + cols.start : FF + cols.stop])
+        lit_s[:, cols] = lit
+        up_s[:, cols] = up
+        active_s[:, cols] = (lit * sigmoid(lit) * up).astype(BF16)
+
+    at_first(lambda: wait_all(sets[2]))
+    weight, lower, _ = reduce_s
+    active = active_s[...]
+    reduce_mid = masked(dot_nt(active, lower[...]), mask)
+    mixed_ref[...] = (middle + dot_nn(beside_half(active, reduce_mid), weight[...])).astype(BF16)
+
     grad = grad_ref[...]
-    grad_mid = masked(ADAPT_SCALE * dot_nt(grad, upper[...]), mask)
+    grad_mid = masked(ADAPT_SCALE * dot_nt(grad, weight[FF:, :]), mask)
     for cols in columns_of(FF):
-        beside = slice(FF + cols.start, FF + cols.stop)
         dactive = dot_nt(grad, weight[cols, :]) + dot_nn(grad_mid, lower[:, cols])
-        lit = lit_ref[:, cols]
-        up = up_ref[:, cols]
+        lit = lit_s[:, cols]
+        up = up_s[:, cols]
         ratio = sigmoid(lit)
         glow = lit * ratio
-        active_s[:, cols] = (glow * up).astype(BF16)
-        dlit_s[:, cols] = (dactive * up * (ratio * (1.0 + lit * (1.0 - ratio)))).astype(BF16)
-        dlit_s[:, beside] = (dactive * glow).astype(BF16)
-    add_factor_grads(
-        total, REDUCE_L, REDUCE_U, grad_mid, active_s[...], mids_ref[:, 2 * RANKS :], grad
-    )
-
-    at_first(lambda: wait_all(sets[1]))
-    weight, upper, lower, _ = expand_s
-    dexpanded = dlit_s[...]
-    grad_mid = masked(ADAPT_SCALE * dot_nt(dexpanded, upper[...]), mask)
-    dsecond = dot_nt(dexpanded, weight[...]) + dot_nn(grad_mid, lower[...])
-    dmiddle = grad.astype(F32) + norm_back(dsecond, middle_ref[...], gain_ref[0:1, :])
+        dexpanded_s[:, cols] = (dactive * up * (ratio + glow * (1.0 - ratio))).astype(BF16)
+        dexpanded_s[:, FF + cols.start : FF + cols.stop] = (dactive * glow).astype(BF16)
+    add_factor_grads(total, REDUCE_L, REDUCE_U, grad_mid, active, reduce_mid, grad)
+
+    weight, lower, _ = expand_s
+    dexpanded = dexpanded_s[...]
+    grad_mid = masked(ADAPT_SCALE * dot_nt(dexpanded, weight[D:, :]), mask)
+    dsecond = dot_nt(dexpanded, weight[:D, :]) + dot_nn(grad_mid, lower[...])
+    dmiddle = grad.astype(F32) + norm_back(dsecond, middle, gain)
     dmiddle_ref[...] = dmiddle
-    add_factor_grads(
-        total,
-        EXPAND_L,
-        EXPAND_U,
-        grad_mid,
-        second_ref[...],
-        mids_ref[:, RANKS : 2 * RANKS],
-        dexpanded,
-    )
-
-    at_first(lambda: wait_all(sets[2]))
-    weight, upper, lower, _ = merge_s
-    grad = dmiddle_ref[...].astype(BF16)
-    grad_mid = masked(ADAPT_SCALE * dot_nt(grad, upper[...]), mask)
+    add_factor_grads(total, EXPAND_L, EXPAND_U, grad_mid, second, expand_mid, dexpanded)
+
+    weight, lower, _ = merge_s
+    grad = dmiddle.astype(BF16)
+    grad_mid = masked(ADAPT_SCALE * dot_nt(grad, weight[MIX:, :]), mask)
     for cols in columns_of(MIX):
         djoined = dot_nt(grad, weight[cols, :]) + dot_nn(grad_mid, lower[:, cols])
         if cols.start < DSSM:
             dmamba_ref[:, cols] = djoined
         else:
             dattended_ref[...] = djoined.astype(BF16)
-    add_factor_grads(
-        total, MERGE_L, MERGE_U, grad_mid, joined_ref[...], mids_ref[:, 0:RANKS], grad
-    )
+    add_factor_grads(total, MERGE_L, MERGE_U, grad_mid, joined, merge_mid, grad)
 
     @pl.when(pl.program_id(0) == pl.num_programs(0) - 1)
     def _():
-        grads_ref[...] = total[...].astype(BF16)
+        half = total.shape[1] // 2
+        for place in range(2):
+            grads_ref[place] = total[:, place * half : (place + 1) * half].astype(BF16)
 
 
 MIXER_GRADS_W = D + UNITED + 128
@@ -987,22 +1015,22 @@
 def mixer_backward_kernel(
     info_ref, grad_ref, hidden_ref, x_ref, dmiddle_ref, mid_ref, mask_ref, gain_ref, *rest
 ):
-    pieces = rest[:PIECES]
-    out_ref, grads_ref = rest[PIECES : PIECES + 2]
-    scratch = rest[PIECES + 2 : PIECES + 6]
-    total = rest[PIECES + 6]
+    pieces, rest = taken(rest, MIXER_PIECES)
+    out_ref, grads_ref = rest[:2]
+    scratch = rest[2:6]
+    total = rest[6]
     weight, upper, lower, _ = scratch
-    copies = weight_copies(info_ref, MIXER, pieces, scratch)
+    copies = mixer_copies(info_ref, pieces, scratch)
 
     def begin():
-        start_all(copies)
+        start_mixer(copies, weight)
         total[...] = jnp.zeros_like(total)
 
     at_first(begin)
     at_first(lambda: wait_all(copies))
     grad = grad_ref[...]
     grad_mid = masked(ADAPT_SCALE * dot_nt(grad, upper[...]), mask_ref[...].astype(F32))
-    dhidden = dot_nt(grad, weight[...]) + dot_nn(grad_mid, lower[...])
+    dhidden = dot_nn(grad, weight[...]) + dot_nn(grad_mid, lower[...])
     value = x_ref[...].astype(F32)
     out_ref[...] = (dmiddle_ref[...] + norm_back(dhidden, value, gain_ref[0:1, :])).astype(BF16)
     add_factor_grads(
@@ -1017,7 +1045,9 @@
 
     @pl.when(pl.program_id(0) == pl.num_programs(0) - 1)
     def _():
-        grads_ref[...] = total[...].astype(BF16)
+        half = total.shape[1] // 2
+        for place in range(2):
+            grads_ref[place] = total[:, place * half : (place + 1) * half].astype(BF16)
 
 
 def row_call(kernel, rows, ins, fixed_ins, raw, outs, fixed_outs, scratch, info, name, flops, moved):
@@ -1055,7 +1085,7 @@
         pieces,
         [(UNITED, F32), (D, BF16), (RANKS, BF16)],
         [],
-        weight_scratch(MIXER),
+        mixer_scratch(),
         info,
         "mixer_forward",
         2 * rows * D * UNITED,
@@ -1063,49 +1093,30 @@
     )
 
 
-def block_forward(info, joined, x, mask, gain, merge_p, expand_p, reduce_p):
+def block(info, joined, x, grad, mask, gain, merge_p, expand_p, reduce_p):
     rows = x.shape[0]
     return row_call(
-        block_forward_kernel,
+        block_kernel,
         rows,
-        [joined, x, mask],
+        [joined, x, grad, mask],
         [gain[None, :]],
         [*merge_p, *expand_p, *reduce_p],
-        [(D, BF16), (D, F32), (D, BF16), (FF, F32), (FF, F32), (3 * RANKS, BF16)],
-        [],
+        [(D, BF16), (DSSM, F32), (MIX - DSSM, BF16), (D, F32)],
+        [(2, RANKS, GRADS_W // 2)],
         weight_scratch(MERGE)
         + weight_scratch(EXPAND)
         + weight_scratch(REDUCE)
-        + [pltpu.VMEM((ROW_BLOCK, FF), BF16)],
-        info,
-        "block_forward",
-        2 * rows * D * (MIX + 3 * FF),
-        2 * D * (MIX + 3 * FF) + 12 * rows * FF,
-    )
-
-
-def block_backward(info, grad, joined, middle, second, lit, up, mids, mask, gain, merge_p, expand_p, reduce_p):
-    rows = grad.shape[0]
-    return row_call(
-        block_backward_kernel,
-        rows,
-        [grad, joined, middle, second, lit, up, mids, mask],
-        [gain[None, :]],
-        [*reduce_p, *expand_p, *merge_p],
-        [(DSSM, F32), (MIX - DSSM, BF16), (D, F32)],
-        [(RANKS, GRADS_W)],
-        weight_scratch(REDUCE)
-        + weight_scratch(EXPAND)
-        + weight_scratch(MERGE)
         + [
+            pltpu.VMEM((ROW_BLOCK, FF), F32),
+            pltpu.VMEM((ROW_BLOCK, FF), F32),
             pltpu.VMEM((ROW_BLOCK, FF), BF16),
             pltpu.VMEM((ROW_BLOCK, 2 * FF), BF16),
             pltpu.VMEM((RANKS, GRADS_W), F32),
         ],
         info,
-        "block_backward",
-        2 * rows * D * (MIX + 3 * FF),
-        2 * D * (MIX + 3 * FF) + 12 * rows * FF,
+        "block",
+        5 * rows * D * (MIX + 3 * FF),
+        2 * D * (MIX + 3 * FF) + 12 * rows * D,
     )
 
 
@@ -1118,8 +1129,8 @@
         [gain[None, :]],
         pieces,
         [(D, BF16)],
-        [(RANKS, MIXER_GRADS_W)],
-        weight_scratch(MIXER) + [pltpu.VMEM((RANKS, MIXER_GRADS_W), F32)],
+        [(2, RANKS, MIXER_GRADS_W // 2)],
+        mixer_scratch() + [pltpu.VMEM((RANKS, MIXER_GRADS_W), F32)],
         info,
         "mixer_backward",
         2 * rows * D * UNITED,
@@ -1129,22 +1140,19 @@
 
 SEQ_SLOTS = 3
 RANK = 16
-STEP_W = 24
 
 
 def swap_pairs(count, bit):
     return [(i, i ^ bit) for i in range(count)]
 
 
-def send_quarter(weight, upper, quarter):
-    part, own = weight.shape[0] // QUARTERS, upper.shape[0] // QUARTERS
-    return jnp.concatenate(
-        [
-            lax.dynamic_slice_in_dim(weight, quarter * part, part, 0),
-            lax.dynamic_slice_in_dim(upper, quarter * own, own, 0),
-        ],
-        axis=0,
-    )
+def part_of(value, parts, place, axis=0):
+    size = value.shape[axis] // parts
+    return lax.dynamic_slice_in_dim(value, place * size, size, axis)
+
+
+def sent_rows(weight, upper, parts, place):
+    return jnp.concatenate([part_of(weight, parts, place), part_of(upper, parts, place)], axis=0)
 
 
 def across(value):
@@ -1160,68 +1168,52 @@
     return (first, second, beside(first, 1), beside(second, 1))
 
 
-def aligned_columns(value):
-    gate, conv = value[:, :DSSM], value[:, DSSM : DSSM + XBC]
-    step = value[:, DSSM + XBC : DSSM + XBC + STEP_W]
-    attention = value[:, DSSM + XBC + STEP_W :]
-    padding = jnp.zeros((value.shape[0], SPAN - STEP_W), value.dtype)
-    return jnp.concatenate([gate, attention, conv, step, padding], axis=1)
-
-
-def given_columns(value):
-    conv_at = CONV_C.start
-    return jnp.concatenate(
-        [
-            value[:, :DSSM],
-            value[:, conv_at : conv_at + XBC],
-            value[:, STEP_C.start : STEP_C.start + STEP_W],
-            value[:, DSSM:conv_at],
-        ],
-        axis=1,
-    )
-
-
 def after(value, *others):
     return lax.optimization_barrier((value, *others))[0]
 
 
-def reduce_factors(grads):
-    rows, width = grads.shape
-    half, mine = width // 2, rows // 2
-    rep = lax.axis_index("rep")
-    side = lax.axis_index("shard")
-    core = rep % 2
-    count = lax.axis_size("rep") // 2
-    groups = [[2 * i + place for i in range(count)] for place in range(2)]
-    kept = lax.dynamic_slice_in_dim(grads, core * half, half, 1)
-    sent = lax.dynamic_slice_in_dim(grads, (1 - core) * half, half, 1)
-    total = kept.astype(F32) + beside(sent, 1).astype(F32)
+def core_sums(grads):
+    core = lax.axis_index("rep") % 2
+    kept = lax.dynamic_index_in_dim(grads, core, 0, keepdims=False)
+    sent = lax.dynamic_index_in_dim(grads, 1 - core, 0, keepdims=False)
+    return kept.astype(F32) + beside(sent, 1).astype(F32)
+
+
+def row_sums(total, side, send):
+    mine = total.shape[0] // 2
     kept = lax.dynamic_slice_in_dim(total, side * mine, mine, 0)
     sent = lax.dynamic_slice_in_dim(total, (1 - side) * mine, mine, 0).astype(BF16)
-    total = (kept + across(sent).astype(F32)).astype(BF16)
-    parts = lax.all_to_all(
-        total.reshape(count, mine // count, half),
-        "rep",
-        split_axis=0,
-        concat_axis=0,
-        axis_index_groups=groups,
-        tiled=True,
-    )
-    own = jnp.sum(parts.astype(F32), axis=0, keepdims=True).astype(BF16)
-    whole = lax.all_to_all(
-        jnp.broadcast_to(own, (count, *own.shape[1:])),
-        "rep",
-        split_axis=0,
-        concat_axis=0,
-        axis_index_groups=groups,
-        tiled=True,
-    ).reshape(mine, half)
-    other = beside(whole, 1)
+    return kept + send(sent).astype(F32)
+
+
+def shard_sums(total):
+    return row_sums(total, lax.axis_index("shard"), across)
+
+
+def chip_bits():
+    count, bits = lax.axis_size("rep") // 2, []
+    while 2 ** len(bits) < count:
+        bits.append(2 ** (len(bits) + 1))
+    return bits
+
+
+def bit_sums(total, bit):
+    return row_sums(total, lax.axis_index("rep") // bit % 2, lambda value: beside(value, bit))
+
+
+def ordered(mine, other, side, axis):
     return jnp.where(
-        core == 0,
-        jnp.concatenate([whole, other], axis=1),
-        jnp.concatenate([other, whole], axis=1),
-    ).astype(F32)
+        side == 0,
+        jnp.concatenate([mine, other], axis=axis),
+        jnp.concatenate([other, mine], axis=axis),
+    )
+
+
+def spread_rows(own, bits):
+    rep = lax.axis_index("rep")
+    for bit in reversed(bits):
+        own = ordered(own, beside(own, bit), rep // bit % 2, 0)
+    return ordered(own, beside(own, 1), rep % 2, 1)
 
 
 def row_orders(assignment, stripe, groups):
@@ -1229,8 +1221,9 @@
     per = units // groups
     total = stripe * units
     sending = jnp.arange(total, dtype=jnp.int32)
-    group, row, piece = sending // (stripe * per), sending // per % stripe, sending % per
-    source = row * units + jnp.take(assignment, group * per + piece)
+    row = sending // per % stripe
+    chosen = jnp.broadcast_to(assignment.reshape(groups, 1, per), (groups, stripe, per))
+    source = row * units + chosen.reshape(total)
     columns = jnp.arange(total, dtype=jnp.int32)
     pick = (source[:, None] == columns[None, :]).astype(BF16)
     working = jnp.arange(total, dtype=jnp.int32)
@@ -1277,7 +1270,10 @@
     rep = lax.axis_index("rep")
     side = lax.axis_index("shard")
     quarter = rep % QUARTERS
-    info = jnp.stack([side, quarter, quarter ^ 2, quarter ^ 1, quarter ^ 3]).astype(jnp.int32)
+    core = rep % 2
+    info = jnp.stack(
+        [side, quarter, quarter ^ 2, quarter ^ 1, quarter ^ 3, core, core ^ 1]
+    ).astype(jnp.int32)
 
     pick, place = row_orders(assignment, stripe, groups)
 
@@ -1287,22 +1283,27 @@
     def work_rows(value):
         return dot_nn(place, value).astype(BF16)
 
-    token_rows = exchange(send_rows(tokens))
-
-    lower_own = jnp.concatenate([mixer_down, merge_down, expand_down, reduce_down], axis=1)
-    lower_sent = lax.dynamic_slice_in_dim(lower_own, quarter * RANK, RANK, 0)
-    mixer_sent = aligned_columns(send_quarter(mixer_weight, mixer_up, quarter))
-    mixer_own = (aligned_columns(mixer_weight), aligned_columns(mixer_up))
-    lower_in = across(lower_sent)
-    mixer_in = across(mixer_sent)
-    merge_in = across(after(send_quarter(merge_weight, merge_up, quarter), mixer_in))
-    expand_in = across(after(send_quarter(expand_weight, expand_up, quarter), merge_in))
-    reduce_in = across(after(send_quarter(reduce_weight, reduce_up, quarter), expand_in))
-    lowers = spread_quarter(lower_in)
-    mixer_p = (*mixer_own, lower_own, *spread_quarter(mixer_in), *lowers)
-    merge_p = (merge_weight, merge_up, lower_own, *spread_quarter(merge_in), *lowers)
-    expand_p = (expand_weight, expand_up, lower_own, *spread_quarter(expand_in), *lowers)
-    reduce_p = (reduce_weight, reduce_up, lower_own, *spread_quarter(reduce_in), *lowers)
+    mixer_t = mixer_weight.T
+    mixer_sent = jnp.pad(part_of(mixer_t, QUARTERS, quarter, 1), ((0, 8), (0, 0)))
+    mixer_sent = [mixer_sent[cols] for cols in MIXER_CHUNKS]
+    mixer_in = [across(chunk) for chunk in mixer_sent]
+    token_rows = exchange(send_rows(after(tokens, *mixer_sent)))
+    factors = jnp.concatenate(
+        [
+            mixer_down,
+            merge_down,
+            expand_down,
+            reduce_down,
+            jnp.pad(mixer_up, ((0, 0), (0, UNITED - GIVEN))),
+        ],
+        axis=1,
+    )
+    factors_in = across(part_of(factors, QUARTERS, quarter))
+    mixer_end = jnp.pad(mixer_t[OWN_ROWS:], ((0, OWN_ROWS + 16 - GIVEN), (0, 0)))
+    grad_sent = send_rows(cotangent)
+    merge_sent = sent_rows(merge_weight, merge_up, 4, quarter)
+    expand_sent = sent_rows(expand_weight, expand_up, 4, quarter)
+    reduce_sent = sent_rows(reduce_weight, reduce_up, 2, core)
 
     finish = jnp.cumsum(lengths[0])
     begin = finish - lengths[0]
@@ -1318,19 +1319,46 @@
     cosine, sines = rotation_tables(position)
     params = ssm_params(filter_taps, filter_bias, step_bias, decay_rate, skip_gain, state_gain)
 
+    mixer_in[0], cosine, sines, mask, *_ = lax.optimization_barrier(
+        (mixer_in[0], cosine, sines, mask, mixer_end, grad_sent, merge_sent, expand_sent, reduce_sent)
+    )
+    mixer_in[1] = after(mixer_in[1], mixer_in[0])
+    merge_in = across(after(merge_sent, mixer_in[1]))
+    lowers = (factors, *spread_quarter(factors_in))
+    mixer_p = (
+        *lowers,
+        mixer_t,
+        mixer_end,
+        *spread_quarter(mixer_in[0]),
+        *spread_quarter(mixer_in[1]),
+    )
+    expand_in = across(after(expand_sent, mixer_in[1]))
     x = work_rows(token_rows)
-    grad_rows = exchange(after(send_rows(cotangent), token_rows))
+    grad_rows = exchange(after(grad_sent, token_rows))
+    merge_in = after(merge_in, x)
+    reduce_in = across(after(reduce_sent, merge_in))
     united, hidden, mixer_mid = mixer_forward(info, x, mask, first_gain, mixer_p)
+    expand_in = after(expand_in, united)
     attended, logs, turned, kv_low = attend_forward(united, cosine, sines, first)
     joined, scan, starts = mamba_forward(united, attended, restart, params)
-    mixed, middle, second, lit, up, mids = block_forward(
-        info, joined, x, mask, second_gain, merge_p, expand_p, reduce_p
-    )
-
-    def leave_rows(value):
-        return exchange(lax.dot_general(
+
+    def rest_of_quarters(first_in):
+        second = beside(first_in, 2)
+        return (first_in, second, beside(first_in, 1), beside(after(second, joined), 1))
+
+    merge_p = (*lowers, merge_weight, merge_up, *rest_of_quarters(merge_in))
+    expand_p = (*lowers, expand_weight, expand_up, *rest_of_quarters(expand_in))
+    reduce_in = after(reduce_in, joined)
+    reduce_p = (*lowers, reduce_weight, reduce_up, reduce_in, beside(reduce_in, 1))
+    grad_top = work_rows(after(grad_rows, joined))
+    mixed, dmamba, dattended, dmiddle, block_grads = block(
+        info, joined, x, grad_top, mask, second_gain, merge_p, expand_p, reduce_p
+    )
+
+    def leaving(value):
+        return lax.dot_general(
             place, value, (((0,), (0,)), ((), ())), preferred_element_type=F32
-        ).astype(BF16))
+        ).astype(BF16)
 
     def input_rows(value, kind):
         return (
@@ -1339,26 +1367,50 @@
             .reshape(stripe, units, width)
         )
 
-    mixed_rows = leave_rows(mixed)
-
-    grad_top = work_rows(grad_rows)
-    dmamba, dattended, dmiddle, block_grads = block_backward(
-        info, grad_top, joined, middle, second, lit, up, mids, mask, second_gain,
-        merge_p, expand_p, reduce_p,
-    )
-    block_final = reduce_factors(block_grads)
+    bits = chip_bits()
+    mixed_rows = exchange(leaving(mixed))
+    block_sums = core_sums(block_grads)
     dquery, dkv = attend_backward(turned, kv_low, dattended, logs, cosine, sines, first)
+    dquery, block_sums = lax.optimization_barrier((dquery, block_sums))
+    block_sums = shard_sums(block_sums)
     dunited = mamba_backward(united, scan, starts, dmamba, dquery, dkv, restart, params)
+    dunited, block_sums, mixed_rows = lax.optimization_barrier((dunited, block_sums, mixed_rows))
+    block_sums = bit_sums(block_sums, bits[0])
     work_grad, mixer_grads = mixer_backward(
         info, dunited, hidden, x, dmiddle, mixer_mid, mask, first_gain, mixer_p
     )
-    token_grads = leave_rows(work_grad)
-    mixer_final = reduce_factors(mixer_grads)
+    work_grad, block_sums = lax.optimization_barrier((work_grad, block_sums))
+    grad_leaving = leaving(work_grad)
+    token_grads = exchange(grad_leaving)
+    mixer_grads, block_sums, mixed_rows, _ = lax.optimization_barrier(
+        (mixer_grads, block_sums, mixed_rows, grad_leaving)
+    )
+
+    def finish(_, carry):
+        mixer_grads, block_sums, _ = carry
+        mixer_sums = bit_sums(shard_sums(core_sums(mixer_grads)), bits[0])
+        sums = jnp.concatenate([mixer_sums, block_sums], axis=1)
+        for bit in bits[1:]:
+            sums = bit_sums(sums, bit)
+        return mixer_grads, block_sums, spread_rows(sums.astype(BF16), bits)
+
+    width_sums = mixer_grads.shape[2] + block_sums.shape[1]
+    _, _, final = lax.fori_loop(
+        0,
+        lax.optimization_barrier(jnp.int32(1)),
+        finish,
+        (mixer_grads, block_sums, jnp.zeros((RANKS // 2, 2 * width_sums), BF16)),
+    )
+    cut = mixer_grads.shape[2]
+    final = final.reshape(RANKS // 2, 2, -1)
+    mixer_final = final[:, :, :cut].reshape(RANKS // 2, -1).astype(F32)
+    block_final = final[:, :, cut:].reshape(RANKS // 2, -1).astype(F32)
+    mixed_out = input_rows(mixed_rows, BF16)
     return (
-        input_rows(mixed_rows, BF16),
+        mixed_out,
         input_rows(token_grads, F32),
         mixer_final[:, :D],
-        given_columns(mixer_final[:, D : D + UNITED]),
+        mixer_final[:, D : D + GIVEN],
         block_final[:, MERGE_L],
         block_final[:, MERGE_U],
         block_final[:, EXPAND_L],

time: 654 us -> 534 us (0.82)
  waiting for transfers between devices: 220 us -> 159 us
  local copies, waits for them, and re-layouts: 62.1 us -> 28 us
  Pallas kernels: 263 us -> 232 us
    ppermute x19 -> x26, waiting for transfers between devices: 29.3 us -> 88.4 us  [beside(): return lax.ppermute(value, 'rep', swap_pairs(lax.axis_size('rep'), bit))]
    all_to_all x4, waiting for transfers between devices: 58.9 us -> 0.01 us  [exchange(): lax.all_to_all(value, ('rep', 'shard'), split_axis=0, concat_axis=0, tile...]
    all_to_all x4 -> x0, waiting for transfers between devices: 51.5 us -> none  [the longest x2 27.4 us: reduce_factors(): lax.all_to_all(total.reshape(count, mine // count, half), 'rep', split_ax...]
    pallas_call x4 -> x3, Pallas kernels: 161 us -> 131 us  [row_call(): pl.pallas_call(kernel, grid_spec=pltpu.PrefetchScalarGridSpec(num_scalar_...]
    all_to_all x4 -> x0, starting transfers between devices: 14.6 us -> none  [the longest x2 7.4 us: reduce_factors(): lax.all_to_all(total.reshape(count, mine // count, half), 'rep', split_ax...]
    concatenate x5 -> x1, local copies, waits for them, and re-layouts: 11.7 us -> 0.05 us  [on_device(): jnp.concatenate([mixer_down, merge_down, expand_down, reduce_down, jnp.pa...]
    unnamed x63 -> x66, local copies, waits for them, and re-layouts: 15.4 us -> 4.37 us
    ppermute x7 -> x8, waiting for transfers between devices: 80.4 us -> 70.1 us  [across(): return lax.ppermute(value, 'shard', swap_pairs(2, 1))]
  transfers between devices with their start and end apart: 34 -> 38, of which waited for: 12 -> 15; matrix products, arithmetic and copies ran while one was open for 13% -> 12% of each run, Pallas kernels for 17% -> 28%
where the time goes in v2:
time: 534 us; the launch traced here: 526 us
  Pallas kernels  232 us (43%)
  waiting for transfers between devices  159 us (30%)
  starting transfers between devices  48.9 us (9%)
  matrix products  38.7 us (7%)
  local copies, waits for them, and re-layouts  28 us (5%)
  other arithmetic  17.8 us (3%)
    pallas_call x3, Pallas kernels, row_call(): pl.pallas_call(kernel, grid_spec=pltpu.PrefetchScalarGridSpec(num_scalar_...  131 us
    ppermute x26, waiting for transfers between devices, beside(): return lax.ppermute(value, 'rep', swap_pairs(lax.axis_size('rep'), bit))  88.4 us
    ppermute x8, waiting for transfers between devices, across(): return lax.ppermute(value, 'shard', swap_pairs(2, 1))  70.1 us
    pallas_call x1, Pallas kernels, mamba_backward(): pl.pallas_call(mamba_backward_kernel, grid_spec=pltpu.PrefetchScalarGridS...  48.8 us
    pallas_call x1, Pallas kernels, mamba_forward(): pl.pallas_call(mamba_forward_kernel, grid_spec=pltpu.PrefetchScalarGridSp...  22 us
    all_to_all x4, starting transfers between devices, exchange(): lax.all_to_all(value, ('rep', 'shard'), split_axis=0, concat_axis=0, tile...  21.8 us
    dot_general x4, matrix products, dot_nn(): lax.dot_general(a, b, (((1,), (0,)), ((), ())), preferred_element_type=F32)  18 us
    ppermute x26, starting transfers between devices, beside(): return lax.ppermute(value, 'rep', swap_pairs(lax.axis_size('rep'), bit))  15.6 us
  transfers between devices with their start and end apart: 38, of which 15 were waited for; matrix products, arithmetic and copies ran while one was open for 12% of the time, Pallas kernels for 28%

profile of v2, /device:TPU:0, one launch (start us, length us, event | category | flops | bytes accessed | tf_op | source)
XLA Modules:
  0.0 526.0 jit_solution(15309785461561589621)
XLA Ops:
  3.0 3.0 collective-permute-start.9
  7.0 3.7 fusion.22
  10.7 6.5 %all-to-all-start = ((bf16[32,32,1024]{2,1,0:T(8,128)(2,1)}), bf16[32,32,1024]{2,1,0:T(8,128)(2,1)}, u32[]{:S(2)}, u32[]{:S(2)}) async-start(bf16[32,32,1024]{2,1,0:T(8,128)(2,1)} %bitcast.79), calls=%async_computation | async-start | bytes 4194304 | tf_op jit(solution)/shard_map/all_to_all | solution.py:1237
  17.5 1.8 collective-permute-start.10
  23.7 1.9 fusion.29
  29.4 3.7 fusion.23
  36.5 20.4 %collective-permute-done.10.rest_1_.rest_12_.rest_23_ = bf16[16,10368]{1,0:T(8,128)(2,1)S(1)} collective-permute-done((bf16[16,10368]{1,0:T(8,128)(2,1)S(1)}, bf16[16,10368]{1,0:T(8,128)(2,1)S(1)}, u32[]{:S(2)}, u32[]{:S(2)}) %collective-permute-start.10) | collective-permute-done | bytes 331808 | tf_op jit(solution)/shard_map/ppermute | solution.py:1159
  60.5 8.7 %collective-permute-done.11.rest_2_.rest_13_.rest_24_ = bf16[16,10368]{1,0:T(8,128)(2,1)} collective-permute-done((bf16[16,10368]{1,0:T(8,128)(2,1)S(1)}, bf16[16,10368]{1,0:T(8,128)(2,1)}, u32[]{:S(2)}, u32[]{:S(2)}) %collective-permute-start.11) | collective-permute-done | bytes 331808 | tf_op jit(solution)/shard_map/ppermute | solution.py:1163
  69.8 10.6 %collective-permute-done.14.rest_8_ = bf16[2048,128]{1,0:T(8,128)(2,1)} collective-permute-done((bf16[2048,128]{1,0:T(8,128)(2,1)}, bf16[2048,128]{1,0:T(8,128)(2,1)}, u32[]{:S(2)}, u32[]{:S(2)}) %collective-permute-start.14) | collective-permute-done | bytes 524320 | tf_op jit(solution)/shard_map/ppermute | solution.py:1163
  80.4 9.8 %collective-permute-done.18.rest_12_ = bf16[2080,128]{1,0:T(8,128)(2,1)} collective-permute-done((bf16[2080,128]{1,0:T(8,128)(2,1)}, bf16[2080,128]{1,0:T(8,128)(2,1)}, u32[]{:S(2)}, u32[]{:S(2)}) %collective-permute-start.18) | collective-permute-done | bytes 532512 | tf_op jit(solution)/shard_map/ppermute | solution.py:1163
  91.1 6.3 %all-to-all-start.1 = ((bf16[32,32,1024]{2,1,0:T(8,128)(2,1)}), bf16[32,32,1024]{2,1,0:T(8,128)(2,1)}, u32[]{:S(2)}, u32[]{:S(2)}) async-start(bf16[32,32,1024]{2,1,0:T(8,128)(2,1)} %bitcast.78), calls=%async_computation.1 | async-start | bytes 4194304 | tf_op jit(solution)/shard_map/all_to_all | solution.py:1237
  97.4 1.9 collective-permute-start.25
  99.3 5.3 %fusion.25.x_ref = bf16[1024,1024]{1,0:T(8,128)(2,1)} fusion(bf16[1024,1024]{1,0:T(8,128)(2,1)} %bitcast.16, s32[1024]{0:T(1024)S(1)} %fusion.46), kind=kOutput, calls=%fused_computation.44 | convolution fusion | flops 2149580800 | bytes 4198400 | tf_op jit(solution)/shard_map/dot_general | solution.py:35
  104.8 23.1 %mixer_forward.1 = (f32[1024,4224]{1,0:T(8,128)}, bf16[1024,1024]{1,0:T(8,128)(2,1)}, bf16[1024,128]{1,0:T(8,128)(2,1)}) custom-call(s32[7]{0:T(128)} %stack.31.info_ref, bf16[1024,1024]{1,0:T(8,128)(2,1)} %fusion.25.x_ref, bf16[1024,128]{1,0:T(8,128)(2,1)} %compare_convert_fusion.1.mask_ref, f32[1,1024]{1,0:T(1,128)} %bitcast.87, ...), custom_call_target="tpu_custom_call" | custom-call | flops 8858370048 | bytes 25952256 | tf_op jit(solution)/shard_map/mixer_forward/pallas_call | solution.py:1057
  127.9 20.6 %collective-permute-done.25.rest_18_ = bf16[144,4096]{1,0:T(8,128)(2,1)} collective-permute-done((bf16[144,4096]{1,0:T(8,128)(2,1)S(1)}, bf16[144,4096]{1,0:T(8,128)(2,1)}, u32[]{:S(2)}, u32[]{:S(2)}) %collective-permute-start.25) | collective-permute-done | bytes 1179680 | tf_op jit(solution)/shard_map/ppermute | solution.py:1159
  149.6 10.3 %collective-permute-done.21.rest_7_ = bf16[272,1024]{1,0:T(8,128)(2,1)} collective-permute-done((bf16[272,1024]{1,0:T(8,128)(2,1)S(1)}, bf16[272,1024]{1,0:T(8,128)(2,1)}, u32[]{:S(2)}, u32[]{:S(2)}) %collective-permute-start.21) | collective-permute-done | bytes 557088 | tf_op jit(solution)/shard_map/ppermute | solution.py:1159
  162.0 15.1 %attend_forward.1 = (bf16[1024,512]{1,0:T(8,128)(2,1)S(1)}, f32[8,8,128]{2,1,0:T(8,128)S(1)}, bf16[1024,512]{1,0:T(8,128)(2,1)S(1)}, bf16[1024,256]{1,0:T(8,128)(2,1)S(1)}) custom-call(s32[8]{0:T(128)S(1)} %get-tuple-element.199.first_ref, f32[1024,4224]{1,0:T(8,128)} %get-tuple-element.156.query_ref.kv_ref.united_ref.above_ref, ...), custom_call_target="tpu_custom_call" | custom-call | flops 15000000512 | bytes 6000000 | tf_op jit(solution)/shard_map/attend_forward/pallas_call | solution.py:645
  177.1 22.0 %mamba_forward.1 = (bf16[1024,2048]{1,0:T(8,128)(2,1)S(1)}, f32[1024,1536]{1,0:T(8,128)}, f32[8,128,1536]{2,1,0:T(8,128)}) custom-call(s32[8]{0:T(128)S(1)} %compare_convert_fusion.2.restart_ref, f32[1024,4224]{1,0:T(8,128)} %get-tuple-element.156.query_ref.kv_ref.united_ref.above_ref, bf16[1024,512]{1,0:T(8,128)(2,1)S(1)} %get-tuple-element.159.attended_ref, ...), custom_call_target="tpu_custom_call" | custom-call | flops 20000000000 | bytes 50000000 | tf_op jit(solution)/shard_map/mamba_forward/pallas_call | solution.py:395
  199.1 2.0 copy-done.3
  202.7 5.3 %fusion.26.grad_ref = bf16[1024,1024]{1,0:T(8,128)(2,1)} fusion(bf16[1024,1024]{1,0:T(8,128)(2,1)} %bitcast.25, s32[1024]{0:T(1024)S(1)} %fusion.46), kind=kOutput, calls=%fused_computation.45 | convolution fusion | flops 2149580800 | bytes 4198400 | tf_op jit(solution)/shard_map/dot_general | solution.py:35
  208.0 84.2 %block.1 = (bf16[1024,1024]{1,0:T(8,128)(2,1)}, f32[1024,1536]{1,0:T(8,128)}, bf16[1024,512]{1,0:T(8,128)(2,1)}, f32[1024,1024]{1,0:T(8,128)}, bf16[2,128,5632]{2,1,0:T(8,128)(2,1)}) custom-call(s32[7]{0:T(128)} %stack.31.info_ref, bf16[1024,2048]{1,0:T(8,128)(2,1)} %copy-done.3, bf16[1024,1024]{1,0:T(8,128)(2,1)} %fusion.25.x_ref, ...), custom_call_target="tpu_custom_call" | custom-call | flops 42949672960 | bytes 29360128 | tf_op jit(solution)/shard_map/block/pallas_call | solution.py:1057
  292.3 2.7 dynamic-slice_bitcast_fusion.1
  295.1 3.8 fusion.27
  298.9 5.0 all-to-all-start.2
  305.1 15.3 %attend_backward.1 = (bf16[1024,512]{1,0:T(8,128)(2,1)S(1)}, bf16[1024,256]{1,0:T(8,128)(2,1)S(1)}) custom-call(s32[8]{0:T(128)S(1)} %get-tuple-element.199.first_ref, bf16[1024,512]{1,0:T(8,128)(2,1)S(1)} %get-tuple-element.174.turned_ref, bf16[1024,256]{1,0:T(8,128)(2,1)S(1)} %get-tuple-element.175.kv_low_ref, bf16[1024,512]{1,0:T(8,128)(2,1)S(1)} %copy-done.4, ...), custom_call_target="tpu_custom_call" | custom-call | flops 15000000512 | bytes 6000000 | tf_op jit(solution)/shard_map/attend_backward/pallas_call | solution.py:682
  320.5 1.7 convert_add_fusion.3
  322.3 2.2 collective-permute-start.32
  324.5 48.8 %mamba_backward.1.grad_ref = bf16[1024,4224]{1,0:T(8,128)(2,1)} custom-call(s32[8]{0:T(128)S(1)} %compare_convert_fusion.2.restart_ref, f32[1024,4224]{1,0:T(8,128)} %get-tuple-element.156.query_ref.kv_ref.united_ref.above_ref, f32[1024,4224]{1,0:T(8,128)} %get-tuple-element.156.query_ref.kv_ref.united_ref.above_ref, ...), custom_call_target="tpu_custom_call" | custom-call | flops 44999999488 | bytes 60000000 | tf_op jit(solution)/shard_map/mamba_backward/pallas_call | solution.py:432
  373.5 1.5 collective-permute-start.33
  375.0 23.9 %mixer_backward.1 = (bf16[1024,1024]{1,0:T(8,128)(2,1)}, bf16[2,128,2688]{2,1,0:T(8,128)(2,1)S(1)}) custom-call(s32[7]{0:T(128)} %stack.31.info_ref, bf16[1024,4224]{1,0:T(8,128)(2,1)} %mamba_backward.1.grad_ref, bf16[1024,1024]{1,0:T(8,128)(2,1)} %get-tuple-element.185.hidden_ref, bf16[1024,1024]{1,0:T(8,128)(2,1)} %fusion.25.x_ref, ...), custom_call_target="tpu_custom_call" | custom-call | flops 8858370048 | bytes 17039360 | tf_op jit(solution)/shard_map/mixer_backward/pallas_call | solution.py:1057
  400.3 5.4 %fusion.28 = bf16[1024,1024]{1,0:T(8,128)(2,1)} fusion(bf16[1024,1024]{1,0:T(8,128)(2,1)} %get-tuple-element.193, s32[1024]{0:T(1024)S(1)} %fusion.46), kind=kOutput, calls=%fused_computation.47 | convolution fusion | flops 2149580800 | bytes 4198400 | tf_op jit(solution)/shard_map/dot_general | solution.py:1359
  405.7 4.0 all-to-all-start.3
  411.2 93.6 %while.13 = (s32[]{:T(128)}, bf16[64,16640]{1,0:T(8,128)(2,1)}, s32[]{:T(128)}, bf16[2,128,2688]{2,1,0:T(8,128)(2,1)S(1)}, f32[32,5632]{1,0:T(8,128)S(1)}, /*ind...) while((s32[]{:T(128)}, bf16[64,16640]{1,0:T(8,128)(2,1)}, ...), condition=%wide.region_4.5_spmd, body=%wide.region_3.4_spmd.sunk | while | flops 20651132 | bytes 45135732 | solution.py:1398
  411.7 1.9 collective-permute-done
  415.6 1.9 collective-permute-start.1
  417.5 18.8 %collective-permute-done.1 = bf16[64,2688]{1,0:T(8,128)(2,1)} collective-permute-done((bf16[64,2688]{1,0:T(8,128)(2,1)}, bf16[64,2688]{1,0:T(8,128)(2,1)}, u32[]{:S(2)}, u32[]{:S(2)}) %collective-permute-start.1) | collective-permute-done | bytes 344096 | tf_op jit(solution)/shard_map/while/body/ppermute | solution.py:1159
  437.4 3.4 collective-permute-start.2
  440.8 5.4 %collective-permute-done.2 = bf16[32,2688]{1,0:T(8,128)(2,1)S(1)} collective-permute-done((bf16[32,2688]{1,0:T(8,128)(2,1)S(1)}, bf16[32,2688]{1,0:T(8,128)(2,1)S(1)}, u32[]{:S(2)}, u32[]{:S(2)}) %collective-permute-start.2) | collective-permute-done | bytes 172064 | tf_op jit(solution)/shard_map/while/body/ppermute | solution.py:1163
  447.2 12.6 %collective-permute-done.3 = bf16[16,8320]{1,0:T(8,128)(2,1)S(1)} collective-permute-done((bf16[16,8320]{1,0:T(8,128)(2,1)S(1)}, bf16[16,8320]{1,0:T(8,128)(2,1)S(1)}, u32[]{:S(2)}, u32[]{:S(2)}) %collective-permute-start.3) | collective-permute-done | bytes 266272 | tf_op jit(solution)/shard_map/while/body/ppermute | solution.py:1163
  460.7 7.7 %collective-permute-done.4 = bf16[8,8320]{1,0:T(8,128)(2,1)S(1)} collective-permute-done((bf16[8,8320]{1,0:T(8,128)(2,1)S(1)}, bf16[8,8320]{1,0:T(8,128)(2,1)S(1)}, u32[]{:S(2)}, u32[]{:S(2)}) %collective-permute-start.4) | collective-permute-done | bytes 133152 | tf_op jit(solution)/shard_map/while/body/ppermute | solution.py:1163
  468.5 8.0 %collective-permute-done.5 = bf16[8,8320]{1,0:T(8,128)(2,1)S(1)} collective-permute-done((bf16[8,8320]{1,0:T(8,128)(2,1)S(1)}, bf16[8,8320]{1,0:T(8,128)(2,1)S(1)}, u32[]{:S(2)}, u32[]{:S(2)}) %collective-permute-start.5) | collective-permute-done | bytes 133152 | tf_op jit(solution)/shard_map/while/body/ppermute | solution.py:1163
  476.6 8.3 %collective-permute-done.6 = bf16[16,8320]{1,0:T(8,128)(2,1)S(1)} collective-permute-done((bf16[16,8320]{1,0:T(8,128)(2,1)S(1)}, bf16[16,8320]{1,0:T(8,128)(2,1)S(1)}, u32[]{:S(2)}, u32[]{:S(2)}) %collective-permute-start.6) | collective-permute-done | bytes 266272 | tf_op jit(solution)/shard_map/while/body/ppermute | solution.py:1163
  485.7 12.5 %collective-permute-done.7 = bf16[32,8320]{1,0:T(8,128)(2,1)S(1)} collective-permute-done((bf16[32,8320]{1,0:T(8,128)(2,1)S(1)}, bf16[32,8320]{1,0:T(8,128)(2,1)S(1)}, u32[]{:S(2)}, u32[]{:S(2)}) %collective-permute-start.7) | collective-permute-done | bytes 532512 | tf_op jit(solution)/shard_map/while/body/ppermute | solution.py:1163
  498.5 2.8 collective-permute-done.8
  501.3 3.5 maximum_select_fusion.11
  504.8 2.6 reshape.270
  514.2 5.4 %fusion.24 = bf16[1024,1024]{1,0:T(8,128)(2,1)} fusion(bf16[1024,1024]{1,0:T(8,128)(2,1)} %bitcast.30, s32[1024]{0:T(1024)S(1)} %copy-done.20), kind=kOutput, calls=%fused_computation.43 | convolution fusion | flops 2149580800 | bytes 4198400 | tf_op jit(solution)/shard_map/dot_general | solution.py:1365
  519.6 6.1 %fusion.11 = f32[4,256,1024]{2,1,0:T(8,128)} fusion(bf16[1024,1024,1]{1,0,2:T(8,128)(2,1)} %bitcast.34, s32[4,256]{1,0:T(4,128)S(1)} %copy-done.21, s32[1024]{0:T(1024)S(1)} %copy-done.20), kind=kOutput, calls=%fused_computation.29 | convolution fusion | flops 2148532224 | bytes 6299648 | tf_op jit(solution)/shard_map/dot_general | solution.py:1365
  (186 shorter events, 42.8 us)
Async XLA Ops:
  3.0 55.2 %collective-permute-start.9 = (bf16[2048,128]{1,0:T(8,128)(2,1)}, bf16[2048,128]{1,0:T(8,128)(2,1)}, u32[]{:S(2)}, u32[]{:S(2)}) collective-permute-start(bf16[2048,128]{1,0:T(8,128)(2,1)} %slice.53), channel_id=1, source_target_pairs={{0,1},{1,0},{2,3},{3,2},{4,5},{5,4},{6,7},{7,6},{8,9},{9,8},{10,11... | collective-permute-start | bytes 1572872 | tf_op jit(solution)/shard_map/ppermute | solution.py:1159
  6.8 52.2 %collective-permute-start.17 = (bf16[2080,128]{1,0:T(8,128)(2,1)}, bf16[2080,128]{1,0:T(8,128)(2,1)}, u32[]{:S(2)}, u32[]{:S(2)}) collective-permute-start(bf16[2080,128]{1,0:T(8,128)(2,1)} %pad_slice_fusion), channel_id=1, source_target_pairs={{0,1},{1,0},{2,3},{3,2},{4,5},{5,4},{6,7},{7,6},{8,9},{9,8},{10,11... | collective-permute-start | bytes 1597448 | tf_op jit(solution)/shard_map/ppermute | solution.py:1159
  7.0 22.0 %copy-start.19 = (s32[1024]{0:T(1024)}, s32[1024]{0:T(1024)S(1)}, u32[]{:S(2)}) copy-start(s32[1024]{0:T(1024)S(1)} %fusion.41) | copy-start | bytes 12292
  10.7 80.3 %all-to-all-start = ((bf16[32,32,1024]{2,1,0:T(8,128)(2,1)}), bf16[32,32,1024]{2,1,0:T(8,128)(2,1)}, u32[]{:S(2)}, u32[]{:S(2)}) async-start(bf16[32,32,1024]{2,1,0:T(8,128)(2,1)} %bitcast.79), calls=%async_computation | async-start | bytes 4194304 | tf_op jit(solution)/shard_map/all_to_all | solution.py:1237
  17.5 39.4 %collective-permute-start.10 = (bf16[16,10368]{1,0:T(8,128)(2,1)S(1)}, bf16[16,10368]{1,0:T(8,128)(2,1)S(1)}, u32[]{:S(2)}, u32[]{:S(2)}) collective-permute-start(bf16[16,10368]{1,0:T(8,128)(2,1)S(1)} %constant_dynamic-slice_fusion), channel_id=1, source_target_pairs={{0,1},{1,0},{2,3},{3,2},{4,5},{5,4},{6,7},{7,6},{8,9},{9,8},{10,11... | collective-permute-start | bytes 995336 | tf_op jit(solution)/shard_map/ppermute | solution.py:1159
  33.1 57.2 %copy-start.25 = (f32[24]{0:T(128)S(1)}, f32[24]{0:T(128)}, u32[]{:S(2)}) copy-start(f32[24]{0:T(128)} %param.39) | copy-start | bytes 292
  33.1 57.2 %copy-start.26 = (f32[24]{0:T(128)S(1)}, f32[24]{0:T(128)}, u32[]{:S(2)}) copy-start(f32[24]{0:T(128)} %param.38) | copy-start | bytes 292
  33.1 57.2 %copy-start.18 = (f32[1792]{0:T(1024)S(1)}, f32[1792]{0:T(1024)}, u32[]{:S(2)}) copy-start(f32[1792]{0:T(1024)} %param.37) | copy-start | bytes 21508
  33.1 57.2 %copy-start.24 = (f32[24]{0:T(128)S(1)}, f32[24]{0:T(128)}, u32[]{:S(2)}) copy-start(f32[24]{0:T(128)} %param.40) | copy-start | bytes 292
  33.1 57.4 %copy-start.17 = (f32[1536]{0:T(1024)S(1)}, f32[1536]{0:T(1024)}, u32[]{:S(2)}) copy-start(f32[1536]{0:T(1024)} %param.41) | copy-start | bytes 18436
  57.0 34.1 %copy-start.28 = (bf16[16,10368]{1,0:T(8,128)(2,1)}, bf16[16,10368]{1,0:T(8,128)(2,1)S(1)}, u32[]{:S(2)}) copy-start(bf16[16,10368]{1,0:T(8,128)(2,1)S(1)} %collective-permute-done.10.rest_1_.rest_12_.rest_23_) | copy-start | bytes 995332
  57.0 12.2 %collective-permute-start.11 = (bf16[16,10368]{1,0:T(8,128)(2,1)S(1)}, bf16[16,10368]{1,0:T(8,128)(2,1)}, u32[]{:S(2)}, u32[]{:S(2)}) collective-permute-start(bf16[16,10368]{1,0:T(8,128)(2,1)S(1)} %collective-permute-done.10.rest_1_.rest_12_.rest_23_), channel_id=1, source_target_pairs={{0,4},{2,6},{4,0},{6,2},{8,12},{10,14},{12,8},{14,10},{16,20},{18,... | collective-permute-start | bytes 995336 | tf_op jit(solution)/shard_map/ppermute | solution.py:1163
  58.2 22.3 %collective-permute-start.14 = (bf16[2048,128]{1,0:T(8,128)(2,1)}, bf16[2048,128]{1,0:T(8,128)(2,1)}, u32[]{:S(2)}, u32[]{:S(2)}) collective-permute-start(bf16[2048,128]{1,0:T(8,128)(2,1)} %collective-permute-done.9.rest_7_), channel_id=1, source_target_pairs={{0,4},{2,6},{4,0},{6,2},{8,12},{10,14},{12,8},{14,10},{16,20},{18,... | collective-permute-start | bytes 1572872 | tf_op jit(solution)/shard_map/ppermute | solution.py:1163
  59.0 31.3 %collective-permute-start.18 = (bf16[2080,128]{1,0:T(8,128)(2,1)}, bf16[2080,128]{1,0:T(8,128)(2,1)}, u32[]{:S(2)}, u32[]{:S(2)}) collective-permute-start(bf16[2080,128]{1,0:T(8,128)(2,1)} %collective-permute-done.17.rest_11_), channel_id=1, source_target_pairs={{0,4},{2,6},{4,0},{6,2},{8,12},{10,14},{12,8},{14,10},{16,20},{18,... | collective-permute-start | bytes 1597448 | tf_op jit(solution)/shard_map/ppermute | solution.py:1163
  60.4 9.3 %collective-permute-start.12 = (bf16[16,10368]{1,0:T(8,128)(2,1)S(1)}, bf16[16,10368]{1,0:T(8,128)(2,1)S(1)}, u32[]{:S(2)}, u32[]{:S(2)}) collective-permute-start(bf16[16,10368]{1,0:T(8,128)(2,1)S(1)} %collective-permute-done.10.rest_1_.rest_12_.rest_23_), channel_id=1, source_target_pairs={{0,2},{2,0},{4,6},{6,4},{8,10},{10,8},{12,14},{14,12},{16,18},{18,... | collective-permute-start | bytes 995336 | tf_op jit(solution)/shard_map/ppermute | solution.py:1163
  69.2 28.2 %collective-permute-start.13 = (bf16[16,10368]{1,0:T(8,128)(2,1)}, bf16[16,10368]{1,0:T(8,128)(2,1)}, u32[]{:S(2)}, u32[]{:S(2)}) collective-permute-start(bf16[16,10368]{1,0:T(8,128)(2,1)} %collective-permute-done.11.rest_2_.rest_13_.rest_24_), channel_id=1, source_target_pairs={{0,2},{2,0},{4,6},{6,4},{8,10},{10,8},{12,14},{14,12},{16,18},{18,... | collective-permute-start | bytes 995336 | tf_op jit(solution)/shard_map/ppermute | solution.py:1163
  69.2 35.4 %collective-permute-start.15 = (bf16[2048,128]{1,0:T(8,128)(2,1)}, bf16[2048,128]{1,0:T(8,128)(2,1)}, u32[]{:S(2)}, u32[]{:S(2)}) collective-permute-start(bf16[2048,128]{1,0:T(8,128)(2,1)} %collective-permute-done.9.rest_7_), channel_id=1, source_target_pairs={{0,2},{2,0},{4,6},{6,4},{8,10},{10,8},{12,14},{14,12},{16,18},{18,... | collective-permute-start | bytes 1572872 | tf_op jit(solution)/shard_map/ppermute | solution.py:1163
  69.7 20.5 %copy-start.29 = (bf16[16,10368]{1,0:T(8,128)(2,1)}, bf16[16,10368]{1,0:T(8,128)(2,1)S(1)}, u32[]{:S(2)}) copy-start(bf16[16,10368]{1,0:T(8,128)(2,1)S(1)} %collective-permute-done.12.rest_3_.rest_14_.rest_25_) | copy-start | bytes 995332
  69.7 35.1 %collective-permute-start.19 = (bf16[2080,128]{1,0:T(8,128)(2,1)}, bf16[2080,128]{1,0:T(8,128)(2,1)}, u32[]{:S(2)}, u32[]{:S(2)}) collective-permute-start(bf16[2080,128]{1,0:T(8,128)(2,1)} %collective-permute-done.17.rest_11_), channel_id=1, source_target_pairs={{0,2},{2,0},{4,6},{6,4},{8,10},{10,8},{12,14},{14,12},{16,18},{18,... | collective-permute-start | bytes 1597448 | tf_op jit(solution)/shard_map/ppermute | solution.py:1163
  80.4 24.4 %collective-permute-start.16 = (bf16[2048,128]{1,0:T(8,128)(2,1)}, bf16[2048,128]{1,0:T(8,128)(2,1)}, u32[]{:S(2)}, u32[]{:S(2)}) collective-permute-start(bf16[2048,128]{1,0:T(8,128)(2,1)} %collective-permute-done.14.rest_8_), channel_id=1, source_target_pairs={{0,2},{2,0},{4,6},{6,4},{8,10},{10,8},{12,14},{14,12},{16,18},{18,... | collective-permute-start | bytes 1572872 | tf_op jit(solution)/shard_map/ppermute | solution.py:1163
  90.3 14.5 %collective-permute-start.20 = (bf16[2080,128]{1,0:T(8,128)(2,1)}, bf16[2080,128]{1,0:T(8,128)(2,1)}, u32[]{:S(2)}, u32[]{:S(2)}) collective-permute-start(bf16[2080,128]{1,0:T(8,128)(2,1)} %collective-permute-done.18.rest_12_), channel_id=1, source_target_pairs={{0,2},{2,0},{4,6},{6,4},{8,10},{10,8},{12,14},{14,12},{16,18},{18,... | collective-permute-start | bytes 1597448 | tf_op jit(solution)/shard_map/ppermute | solution.py:1163
  91.1 111.6 %all-to-all-start.1 = ((bf16[32,32,1024]{2,1,0:T(8,128)(2,1)}), bf16[32,32,1024]{2,1,0:T(8,128)(2,1)}, u32[]{:S(2)}, u32[]{:S(2)}) async-start(bf16[32,32,1024]{2,1,0:T(8,128)(2,1)} %bitcast.78), calls=%async_computation.1 | async-start | bytes 4194304 | tf_op jit(solution)/shard_map/all_to_all | solution.py:1237
  97.4 51.1 %collective-permute-start.25 = (bf16[144,4096]{1,0:T(8,128)(2,1)S(1)}, bf16[144,4096]{1,0:T(8,128)(2,1)}, u32[]{:S(2)}, u32[]{:S(2)}) collective-permute-start(bf16[144,4096]{1,0:T(8,128)(2,1)S(1)} %pad_maximum_fusion), channel_id=1, source_target_pairs={{0,1},{1,0},{2,3},{3,2},{4,5},{5,4},{6,7},{7,6},{8,9},{9,8},{10,11... | collective-permute-start | bytes 3538952 | tf_op jit(solution)/shard_map/ppermute | solution.py:1159
  104.6 55.2 %collective-permute-start.21 = (bf16[272,1024]{1,0:T(8,128)(2,1)S(1)}, bf16[272,1024]{1,0:T(8,128)(2,1)}, u32[]{:S(2)}, u32[]{:S(2)}) collective-permute-start(bf16[272,1024]{1,0:T(8,128)(2,1)S(1)} %copy-done.9), channel_id=1, source_target_pairs={{0,1},{1,0},{2,3},{3,2},{4,5},{5,4},{6,7},{7,6},{8,9},{9,8},{10,11... | collective-permute-start | bytes 1671176 | tf_op jit(solution)/shard_map/ppermute | solution.py:1159
  148.5 28.6 %copy-start.2 = (f32[4,1792]{1,0:T(4,128)S(1)}, f32[4,1792]{1,0:T(4,128)}, u32[]{:S(2)}) copy-start(f32[4,1792]{1,0:T(4,128)} %taps_ref.3) | copy-start | bytes 86020
  148.5 52.6 %collective-permute-start.26 = (bf16[144,4096]{1,0:T(8,128)(2,1)}, bf16[144,4096]{1,0:T(8,128)(2,1)}, u32[]{:S(2)}, u32[]{:S(2)}) collective-permute-start(bf16[144,4096]{1,0:T(8,128)(2,1)} %collective-permute-done.25.rest_18_), channel_id=1, source_target_pairs={{0,4},{2,6},{4,0},{6,2},{8,12},{10,14},{12,8},{14,10},{16,20},{18,... | collective-permute-start | bytes 3538952 | tf_op jit(solution)/shard_map/ppermute | solution.py:1163
  149.6 58.5 %collective-permute-start.27 = (bf16[144,4096]{1,0:T(8,128)(2,1)}, bf16[144,4096]{1,0:T(8,128)(2,1)}, u32[]{:S(2)}, u32[]{:S(2)}) collective-permute-start(bf16[144,4096]{1,0:T(8,128)(2,1)} %collective-permute-done.25.rest_18_), channel_id=1, source_target_pairs={{0,2},{2,0},{4,6},{6,4},{8,10},{10,8},{12,14},{14,12},{16,18},{18,... | collective-permute-start | bytes 3538952 | tf_op jit(solution)/shard_map/ppermute | solution.py:1163
  159.9 41.8 %collective-permute-start.22 = (bf16[272,1024]{1,0:T(8,128)(2,1)}, bf16[272,1024]{1,0:T(8,128)(2,1)}, u32[]{:S(2)}, u32[]{:S(2)}) collective-permute-start(bf16[272,1024]{1,0:T(8,128)(2,1)} %collective-permute-done.21.rest_7_), channel_id=1, source_target_pairs={{0,4},{2,6},{4,0},{6,2},{8,12},{10,14},{12,8},{14,10},{16,20},{18,... | collective-permute-start | bytes 1671176 | tf_op jit(solution)/shard_map/ppermute | solution.py:1163
  161.3 39.7 %collective-permute-start.29 = (bf16[544,1024]{1,0:T(8,128)(2,1)}, bf16[544,1024]{1,0:T(8,128)(2,1)}, u32[]{:S(2)}, u32[]{:S(2)}) collective-permute-start(bf16[544,1024]{1,0:T(8,128)(2,1)} %pad_maximum_fusion.1), channel_id=1, source_target_pairs={{0,1},{1,0},{2,3},{3,2},{4,5},{5,4},{6,7},{7,6},{8,9},{9,8},{10,11... | collective-permute-start | bytes 3342344 | tf_op jit(solution)/shard_map/ppermute | solution.py:1159
  201.1 6.9 %collective-permute-start.28 = (bf16[144,4096]{1,0:T(8,128)(2,1)}, bf16[144,4096]{1,0:T(8,128)(2,1)}, u32[]{:S(2)}, u32[]{:S(2)}) collective-permute-start(bf16[144,4096]{1,0:T(8,128)(2,1)} %collective-permute-done.26.rest_19_), channel_id=1, source_target_pairs={{0,2},{2,0},{4,6},{6,4},{8,10},{10,8},{12,14},{14,12},{16,18},{18,... | collective-permute-start | bytes 3538952 | tf_op jit(solution)/shard_map/ppermute | solution.py:1163
  201.1 6.9 %collective-permute-start.30 = (bf16[544,1024]{1,0:T(8,128)(2,1)}, bf16[544,1024]{1,0:T(8,128)(2,1)}, u32[]{:S(2)}, u32[]{:S(2)}) collective-permute-start(bf16[544,1024]{1,0:T(8,128)(2,1)} %collective-permute-done.29.rest_29_), channel_id=1, source_target_pairs={{0,2},{2,0},{4,6},{6,4},{8,10},{10,8},{12,14},{14,12},{16,18},{18,... | collective-permute-start | bytes 3342344 | tf_op jit(solution)/shard_map/ppermute | solution.py:1163
  201.6 6.4 %collective-permute-start.23 = (bf16[272,1024]{1,0:T(8,128)(2,1)}, bf16[272,1024]{1,0:T(8,128)(2,1)}, u32[]{:S(2)}, u32[]{:S(2)}) collective-permute-start(bf16[272,1024]{1,0:T(8,128)(2,1)} %collective-permute-done.21.rest_7_), channel_id=1, source_target_pairs={{0,2},{2,0},{4,6},{6,4},{8,10},{10,8},{12,14},{14,12},{16,18},{18,... | collective-permute-start | bytes 1671176 | tf_op jit(solution)/shard_map/ppermute | solution.py:1163
  201.7 6.3 %collective-permute-start.24 = (bf16[272,1024]{1,0:T(8,128)(2,1)}, bf16[272,1024]{1,0:T(8,128)(2,1)}, u32[]{:S(2)}, u32[]{:S(2)}) collective-permute-start(bf16[272,1024]{1,0:T(8,128)(2,1)} %collective-permute-done.22.rest_8_), channel_id=1, source_target_pairs={{0,2},{2,0},{4,6},{6,4},{8,10},{10,8},{12,14},{14,12},{16,18},{18,... | collective-permute-start | bytes 1671176 | tf_op jit(solution)/shard_map/ppermute | solution.py:1163
  295.0 25.5 %collective-permute-start.31 = (bf16[128,5632]{1,0:T(8,128)(2,1)}, bf16[128,5632]{1,0:T(8,128)(2,1)}, u32[]{:S(2)}, u32[]{:S(2)}) collective-permute-start(bf16[128,5632]{1,0:T(8,128)(2,1)} %dynamic-slice_bitcast_fusion.1), channel_id=1, source_target_pairs={{0,2},{2,0},{4,6},{6,4},{8,10},{10,8},{12,14},{14,12},{16,18},{18,... | collective-permute-start | bytes 4325384 | tf_op jit(solution)/shard_map/ppermute | solution.py:1163
  298.9 74.5 %all-to-all-start.2 = ((bf16[32,32,1024]{2,1,0:T(8,128)(2,1)}), bf16[32,32,1024]{2,1,0:T(8,128)(2,1)}, u32[]{:S(2)}, u32[]{:S(2)}) async-start(bf16[32,32,1024]{2,1,0:T(8,128)(2,1)} %bitcast.80), calls=%async_computation.2 | async-start | bytes 4194304 | tf_op jit(solution)/shard_map/all_to_all | solution.py:1237
  322.3 51.0 %collective-permute-start.32 = (bf16[64,5632]{1,0:T(8,128)(2,1)S(1)}, bf16[64,5632]{1,0:T(8,128)(2,1)S(1)}, u32[]{:S(2)}, u32[]{:S(2)}) collective-permute-start(bf16[64,5632]{1,0:T(8,128)(2,1)S(1)} %dynamic-slice_convert_fusion.3), channel_id=1, source_target_pairs={{0,1},{1,0},{2,3},{3,2},{4,5},{5,4},{6,7},{7,6},{8,9},{9,8},{10,11... | collective-permute-start | bytes 2162696 | tf_op jit(solution)/shard_map/ppermute | solution.py:1159
  373.4 25.6 %copy-start.7 = (f32[64,5632]{1,0:T(8,128)}, f32[64,5632]{1,0:T(8,128)S(1)}, u32[]{:S(2)}) copy-start(f32[64,5632]{1,0:T(8,128)S(1)} %convert_add_fusion.4) | copy-start | bytes 4325380
  373.5 25.5 %collective-permute-start.33 = (bf16[32,5632]{1,0:T(8,128)(2,1)S(1)}, bf16[32,5632]{1,0:T(8,128)(2,1)}, u32[]{:S(2)}, u32[]{:S(2)}) collective-permute-start(bf16[32,5632]{1,0:T(8,128)(2,1)S(1)} %dynamic-slice_convert_fusion.4), channel_id=1, source_target_pairs={{0,4},{2,6},{4,0},{6,2},{8,12},{10,14},{12,8},{14,10},{16,20},{18,... | collective-permute-start | bytes 1081352 | tf_op jit(solution)/shard_map/ppermute | solution.py:1163
  405.7 113.9 %all-to-all-start.3 = ((bf16[32,32,1024]{2,1,0:T(8,128)(2,1)}), bf16[32,32,1024]{2,1,0:T(8,128)(2,1)}, u32[]{:S(2)}, u32[]{:S(2)}) async-start(bf16[32,32,1024]{2,1,0:T(8,128)(2,1)} %bitcast.77), calls=%async_computation.3 | async-start | bytes 4194304 | tf_op jit(solution)/shard_map/all_to_all | solution.py:1237
  411.2 2.3 collective-permute-start
  415.6 20.7 %collective-permute-start.1 = (bf16[64,2688]{1,0:T(8,128)(2,1)}, bf16[64,2688]{1,0:T(8,128)(2,1)}, u32[]{:S(2)}, u32[]{:S(2)}) collective-permute-start(bf16[64,2688]{1,0:T(8,128)(2,1)} %dynamic-slice_convert_fusion.8), channel_id=1, source_target_pairs={{0,1},{1,0},{2,3},{3,2},{4,5},{5,4},{6,7},{7,6},{8,9},{9,8},{10,11... | collective-permute-start | bytes 1032200 | tf_op jit(solution)/shard_map/while/body/ppermute | solution.py:1159
  437.4 8.8 %collective-permute-start.2 = (bf16[32,2688]{1,0:T(8,128)(2,1)S(1)}, bf16[32,2688]{1,0:T(8,128)(2,1)S(1)}, u32[]{:S(2)}, u32[]{:S(2)}) collective-permute-start(bf16[32,2688]{1,0:T(8,128)(2,1)S(1)} %dynamic-slice_convert_fusion.9), channel_id=1, source_target_pairs={{0,4},{2,6},{4,0},{6,2},{8,12},{10,14},{12,8},{14,10},{16,20},{18,... | collective-permute-start | bytes 516104 | tf_op jit(solution)/shard_map/while/body/ppermute | solution.py:1163
  446.3 13.5 %collective-permute-start.3 = (bf16[16,8320]{1,0:T(8,128)(2,1)S(1)}, bf16[16,8320]{1,0:T(8,128)(2,1)S(1)}, u32[]{:S(2)}, u32[]{:S(2)}) collective-permute-start(bf16[16,8320]{1,0:T(8,128)(2,1)S(1)} %fusion.67), channel_id=1, source_target_pairs={{0,8},{2,10},{4,12},{6,14},{8,0},{10,2},{12,4},{14,6},{16,24},{18,... | collective-permute-start | bytes 798728 | tf_op jit(solution)/shard_map/while/body/ppermute | solution.py:1163
  459.9 8.5 %collective-permute-start.4 = (bf16[8,8320]{1,0:T(8,128)(2,1)S(1)}, bf16[8,8320]{1,0:T(8,128)(2,1)S(1)}, u32[]{:S(2)}, u32[]{:S(2)}) collective-permute-start(bf16[8,8320]{1,0:T(8,128)(2,1)S(1)} %dynamic-slice_convert_fusion.10), channel_id=1, source_target_pairs={{0,16},{2,18},{4,20},{6,22},{8,24},{10,26},{12,28},{14,30},{16,0},... | collective-permute-start | bytes 399368 | tf_op jit(solution)/shard_map/while/body/ppermute | solution.py:1163
  468.4 8.0 %collective-permute-start.5 = (bf16[8,8320]{1,0:T(8,128)(2,1)S(1)}, bf16[8,8320]{1,0:T(8,128)(2,1)S(1)}, u32[]{:S(2)}, u32[]{:S(2)}) collective-permute-start(bf16[8,8320]{1,0:T(8,128)(2,1)S(1)} %add_convert_fusion.2), channel_id=1, source_target_pairs={{0,16},{2,18},{4,20},{6,22},{8,24},{10,26},{12,28},{14,30},{16,0},... | collective-permute-start | bytes 399368 | tf_op jit(solution)/shard_map/while/body/ppermute | solution.py:1163
  476.5 8.4 %collective-permute-start.6 = (bf16[16,8320]{1,0:T(8,128)(2,1)S(1)}, bf16[16,8320]{1,0:T(8,128)(2,1)S(1)}, u32[]{:S(2)}, u32[]{:S(2)}) collective-permute-start(bf16[16,8320]{1,0:T(8,128)(2,1)S(1)} %maximum_select_fusion.8), channel_id=1, source_target_pairs={{0,8},{2,10},{4,12},{6,14},{8,0},{10,2},{12,4},{14,6},{16,24},{18,... | collective-permute-start | bytes 798728 | tf_op jit(solution)/shard_map/while/body/ppermute | solution.py:1163
  485.0 13.2 %collective-permute-start.7 = (bf16[32,8320]{1,0:T(8,128)(2,1)S(1)}, bf16[32,8320]{1,0:T(8,128)(2,1)S(1)}, u32[]{:S(2)}, u32[]{:S(2)}) collective-permute-start(bf16[32,8320]{1,0:T(8,128)(2,1)S(1)} %maximum_select_fusion.9), channel_id=1, source_target_pairs={{0,4},{2,6},{4,0},{6,2},{8,12},{10,14},{12,8},{14,10},{16,20},{18,... | collective-permute-start | bytes 1597448 | tf_op jit(solution)/shard_map/while/body/ppermute | solution.py:1163
  498.4 2.9 collective-permute-start.8
  (22 other events, 111.5 us)

commit v3 on v2

--- a/solution.py
+++ b/solution.py
@@ -29,6 +29,11 @@
 GIVEN = 4120
 TAIL_AT = DSSM + XBC
 STEP_W = 24
+D = 1024
+RANKS = 128
+QUARTERS = 4
+ADAPT_SCALE = 0.5
+MIXER_GRADS_W = D + UNITED + 128
 
 
 def dot_nn(a, b):
@@ -173,6 +178,85 @@
 
 
 def mamba_backward_kernel(
+    restart_ref,
+    info_ref,
+    united_ref,
+    above_ref,
+    scan_ref,
+    start_ref,
+    grad_ref,
+    dquery_ref,
+    dkv_ref,
+    hidden_ref,
+    mid_ref,
+    mask_ref,
+    taps_ref,
+    bias_ref,
+    step_bias_ref,
+    decay_ref,
+    skip_ref,
+    gain_ref,
+    wide_ref,
+    *rest,
+):
+    *pieces, dunited_ref, grad_mid_ref, grads_ref = rest[: QUARTERS + 4]
+    scratch = rest[QUARTERS + 4 :]
+    upper, sems, total, both = scratch[-4:]
+    copies = with_sems(
+        factor_jobs(info_ref, pieces[0], pieces[1:], pl.ds(D, UNITED), upper), sems
+    )
+
+    def begin():
+        start_all(copies)
+        total[...] = jnp.zeros_like(total)
+
+    at_first(begin)
+    mamba_backward_chunk(
+        restart_ref,
+        united_ref,
+        above_ref,
+        scan_ref,
+        start_ref,
+        grad_ref,
+        dquery_ref,
+        dkv_ref,
+        taps_ref,
+        bias_ref,
+        step_bias_ref,
+        decay_ref,
+        skip_ref,
+        gain_ref,
+        wide_ref,
+        dunited_ref,
+        *scratch[:-4],
+    )
+    at_first(lambda: wait_all(copies))
+    late = pl.program_id(0) % 2 == 0
+
+    @pl.when(late)
+    def _():
+        both[SPAN:, :] = dunited_ref[...]
+
+    @pl.when(jnp.logical_not(late))
+    def _():
+        both[:SPAN, :] = dunited_ref[...]
+        dunited = both[...]
+        grad_mid = masked(ADAPT_SCALE * dot_nt(dunited, upper[...]), mask_ref[...].astype(F32))
+        grad_mid_ref[...] = grad_mid
+        add_factor_grads(
+            total,
+            slice(0, D),
+            slice(D, D + UNITED),
+            grad_mid,
+            hidden_ref[...],
+            mid_ref[...],
+            dunited,
+        )
+
+    store_grads(total, grads_ref)
+
+
+def mamba_backward_chunk(
     restart_ref,
     united_ref,
     above_ref,
@@ -420,19 +504,24 @@
     )(restart, united, attended, *params)
 
 
-def mamba_backward(united, scan, starts, grad, dquery, dkv, restart, params):
+def mamba_backward(
+    united, scan, starts, grad, dquery, dkv, hidden, mid, mask, restart, info, params, factors
+):
     rows = united.shape[0]
     chunks = rows // SPAN
 
     def at(width):
         return pl.BlockSpec((SPAN, width), lambda i, *_: (chunks - 1 - i, 0))
+
+    def at_two(width):
+        return pl.BlockSpec((2 * SPAN, width), lambda i, *_: ((chunks - 1 - i) // 2, 0))
 
     wide = pltpu.VMEM((SPAN, DSSM), F32)
     tall = pltpu.VMEM((SPAN + HALO, XBC), F32)
     return pl.pallas_call(
         mamba_backward_kernel,
         grid_spec=pltpu.PrefetchScalarGridSpec(
-            num_scalar_prefetch=1,
+            num_scalar_prefetch=2,
             grid=(chunks,),
             in_specs=[
                 at(UNITED),
@@ -445,20 +534,39 @@
                 at(DSSM),
                 at(dquery.shape[1]),
                 at(dkv.shape[1]),
+                at_two(D),
+                at_two(RANKS),
+                at_two(RANKS),
             ]
-            + PARAM_SPECS,
-            out_specs=[at(UNITED)],
-            scratch_shapes=[tall, tall] + [wide] * 8 + [pltpu.VMEM((8, DSSM), F32)],
+            + PARAM_SPECS
+            + [pl.BlockSpec(memory_space=pl.ANY)] * (1 + QUARTERS),
+            out_specs=[at(UNITED), at_two(RANKS), fixed((2, RANKS, MIXER_GRADS_W // 2))],
+            scratch_shapes=[tall, tall]
+            + [wide] * 8
+            + [
+                pltpu.VMEM((8, DSSM), F32),
+                pltpu.VMEM((RANKS, UNITED), BF16),
+                pltpu.SemaphoreType.DMA((1 + QUARTERS,)),
+                pltpu.VMEM((RANKS, MIXER_GRADS_W), F32),
+                pltpu.VMEM((2 * SPAN, UNITED), BF16),
+            ],
         ),
-        out_shape=[jax.ShapeDtypeStruct((rows, UNITED), BF16)],
+        out_shape=[
+            jax.ShapeDtypeStruct((rows, UNITED), BF16),
+            jax.ShapeDtypeStruct((rows, RANKS), BF16),
+            jax.ShapeDtypeStruct((2, RANKS, MIXER_GRADS_W // 2), BF16),
+        ],
         compiler_params=pltpu.CompilerParams(
-            vmem_limit_bytes=48 << 20, dimension_semantics=("arbitrary",)
+            vmem_limit_bytes=56 << 20, dimension_semantics=("arbitrary",)
         ),
         cost_estimate=pl.CostEstimate(
             flops=45 * 10**9, bytes_accessed=60 * 10**6, transcendentals=0
         ),
         name="mamba_backward",
-    )(restart, united, united, scan, starts, grad, dquery, dkv, *params)[0]
+    )(
+        restart, info, united, united, scan, starts, grad, dquery, dkv, hidden, mid, mask,
+        *params, *factors,
+    )
 
 
 ATT_HEADS = 8
@@ -715,29 +823,21 @@
     )(first, turned, kv_low, grad, logs, cosine, sines)
 
 
-RANKS = 128
 ROW_BLOCK = 256
-D = 1024
 FF = 2048
 MIX = 2048
-QUARTERS = 4
-ADAPT_SCALE = 0.5
 COLUMN_STEP = 512
-MERGE = (MIX, D, D, 4)
-EXPAND = (D, 2 * FF, D + MIX, 4)
-REDUCE = (FF, D, 2 * D + MIX, 2)
+MERGE = (MIX, D, 0, 4, (slice(0, D),))
+EXPAND = (D, 2 * FF, MIX, 4, (slice(0, FF), slice(FF, 2 * FF)))
+REDUCE = (FF, D, D + MIX, 2, (slice(0, D),))
 MIXER_CHUNKS = (slice(0, 2048), slice(2048, 4128))
 OWN_ROWS = 4112
-LOWER_W = 2 * D + MIX + FF
-FACTORS_W = LOWER_W + UNITED
-
-
 def piece_count(shape):
-    return 3 + QUARTERS + shape[3]
+    return 3 + QUARTERS + shape[3] * len(shape[4])
 
 
 def copy_count(shape):
-    return 3 + QUARTERS + 2 * shape[3]
+    return 3 + QUARTERS + 2 * shape[3] * len(shape[4])
 
 
 MIXER_PIECES = 3 + QUARTERS + QUARTERS * len(MIXER_CHUNKS)
@@ -788,7 +888,7 @@
 
 
 def weight_copies(info_ref, shape, pieces, scratch):
-    depth, _, column, parts = shape
+    depth, _, column, parts, chunks = shape
     own_l, *sent_l = pieces[: 1 + QUARTERS]
     own_w, own_u, *sent_w = pieces[1 + QUARTERS :]
     weight, lower, sems = scratch
@@ -797,12 +897,14 @@
     jobs = factor_jobs(info_ref, own_l, sent_l, pl.ds(column, depth), lower)
     jobs.append((own_w, weight.at[rows_at(side * half, half), :]))
     jobs.append((own_u, weight.at[rows_at(depth + side * (RANKS // 2), RANKS // 2), :]))
-    for number, sent in enumerate(sent_w):
+    for number in range(parts):
         place = info_ref[(1 if parts == QUARTERS else 1 + QUARTERS) + number]
         start = (1 - side) * half + place * part
         base = depth + (1 - side) * (RANKS // 2) + place * few
-        jobs.append((sent.at[pl.ds(0, part), :], weight.at[rows_at(start, part), :]))
-        jobs.append((sent.at[pl.ds(part, few), :], weight.at[rows_at(base, few), :]))
+        for chunk, cols in enumerate(chunks):
+            sent = sent_w[chunk * parts + number]
+            jobs.append((sent.at[pl.ds(0, part), :], weight.at[rows_at(start, part), cols]))
+            jobs.append((sent.at[pl.ds(part, few), :], weight.at[rows_at(base, few), cols]))
     return with_sems(jobs, sems)
 
 
@@ -817,7 +919,7 @@
         return pl.ds(pl.multiple_of(start, 128), count)
 
     jobs = factor_jobs(info_ref, own_l, sent_l, pl.ds(0, D), lower)
-    jobs += factor_jobs(info_ref, own_l, sent_l, pl.ds(LOWER_W, UNITED), upper)
+    jobs += factor_jobs(info_ref, own_l, sent_l, pl.ds(D, UNITED), upper)
     mine = lanes_at(side * half, half)
     jobs.append((own_w.at[pl.ds(0, OWN_ROWS), :], weight.at[pl.ds(0, OWN_ROWS), mine]))
     jobs.append((own_end, weight.at[pl.ds(OWN_ROWS, 16), mine]))
@@ -917,6 +1019,14 @@
 GRADS_W = MIX + 3 * D + 3 * FF
 
 
+def store_grads(total, grads_ref):
+    @pl.when(pl.program_id(0) == pl.num_programs(0) - 1)
+    def _():
+        half = total.shape[1] // 2
+        for place in range(2):
+            grads_ref[place] = total[:, place * half : (place + 1) * half].astype(BF16)
+
+
 def add_factor_grads(total, lower_cols, upper_cols, grad_mid, hidden, mid, grad):
     gm_t = grad_mid.astype(F32).T.astype(BF16)
     mid_t = (mid.astype(F32) * ADAPT_SCALE).T.astype(BF16)
@@ -1002,52 +1112,21 @@
             dattended_ref[...] = djoined.astype(BF16)
     add_factor_grads(total, MERGE_L, MERGE_U, grad_mid, joined, merge_mid, grad)
 
-    @pl.when(pl.program_id(0) == pl.num_programs(0) - 1)
-    def _():
-        half = total.shape[1] // 2
-        for place in range(2):
-            grads_ref[place] = total[:, place * half : (place + 1) * half].astype(BF16)
-
-
-MIXER_GRADS_W = D + UNITED + 128
+    store_grads(total, grads_ref)
 
 
 def mixer_backward_kernel(
-    info_ref, grad_ref, hidden_ref, x_ref, dmiddle_ref, mid_ref, mask_ref, gain_ref, *rest
+    info_ref, grad_ref, grad_mid_ref, x_ref, dmiddle_ref, gain_ref, *rest
 ):
     pieces, rest = taken(rest, MIXER_PIECES)
-    out_ref, grads_ref = rest[:2]
-    scratch = rest[2:6]
-    total = rest[6]
-    weight, upper, lower, _ = scratch
+    out_ref, *scratch = rest
+    weight, _, lower, _ = scratch
     copies = mixer_copies(info_ref, pieces, scratch)
-
-    def begin():
-        start_mixer(copies, weight)
-        total[...] = jnp.zeros_like(total)
-
-    at_first(begin)
+    at_first(lambda: start_mixer(copies, weight))
     at_first(lambda: wait_all(copies))
-    grad = grad_ref[...]
-    grad_mid = masked(ADAPT_SCALE * dot_nt(grad, upper[...]), mask_ref[...].astype(F32))
-    dhidden = dot_nn(grad, weight[...]) + dot_nn(grad_mid, lower[...])
+    dhidden = dot_nn(grad_ref[...], weight[...]) + dot_nn(grad_mid_ref[...], lower[...])
     value = x_ref[...].astype(F32)
     out_ref[...] = (dmiddle_ref[...] + norm_back(dhidden, value, gain_ref[0:1, :])).astype(BF16)
-    add_factor_grads(
-        total,
-        slice(0, D),
-        slice(D, D + UNITED),
-        grad_mid,
-        hidden_ref[...],
-        mid_ref[...],
-        grad,
-    )
-
-    @pl.when(pl.program_id(0) == pl.num_programs(0) - 1)
-    def _():
-        half = total.shape[1] // 2
-        for place in range(2):
-            grads_ref[place] = total[:, place * half : (place + 1) * half].astype(BF16)
 
 
 def row_call(kernel, rows, ins, fixed_ins, raw, outs, fixed_outs, scratch, info, name, flops, moved):
@@ -1068,7 +1147,7 @@
         out_shape=[jax.ShapeDtypeStruct((rows, width), kind) for width, kind in outs]
         + [jax.ShapeDtypeStruct(shape, BF16) for shape in fixed_outs],
         compiler_params=pltpu.CompilerParams(
-            vmem_limit_bytes=60 << 20, dimension_semantics=("arbitrary",)
+            vmem_limit_bytes=58 << 20, dimension_semantics=("arbitrary",)
         ),
         cost_estimate=pl.CostEstimate(flops=flops, bytes_accessed=moved, transcendentals=0),
         name=name,
@@ -1120,22 +1199,22 @@
     )
 
 
-def mixer_backward(info, grad, hidden, x, dmiddle, mid, mask, gain, pieces):
+def mixer_backward(info, grad, grad_mid, x, dmiddle, gain, pieces):
     rows = x.shape[0]
     return row_call(
         mixer_backward_kernel,
         rows,
-        [grad, hidden, x, dmiddle, mid, mask],
+        [grad, grad_mid, x, dmiddle],
         [gain[None, :]],
         pieces,
         [(D, BF16)],
-        [(2, RANKS, MIXER_GRADS_W // 2)],
-        mixer_scratch() + [pltpu.VMEM((RANKS, MIXER_GRADS_W), F32)],
+        [],
+        mixer_scratch(),
         info,
         "mixer_backward",
         2 * rows * D * UNITED,
         2 * D * UNITED + 8 * rows * D,
-    )
+    )[0]
 
 
 SEQ_SLOTS = 3
@@ -1175,45 +1254,91 @@
 def core_sums(grads):
     core = lax.axis_index("rep") % 2
     kept = lax.dynamic_index_in_dim(grads, core, 0, keepdims=False)
-    sent = lax.dynamic_index_in_dim(grads, 1 - core, 0, keepdims=False)
+    sent = lax.dynamic_index_in_dim(grads, 1 - core, 0, keepdims=False).astype(BF16)
     return kept.astype(F32) + beside(sent, 1).astype(F32)
 
 
-def row_sums(total, side, send):
+def shard_sums(total):
+    side = lax.axis_index("shard")
+    axis = total.ndim - 2
+    mine = total.shape[axis] // 2
+    kept = lax.dynamic_slice_in_dim(total, side * mine, mine, axis)
+    sent = lax.dynamic_slice_in_dim(total, (1 - side) * mine, mine, axis).astype(BF16)
+    return kept.astype(F32) + across(sent).astype(F32)
+
+
+def all_sums(total):
+    chips, shards = lax.axis_size("rep") // 2, lax.axis_size("shard")
+    order = [(side, 2 * far + near) for side in range(shards) for near in range(2) for far in range(chips // 2)]
+    groups = [[(2 * chip + core) * shards + side for side, chip in order] for core in range(2)]
+    count = chips * shards
+    parts = lax.all_to_all(
+        total.astype(BF16).reshape(count, total.shape[0] // count, total.shape[1]),
+        ("rep", "shard"),
+        split_axis=0,
+        concat_axis=0,
+        axis_index_groups=groups,
+        tiled=True,
+    )
+    return jnp.sum(parts.astype(F32), axis=0)
+
+
+def far_bits():
+    return [bit for bit in (4 << shift for shift in range(16)) if bit < lax.axis_size("rep")]
+
+
+def swaps():
+    found = [0]
+    for bit in far_bits():
+        found += [one + bit for one in found]
+    return found[1:]
+
+
+def near_sums(total):
     mine = total.shape[0] // 2
+    side = lax.axis_index("rep") // 2 % 2
     kept = lax.dynamic_slice_in_dim(total, side * mine, mine, 0)
     sent = lax.dynamic_slice_in_dim(total, (1 - side) * mine, mine, 0).astype(BF16)
-    return kept + send(sent).astype(F32)
-
-
-def shard_sums(total):
-    return row_sums(total, lax.axis_index("shard"), across)
-
-
-def chip_bits():
-    count, bits = lax.axis_size("rep") // 2, []
-    while 2 ** len(bits) < count:
-        bits.append(2 ** (len(bits) + 1))
-    return bits
-
-
-def bit_sums(total, bit):
-    return row_sums(total, lax.axis_index("rep") // bit % 2, lambda value: beside(value, bit))
-
-
-def ordered(mine, other, side, axis):
+    return kept.astype(F32) + beside(sent, 2).astype(F32)
+
+
+def far_sums(total):
+    place = lax.axis_index("rep") // 4
+    size = total.shape[0] // (1 + len(swaps()))
+    own = lax.dynamic_slice_in_dim(total, place * size, size, 0).astype(F32)
+    for swap in swaps():
+        sent = lax.dynamic_slice_in_dim(total, (place ^ (swap // 4)) * size, size, 0).astype(BF16)
+        own = own + beside(sent, swap).astype(F32)
+    return own
+
+
+def far_rows(own):
+    place = lax.axis_index("rep") // 4
+    parts = jnp.stack([own] + [beside(own, swap) for swap in swaps()])
+    bit = 1
+    while bit < parts.shape[0]:
+        pairs = parts.reshape(-1, 2, bit, *own.shape)
+        parts = jnp.where(place // bit % 2 == 0, pairs, pairs[:, ::-1]).reshape(-1, *own.shape)
+        bit *= 2
+    return parts.reshape(-1, own.shape[1])
+
+
+def near_rows(own):
+    other = beside(own, 2)
     return jnp.where(
-        side == 0,
-        jnp.concatenate([mine, other], axis=axis),
-        jnp.concatenate([other, mine], axis=axis),
-    )
-
-
-def spread_rows(own, bits):
-    rep = lax.axis_index("rep")
-    for bit in reversed(bits):
-        own = ordered(own, beside(own, bit), rep // bit % 2, 0)
-    return ordered(own, beside(own, 1), rep % 2, 1)
+        lax.axis_index("rep") // 2 % 2 == 0,
+        jnp.concatenate([own, other], axis=0),
+        jnp.concatenate([other, own], axis=0),
+    )
+
+
+def core_columns(whole):
+    other = beside(whole, 1)
+    return jnp.where(
+        lax.axis_index("rep") % 2 == 0,
+        jnp.concatenate([whole, other], axis=1),
+        jnp.concatenate([other, whole], axis=1),
+    )
 
 
 def row_orders(assignment, stripe, groups):
@@ -1283,27 +1408,35 @@
     def work_rows(value):
         return dot_nn(place, value).astype(BF16)
 
+    def over_core(value):
+        return beside(value, 1)
+
+    def over_x(value):
+        return beside(value, 2)
+
     mixer_t = mixer_weight.T
     mixer_sent = jnp.pad(part_of(mixer_t, QUARTERS, quarter, 1), ((0, 8), (0, 0)))
     mixer_sent = [mixer_sent[cols] for cols in MIXER_CHUNKS]
-    mixer_in = [across(chunk) for chunk in mixer_sent]
+    in_one = across(mixer_sent[0])
     token_rows = exchange(send_rows(after(tokens, *mixer_sent)))
-    factors = jnp.concatenate(
-        [
-            mixer_down,
-            merge_down,
-            expand_down,
-            reduce_down,
-            jnp.pad(mixer_up, ((0, 0), (0, UNITED - GIVEN))),
-        ],
-        axis=1,
-    )
-    factors_in = across(part_of(factors, QUARTERS, quarter))
+
+    in_two = across(after(mixer_sent[1], in_one))
+    one_x = over_x(in_one)
+    cotangent, lengths, merge_weight, expand_weight, reduce_weight, _ = lax.optimization_barrier(
+        (cotangent, lengths, merge_weight, expand_weight, reduce_weight, in_one)
+    )
+    mixer_f = jnp.concatenate(
+        [mixer_down, jnp.pad(mixer_up, ((0, 0), (0, UNITED - GIVEN)))], axis=1
+    )
+    in_f = across(after(part_of(mixer_f, QUARTERS, quarter), in_one))
+    grad_sent = send_rows(cotangent)
     mixer_end = jnp.pad(mixer_t[OWN_ROWS:], ((0, OWN_ROWS + 16 - GIVEN), (0, 0)))
-    grad_sent = send_rows(cotangent)
+    block_f = jnp.concatenate([merge_down, expand_down, reduce_down], axis=1)
     merge_sent = sent_rows(merge_weight, merge_up, 4, quarter)
     expand_sent = sent_rows(expand_weight, expand_up, 4, quarter)
+    expand_sent = [expand_sent[:, cols] for cols in EXPAND[4]]
     reduce_sent = sent_rows(reduce_weight, reduce_up, 2, core)
+    block_f_sent = part_of(block_f, QUARTERS, quarter)
 
     finish = jnp.cumsum(lengths[0])
     begin = finish - lengths[0]
@@ -1319,37 +1452,71 @@
     cosine, sines = rotation_tables(position)
     params = ssm_params(filter_taps, filter_bias, step_bias, decay_rate, skip_gain, state_gain)
 
-    mixer_in[0], cosine, sines, mask, *_ = lax.optimization_barrier(
-        (mixer_in[0], cosine, sines, mask, mixer_end, grad_sent, merge_sent, expand_sent, reduce_sent)
-    )
-    mixer_in[1] = after(mixer_in[1], mixer_in[0])
-    merge_in = across(after(merge_sent, mixer_in[1]))
-    lowers = (factors, *spread_quarter(factors_in))
+    in_two, cosine, sines, mask, *_ = lax.optimization_barrier(
+        (in_two, cosine, sines, mask, mixer_end, grad_sent, merge_sent, *expand_sent, reduce_sent)
+        + (block_f,)
+    )
+
+    two_x = over_x(in_two)
+    merge_in = across(after(merge_sent, in_two))
+    expand_one = across(after(expand_sent[0], in_two))
+    in_f = after(in_f, in_two)
+    f_x = over_x(in_f)
+    one_x, two_x, f_x, merge_in = lax.optimization_barrier((one_x, two_x, f_x, merge_in))
+    mixer_f_p = (mixer_f, in_f, f_x, over_core(in_f), over_core(f_x))
     mixer_p = (
-        *lowers,
+        *mixer_f_p,
         mixer_t,
         mixer_end,
-        *spread_quarter(mixer_in[0]),
-        *spread_quarter(mixer_in[1]),
-    )
-    expand_in = across(after(expand_sent, mixer_in[1]))
+        in_one,
+        one_x,
+        over_core(in_one),
+        over_core(one_x),
+        in_two,
+        two_x,
+        over_core(in_two),
+        over_core(two_x),
+    )
+    grad_rows = exchange(after(grad_sent, token_rows))
     x = work_rows(token_rows)
-    grad_rows = exchange(after(grad_sent, token_rows))
-    merge_in = after(merge_in, x)
-    reduce_in = across(after(reduce_sent, merge_in))
+
+    gate = merge_in
+    block_f_in = across(after(block_f_sent, gate))
+    merge_x = over_x(merge_in)
+    expand_two = across(after(expand_sent[1], gate))
     united, hidden, mixer_mid = mixer_forward(info, x, mask, first_gain, mixer_p)
-    expand_in = after(expand_in, united)
+    united, block_f_in, expand_one = lax.optimization_barrier((united, block_f_in, expand_one))
+
+    reduce_in = across(after(reduce_sent, united))
+    expand_one_x = over_x(expand_one)
+    block_f_x = over_x(block_f_in)
     attended, logs, turned, kv_low = attend_forward(united, cosine, sines, first)
+    attended, merge_x, expand_two = lax.optimization_barrier((attended, merge_x, expand_two))
+
+    expand_two_x = over_x(expand_two)
+    near = [over_core(v) for v in (merge_in, merge_x, expand_one, expand_two, block_f_in)]
     joined, scan, starts = mamba_forward(united, attended, restart, params)
-
-    def rest_of_quarters(first_in):
-        second = beside(first_in, 2)
-        return (first_in, second, beside(first_in, 1), beside(after(second, joined), 1))
-
-    merge_p = (*lowers, merge_weight, merge_up, *rest_of_quarters(merge_in))
-    expand_p = (*lowers, expand_weight, expand_up, *rest_of_quarters(expand_in))
-    reduce_in = after(reduce_in, joined)
-    reduce_p = (*lowers, reduce_weight, reduce_up, reduce_in, beside(reduce_in, 1))
+    joined, reduce_in, expand_one_x, expand_two_x, block_f_x, *near = lax.optimization_barrier(
+        (joined, reduce_in, expand_one_x, expand_two_x, block_f_x, *near)
+    )
+
+    merge_c, merge_xc, expand_one_c, expand_two_c, block_f_c = near
+    lowers = (block_f, block_f_in, block_f_x, block_f_c, over_core(block_f_x))
+    merge_p = (*lowers, merge_weight, merge_up, merge_in, merge_x, merge_c, merge_xc)
+    expand_p = (
+        *lowers,
+        expand_weight,
+        expand_up,
+        expand_one,
+        expand_one_x,
+        expand_one_c,
+        over_core(expand_one_x),
+        expand_two,
+        expand_two_x,
+        expand_two_c,
+        over_core(expand_two_x),
+    )
+    reduce_p = (*lowers, reduce_weight, reduce_up, reduce_in, over_core(reduce_in))
     grad_top = work_rows(after(grad_rows, joined))
     mixed, dmamba, dattended, dmiddle, block_grads = block(
         info, joined, x, grad_top, mask, second_gain, merge_p, expand_p, reduce_p
@@ -1367,41 +1534,53 @@
             .reshape(stripe, units, width)
         )
 
-    bits = chip_bits()
-    mixed_rows = exchange(leaving(mixed))
     block_sums = core_sums(block_grads)
+    dattended, block_sums, mixed = lax.optimization_barrier((dattended, block_sums, mixed))
+    block_sums = shard_sums(block_sums)
+    mixed_leaving = leaving(mixed)
     dquery, dkv = attend_backward(turned, kv_low, dattended, logs, cosine, sines, first)
-    dquery, block_sums = lax.optimization_barrier((dquery, block_sums))
-    block_sums = shard_sums(block_sums)
-    dunited = mamba_backward(united, scan, starts, dmamba, dquery, dkv, restart, params)
-    dunited, block_sums, mixed_rows = lax.optimization_barrier((dunited, block_sums, mixed_rows))
-    block_sums = bit_sums(block_sums, bits[0])
-    work_grad, mixer_grads = mixer_backward(
-        info, dunited, hidden, x, dmiddle, mixer_mid, mask, first_gain, mixer_p
-    )
-    work_grad, block_sums = lax.optimization_barrier((work_grad, block_sums))
+    dquery, block_sums, mixed_leaving = lax.optimization_barrier(
+        (dquery, block_sums, mixed_leaving)
+    )
+    mixed_rows = exchange(mixed_leaving)
+    block_sums = near_sums(block_sums)
+    dunited, grad_mid, mixer_grads = mamba_backward(
+        united, scan, starts, dmamba, dquery, dkv, hidden, mixer_mid, mask, restart, info, params,
+        mixer_f_p,
+    )
+    dunited, block_sums, mixed_rows, mixer_grads = lax.optimization_barrier(
+        (dunited, block_sums, mixed_rows, mixer_grads)
+    )
+    mixer_sums = core_sums(mixer_grads)
+    dunited, mixer_sums = lax.optimization_barrier((dunited, mixer_sums))
+    mixer_sums = all_sums(mixer_sums)
+    block_sums = far_sums(block_sums)
+    work_grad = mixer_backward(info, dunited, grad_mid, x, dmiddle, first_gain, mixer_p)
+    work_grad, block_sums, mixer_sums = lax.optimization_barrier(
+        (work_grad, block_sums, mixer_sums)
+    )
     grad_leaving = leaving(work_grad)
     token_grads = exchange(grad_leaving)
-    mixer_grads, block_sums, mixed_rows, _ = lax.optimization_barrier(
-        (mixer_grads, block_sums, mixed_rows, grad_leaving)
+    mixer_sums, block_sums, mixed_rows, _ = lax.optimization_barrier(
+        (mixer_sums, block_sums, mixed_rows, grad_leaving)
     )
 
     def finish(_, carry):
-        mixer_grads, block_sums, _ = carry
-        mixer_sums = bit_sums(shard_sums(core_sums(mixer_grads)), bits[0])
+        mixer_sums, block_sums, _ = carry
         sums = jnp.concatenate([mixer_sums, block_sums], axis=1)
-        for bit in bits[1:]:
-            sums = bit_sums(sums, bit)
-        return mixer_grads, block_sums, spread_rows(sums.astype(BF16), bits)
-
-    width_sums = mixer_grads.shape[2] + block_sums.shape[1]
+        return mixer_sums, block_sums, core_columns(near_rows(far_rows(sums.astype(BF16))))
+
+    cut = mixer_sums.shape[1]
     _, _, final = lax.fori_loop(
         0,
         lax.optimization_barrier(jnp.int32(1)),
         finish,
-        (mixer_grads, block_sums, jnp.zeros((RANKS // 2, 2 * width_sums), BF16)),
-    )
-    cut = mixer_grads.shape[2]
+        (
+            mixer_sums,
+            block_sums,
+            jnp.zeros((RANKS // 2, 2 * (cut + block_sums.shape[1])), BF16),
+        ),
+    )
     final = final.reshape(RANKS // 2, 2, -1)
     mixer_final = final[:, :, :cut].reshape(RANKS // 2, -1).astype(F32)
     block_final = final[:, :, cut:].reshape(RANKS // 2, -1).astype(F32)

time: 534 us -> 482 us (0.903)
  waiting for transfers between devices: 159 us -> 76 us
  starting transfers between devices: 48.9 us -> 74.9 us
  Pallas kernels: 232 us -> 239 us
    ppermute x8 -> x9, waiting for transfers between devices: 70.1 us -> 14 us  [across(): return lax.ppermute(value, 'shard', swap_pairs(2, 1))]
    ppermute x26 -> x33, waiting for transfers between devices: 88.4 us -> 60.5 us  [beside(): return lax.ppermute(value, 'rep', swap_pairs(lax.axis_size('rep'), bit))]
    ppermute x26 -> x33, starting transfers between devices: 15.6 us -> 35.6 us  [beside(): return lax.ppermute(value, 'rep', swap_pairs(lax.axis_size('rep'), bit))]
    pallas_call x1, Pallas kernels: 48.8 us -> 59.3 us  [mamba_backward(): pl.pallas_call(mamba_backward_kernel, grid_spec=pltpu.PrefetchScalarGridS...]
    all_to_all x0 -> x1, starting transfers between devices: none -> 6.93 us  [all_sums(): lax.all_to_all(total.astype(BF16).reshape(count, total.shape[0] // count,...]
    ppermute x8 -> x9, starting transfers between devices: 11.5 us -> 9.88 us  [across(): return lax.ppermute(value, 'shard', swap_pairs(2, 1))]
  transfers between devices with their start and end apart: 38 -> 47, of which waited for: 15 -> 11; matrix products, arithmetic and copies ran while one was open for 12% -> 13% of each run, Pallas kernels for 28% -> 32%
where the time goes in v3:
time: 482 us; the launch traced here: 478 us
  Pallas kernels  239 us (50%)
  waiting for transfers between devices  76 us (16%)
  starting transfers between devices  74.9 us (16%)
  matrix products  37.2 us (8%)
  local copies, waits for them, and re-layouts  32.8 us (7%)
  other arithmetic  16.7 us (3%)
    pallas_call x3, Pallas kernels, row_call(): pl.pallas_call(kernel, grid_spec=pltpu.PrefetchScalarGridSpec(num_scalar_...  127 us
    ppermute x33, waiting for transfers between devices, beside(): return lax.ppermute(value, 'rep', swap_pairs(lax.axis_size('rep'), bit))  60.5 us
    pallas_call x1, Pallas kernels, mamba_backward(): pl.pallas_call(mamba_backward_kernel, grid_spec=pltpu.PrefetchScalarGridS...  59.3 us
    ppermute x33, starting transfers between devices, beside(): return lax.ppermute(value, 'rep', swap_pairs(lax.axis_size('rep'), bit))  35.6 us
    all_to_all x4, starting transfers between devices, exchange(): lax.all_to_all(value, ('rep', 'shard'), split_axis=0, concat_axis=0, tile...  22.4 us
    pallas_call x1, Pallas kernels, mamba_forward(): pl.pallas_call(mamba_forward_kernel, grid_spec=pltpu.PrefetchScalarGridSp...  22 us
    dot_general x4, matrix products, dot_nn(): lax.dot_general(a, b, (((1,), (0,)), ((), ())), preferred_element_type=F32)  18.1 us
    pallas_call x1, Pallas kernels, attend_backward(): pl.pallas_call(attend_backward_kernel, grid_spec=pltpu.PrefetchScalarGrid...  15.3 us
  transfers between devices with their start and end apart: 47, of which 11 were waited for; matrix products, arithmetic and copies ran while one was open for 13% of the time, Pallas kernels for 32%

profile of v3, /device:TPU:0, one launch (start us, length us, event | category | flops | bytes accessed | tf_op | source)
XLA Modules:
  0.0 478.3 jit_solution(3564703491015666474)
XLA Ops:
  3.0 3.0 collective-permute-start.2
  6.2 3.7 fusion.19
  9.9 5.2 %all-to-all-start = ((bf16[32,32,1024]{2,1,0:T(8,128)(2,1)}), bf16[32,32,1024]{2,1,0:T(8,128)(2,1)}, u32[]{:S(2)}, u32[]{:S(2)}) async-start(bf16[32,32,1024]{2,1,0:T(8,128)(2,1)} %bitcast.95), calls=%async_computation | async-start | bytes 4194304 | tf_op jit(solution)/shard_map/all_to_all | solution.py:1362
  18.8 4.1 collective-permute-done.2.rest_7_
  23.1 2.8 collective-permute-start.3
  28.5 1.9 fusion.29
  34.8 7.7 %collective-permute-start.5 = (bf16[2048,128]{1,0:T(8,128)(2,1)}, bf16[2048,128]{1,0:T(8,128)(2,1)}, u32[]{:S(2)}, u32[]{:S(2)}) collective-permute-start(bf16[2048,128]{1,0:T(8,128)(2,1)} %collective-permute-done.2.rest_7_), channel_id=1, source_target_pairs={{0,4},{2,6},{4,0},{6,2},{8,12},{10,14},{12,8},{14,10},{16,20},{18,... | collective-permute-start | bytes 1572872 | tf_op jit(solution)/shard_map/ppermute | solution.py:1242
  42.6 3.8 fusion.20
  46.4 2.3 collective-permute-done.3.rest_11_
  48.7 3.5 collective-permute-start.6
  56.0 14.9 %collective-permute-done.7.rest_2_ = bf16[16,5248]{1,0:T(8,128)(2,1)S(1)} collective-permute-done((bf16[16,5248]{1,0:T(8,128)(2,1)S(1)}, bf16[16,5248]{1,0:T(8,128)(2,1)S(1)}, u32[]{:S(2)}, u32[]{:S(2)}) %collective-permute-start.7) | collective-permute-done | bytes 167968 | tf_op jit(solution)/shard_map/ppermute | solution.py:1242
  72.9 5.3 %fusion.22.x_ref = bf16[1024,1024]{1,0:T(8,128)(2,1)} fusion(bf16[1024,1024]{1,0:T(8,128)(2,1)} %bitcast.17, s32[1024]{0:T(1024)S(1)} %fusion.46), kind=kOutput, calls=%fused_computation.29 | convolution fusion | flops 2149580800 | bytes 4198400 | tf_op jit(solution)/shard_map/dot_general | solution.py:40
  80.1 2.0 collective-permute-start.15
  82.1 23.5 %mixer_forward.1 = (f32[1024,4224]{1,0:T(8,128)}, bf16[1024,1024]{1,0:T(8,128)(2,1)}, bf16[1024,128]{1,0:T(8,128)(2,1)}) custom-call(s32[7]{0:T(128)} %stack.52.info_ref, bf16[1024,1024]{1,0:T(8,128)(2,1)} %fusion.22.x_ref, bf16[1024,128]{1,0:T(8,128)(2,1)} %compare_convert_fusion.1.mask_ref, f32[1,1024]{1,0:T(1,128)} %bitcast.109, ...), custom_call_target="tpu_custom_call" | custom-call | flops 8858370048 | bytes 25952256 | tf_op jit(solution)/shard_map/mixer_forward/pallas_call | solution.py:1136
  106.7 4.8 %all-to-all-start.1 = ((bf16[32,32,1024]{2,1,0:T(8,128)(2,1)}), bf16[32,32,1024]{2,1,0:T(8,128)(2,1)}, u32[]{:S(2)}, u32[]{:S(2)}) async-start(bf16[32,32,1024]{2,1,0:T(8,128)(2,1)} %bitcast.94), calls=%async_computation.1 | async-start | bytes 4194304 | tf_op jit(solution)/shard_map/all_to_all | solution.py:1362
  111.6 15.1 %attend_forward.1 = (bf16[1024,512]{1,0:T(8,128)(2,1)S(1)}, f32[8,8,128]{2,1,0:T(8,128)S(1)}, bf16[1024,512]{1,0:T(8,128)(2,1)S(1)}, bf16[1024,256]{1,0:T(8,128)(2,1)S(1)}) custom-call(s32[8]{0:T(128)S(1)} %get-tuple-element.288.first_ref, f32[1024,4224]{1,0:T(8,128)} %get-tuple-element.227.query_ref.kv_ref.united_ref.above_ref, ...), custom_call_target="tpu_custom_call" | custom-call | flops 15000000512 | bytes 6000000 | tf_op jit(solution)/shard_map/attend_forward/pallas_call | solution.py:753
  126.7 4.9 %collective-permute-done.18.rest_22_ = bf16[144,2048]{1,0:T(8,128)(2,1)} collective-permute-done((bf16[144,2048]{1,0:T(8,128)(2,1)S(1)}, bf16[144,2048]{1,0:T(8,128)(2,1)}, u32[]{:S(2)}, u32[]{:S(2)}) %collective-permute-start.18) | collective-permute-done | bytes 589856 | tf_op jit(solution)/shard_map/ppermute | solution.py:1238
  131.8 5.2 %collective-permute-start.22 = (bf16[16,5120]{1,0:T(8,128)(2,1)S(1)}, bf16[16,5120]{1,0:T(8,128)(2,1)S(1)}, u32[]{:S(2)}, u32[]{:S(2)}) collective-permute-start(bf16[16,5120]{1,0:T(8,128)(2,1)S(1)} %copy-done.45), channel_id=1, source_target_pairs={{0,4},{2,6},{4,0},{6,2},{8,12},{10,14},{12,8},{14,10},{16,20},{18,... | collective-permute-start | bytes 491528 | tf_op jit(solution)/shard_map/ppermute | solution.py:1242
  137.7 7.1 %collective-permute-done.22.rest_2_.rest_13_.rest_28_ = bf16[16,5120]{1,0:T(8,128)(2,1)S(1)} collective-permute-done((bf16[16,5120]{1,0:T(8,128)(2,1)S(1)}, bf16[16,5120]{1,0:T(8,128)(2,1)S(1)}, u32[]{:S(2)}, u32[]{:S(2)}) %collective-permute-start.22) | collective-permute-done | bytes 163872 | tf_op jit(solution)/shard_map/ppermute | solution.py:1242
  146.6 22.0 %mamba_forward.1 = (bf16[1024,2048]{1,0:T(8,128)(2,1)S(1)}, f32[1024,1536]{1,0:T(8,128)}, f32[8,128,1536]{2,1,0:T(8,128)}) custom-call(s32[8]{0:T(128)S(1)} %compare_convert_fusion.2.restart_ref, f32[1024,4224]{1,0:T(8,128)} %get-tuple-element.227.query_ref.kv_ref.united_ref.above_ref, bf16[1024,512]{1,0:T(8,128)(2,1)S(1)} %get-tuple-element.232.attended_ref, ...), custom_call_target="tpu_custom_call" | custom-call | flops 20000000000 | bytes 50000000 | tf_op jit(solution)/shard_map/mamba_forward/pallas_call | solution.py:479
  168.6 2.0 copy-done.10
  170.6 3.0 collective-permute-done.21.rest_23_
  173.6 2.6 collective-permute-done.19.rest_33_
  177.3 5.3 %fusion.23.grad_ref = bf16[1024,1024]{1,0:T(8,128)(2,1)} fusion(bf16[1024,1024]{1,0:T(8,128)(2,1)} %bitcast.26, s32[1024]{0:T(1024)S(1)} %fusion.46), kind=kOutput, calls=%fused_computation.30 | convolution fusion | flops 2149580800 | bytes 4198400 | tf_op jit(solution)/shard_map/dot_general | solution.py:40
  183.5 84.4 %block.1 = (bf16[1024,1024]{1,0:T(8,128)(2,1)}, f32[1024,1536]{1,0:T(8,128)}, bf16[1024,512]{1,0:T(8,128)(2,1)}, f32[1024,1024]{1,0:T(8,128)}, bf16[2,128,5632]{2,1,0:T(8,128)(2,1)}) custom-call(s32[7]{0:T(128)} %stack.52.info_ref, bf16[1024,2048]{1,0:T(8,128)(2,1)} %copy-done.10, bf16[1024,1024]{1,0:T(8,128)(2,1)} %fusion.22.x_ref, ...), custom_call_target="tpu_custom_call" | custom-call | flops 42949672960 | bytes 29360128 | tf_op jit(solution)/shard_map/block/pallas_call | solution.py:1136
  267.9 2.6 dynamic-slice_bitcast_fusion
  270.5 3.5 collective-permute-done.32
  274.0 2.2 convert_add_fusion
  276.5 15.3 %attend_backward.1 = (bf16[1024,512]{1,0:T(8,128)(2,1)S(1)}, bf16[1024,256]{1,0:T(8,128)(2,1)S(1)}) custom-call(s32[8]{0:T(128)S(1)} %get-tuple-element.288.first_ref, bf16[1024,512]{1,0:T(8,128)(2,1)S(1)} %get-tuple-element.254.turned_ref, bf16[1024,256]{1,0:T(8,128)(2,1)S(1)} %get-tuple-element.255.kv_low_ref, bf16[1024,512]{1,0:T(8,128)(2,1)S(1)} %copy-done.11, ...), custom_call_target="tpu_custom_call" | custom-call | flops 15000000512 | bytes 6000000 | tf_op jit(solution)/shard_map/attend_backward/pallas_call | solution.py:790
  291.9 3.8 fusion.24
  297.7 6.1 %all-to-all-start.2 = ((bf16[32,32,1024]{2,1,0:T(8,128)(2,1)}), bf16[32,32,1024]{2,1,0:T(8,128)(2,1)S(1)}, u32[]{:S(2)}, u32[]{:S(2)}) async-start(bf16[32,32,1024]{2,1,0:T(8,128)(2,1)} %bitcast.97), calls=%async_computation.2 | async-start | bytes 4194304 | tf_op jit(solution)/shard_map/all_to_all | solution.py:1362
  303.8 59.3 %mamba_backward.1 = (bf16[1024,4224]{1,0:T(8,128)(2,1)}, bf16[1024,128]{1,0:T(8,128)(2,1)}, bf16[2,128,2688]{2,1,0:T(8,128)(2,1)}) custom-call(s32[8]{0:T(128)} %copy-done.9, s32[7]{0:T(128)} %stack.52.info_ref, f32[1024,4224]{1,0:T(8,128)} %get-tuple-element.227.query_ref.kv_ref.united_ref.above_ref, ...), custom_call_target="tpu_custom_call" | custom-call | flops 44999999488 | bytes 60000000 | tf_op jit(solution)/shard_map/mamba_backward/pallas_call | solution.py:521
  363.2 1.9 convert_add_fusion.3
  365.1 2.1 dynamic-slice_bitcast_fusion.2
  369.4 3.5 collective-permute-start.38
  373.8 2.1 convert_add_fusion.2
  375.9 6.9 %all-to-all-start.3 = ((bf16[16,8,2688]{2,1,0:T(8,128)(2,1)}), bf16[16,8,2688]{2,1,0:T(8,128)(2,1)S(1)}, u32[]{:S(2)}, u32[]{:S(2)}) async-start(bf16[16,8,2688]{2,1,0:T(8,128)(2,1)} %bitcast.68), calls=%async_computation.3 | async-start | bytes 1376256 | tf_op jit(solution)/shard_map/all_to_all | solution.py:1275
  383.9 19.2 %mixer_backward.1 = bf16[1024,1024]{1,0:T(8,128)(2,1)} custom-call(s32[7]{0:T(128)} %stack.52.info_ref, bf16[1024,4224]{1,0:T(8,128)(2,1)} %get-tuple-element.274.grad_ref, bf16[1024,128]{1,0:T(8,128)(2,1)} %get-tuple-element.275.grad_mid_ref, bf16[1024,1024]{1,0:T(8,128)(2,1)} %fusion.22.x_ref, f32[1024,1024]{1,0:T(8,128)} %get-tuple-element.276.dmiddle_ref, ...), custom_call_target="tpu_custom_call" | custom-call | flops 8858370048 | bytes 17039360 | tf_op jit(solution)/shard_map/mixer_backward/pallas_call | solution.py:1136
  403.3 5.4 %fusion.25 = bf16[1024,1024]{1,0:T(8,128)(2,1)} fusion(bf16[1024,1024]{1,0:T(8,128)(2,1)} %mixer_backward.1, s32[1024]{0:T(1024)S(1)} %fusion.46), kind=kOutput, calls=%fused_computation.32 | convolution fusion | flops 2149580800 | bytes 4198400 | tf_op jit(solution)/shard_map/dot_general | solution.py:1526
  408.7 3.9 collective-permute-start.41
  413.2 3.8 fusion.21
  417.0 6.3 %all-to-all-start.4 = ((bf16[32,32,1024]{2,1,0:T(8,128)(2,1)}), bf16[32,32,1024]{2,1,0:T(8,128)(2,1)}, u32[]{:S(2)}, u32[]{:S(2)}) async-start(bf16[32,32,1024]{2,1,0:T(8,128)(2,1)} %bitcast.36), calls=%async_computation.4 | async-start | bytes 4194304 | tf_op jit(solution)/shard_map/all_to_all | solution.py:1362
  424.8 36.2 %while.13 = (s32[]{:T(128)}, bf16[64,16640]{1,0:T(8,128)(2,1)}, s32[]{:T(128)}, bf16[4,8,8320]{2,1,0:T(8,128)(2,1)S(1)}, s32[]{:T(128)}, /*index=5*/u32[]{:T(128...) while((s32[]{:T(128)}, bf16[64,16640]{1,0:T(8,128)(2,1)}, s32[]{:T(128)}, ...), condition=%wide.region_5.6_spmd, body=%wide.region_4.5_spmd.sunk | while | flops 14909519 | bytes 14910396 | solution.py:1574
  425.0 1.9 collective-permute-start
  427.0 29.4 %collective-permute-done = bf16[32,8320]{1,0:T(8,128)(2,1)S(1)} collective-permute-done((bf16[32,8320]{1,0:T(8,128)(2,1)S(1)}, bf16[32,8320]{1,0:T(8,128)(2,1)S(1)}, u32[]{:S(2)}, u32[]{:S(2)}) %collective-permute-start) | collective-permute-done | bytes 532512 | tf_op jit(solution)/shard_map/while/body/ppermute | solution.py:1242
  456.6 2.7 collective-permute-done.1
  461.1 2.6 reshape.330
  472.0 6.1 %fusion.8 = f32[4,256,1024]{2,1,0:T(8,128)} fusion(bf16[1024,1024,1]{1,0,2:T(8,128)(2,1)} %bitcast.38, s32[4,256]{1,0:T(4,128)S(1)} %multiply_add_fusion, s32[1024]{0:T(1024)S(1)} %copy-done.27), kind=kOutput, calls=%fused_computation.14 | convolution fusion | flops 2148532224 | bytes 6299648 | tf_op jit(solution)/shard_map/dot_general | solution.py:1532
  (239 shorter events, 45.6 us)
Async XLA Ops:
  3.0 19.9 %collective-permute-start.2 = (bf16[2048,128]{1,0:T(8,128)(2,1)}, bf16[2048,128]{1,0:T(8,128)(2,1)}, u32[]{:S(2)}, u32[]{:S(2)}) collective-permute-start(bf16[2048,128]{1,0:T(8,128)(2,1)} %slice.61), channel_id=1, source_target_pairs={{0,1},{1,0},{2,3},{3,2},{4,5},{5,4},{6,7},{7,6},{8,9},{9,8},{10,11... | collective-permute-start | bytes 1572872 | tf_op jit(solution)/shard_map/ppermute | solution.py:1238
  9.9 62.9 %all-to-all-start = ((bf16[32,32,1024]{2,1,0:T(8,128)(2,1)}), bf16[32,32,1024]{2,1,0:T(8,128)(2,1)}, u32[]{:S(2)}, u32[]{:S(2)}) async-start(bf16[32,32,1024]{2,1,0:T(8,128)(2,1)} %bitcast.95), calls=%async_computation | async-start | bytes 4194304 | tf_op jit(solution)/shard_map/all_to_all | solution.py:1362
  23.1 25.6 %collective-permute-start.3 = (bf16[2080,128]{1,0:T(8,128)(2,1)S(1)}, bf16[2080,128]{1,0:T(8,128)(2,1)}, u32[]{:S(2)}, u32[]{:S(2)}) collective-permute-start(bf16[2080,128]{1,0:T(8,128)(2,1)S(1)} %pad_slice_fusion.2), channel_id=1, source_target_pairs={{0,1},{1,0},{2,3},{3,2},{4,5},{5,4},{6,7},{7,6},{8,9},{9,8},{10,11... | collective-permute-start | bytes 1597448 | tf_op jit(solution)/shard_map/ppermute | solution.py:1238
  25.9 28.7 %collective-permute-start.4 = (bf16[16,5248]{1,0:T(8,128)(2,1)S(1)}, bf16[16,5248]{1,0:T(8,128)(2,1)S(1)}, u32[]{:S(2)}, u32[]{:S(2)}) collective-permute-start(bf16[16,5248]{1,0:T(8,128)(2,1)S(1)} %constant_dynamic-slice_fusion.1), channel_id=1, source_target_pairs={{0,1},{1,0},{2,3},{3,2},{4,5},{5,4},{6,7},{7,6},{8,9},{9,8},{10,11... | collective-permute-start | bytes 503816 | tf_op jit(solution)/shard_map/ppermute | solution.py:1238
  34.8 21.1 %collective-permute-start.5 = (bf16[2048,128]{1,0:T(8,128)(2,1)}, bf16[2048,128]{1,0:T(8,128)(2,1)}, u32[]{:S(2)}, u32[]{:S(2)}) collective-permute-start(bf16[2048,128]{1,0:T(8,128)(2,1)} %collective-permute-done.2.rest_7_), channel_id=1, source_target_pairs={{0,4},{2,6},{4,0},{6,2},{8,12},{10,14},{12,8},{14,10},{16,20},{18,... | collective-permute-start | bytes 1572872 | tf_op jit(solution)/shard_map/ppermute | solution.py:1242
  42.6 29.9 %collective-permute-start.11 = (bf16[2048,128]{1,0:T(8,128)(2,1)}, bf16[2048,128]{1,0:T(8,128)(2,1)}, u32[]{:S(2)}, u32[]{:S(2)}) collective-permute-start(bf16[2048,128]{1,0:T(8,128)(2,1)} %collective-permute-done.2.rest_7_), channel_id=1, source_target_pairs={{0,2},{2,0},{4,6},{6,4},{8,10},{10,8},{12,14},{14,12},{16,18},{18,... | collective-permute-start | bytes 1572872 | tf_op jit(solution)/shard_map/ppermute | solution.py:1242
  48.7 22.1 %collective-permute-start.6 = (bf16[2080,128]{1,0:T(8,128)(2,1)}, bf16[2080,128]{1,0:T(8,128)(2,1)}, u32[]{:S(2)}, u32[]{:S(2)}) collective-permute-start(bf16[2080,128]{1,0:T(8,128)(2,1)} %collective-permute-done.3.rest_11_), channel_id=1, source_target_pairs={{0,4},{2,6},{4,0},{6,2},{8,12},{10,14},{12,8},{14,10},{16,20},{18,... | collective-permute-start | bytes 1597448 | tf_op jit(solution)/shard_map/ppermute | solution.py:1242
  52.2 18.7 %collective-permute-start.8 = (bf16[272,1024]{1,0:T(8,128)(2,1)S(1)}, bf16[272,1024]{1,0:T(8,128)(2,1)S(1)}, u32[]{:S(2)}, u32[]{:S(2)}) collective-permute-start(bf16[272,1024]{1,0:T(8,128)(2,1)S(1)} %pad_maximum_fusion.2), channel_id=1, source_target_pairs={{0,1},{1,0},{2,3},{3,2},{4,5},{5,4},{6,7},{7,6},{8,9},{9,8},{10,11... | collective-permute-start | bytes 1671176 | tf_op jit(solution)/shard_map/ppermute | solution.py:1238
  54.6 16.3 %collective-permute-start.7 = (bf16[16,5248]{1,0:T(8,128)(2,1)S(1)}, bf16[16,5248]{1,0:T(8,128)(2,1)S(1)}, u32[]{:S(2)}, u32[]{:S(2)}) collective-permute-start(bf16[16,5248]{1,0:T(8,128)(2,1)S(1)} %collective-permute-done.4.rest_1_), channel_id=1, source_target_pairs={{0,4},{2,6},{4,0},{6,2},{8,12},{10,14},{12,8},{14,10},{16,20},{18,... | collective-permute-start | bytes 503816 | tf_op jit(solution)/shard_map/ppermute | solution.py:1242
  55.9 22.4 %collective-permute-start.13 = (bf16[2080,128]{1,0:T(8,128)(2,1)}, bf16[2080,128]{1,0:T(8,128)(2,1)}, u32[]{:S(2)}, u32[]{:S(2)}) collective-permute-start(bf16[2080,128]{1,0:T(8,128)(2,1)} %collective-permute-done.3.rest_11_), channel_id=1, source_target_pairs={{0,2},{2,0},{4,6},{6,4},{8,10},{10,8},{12,14},{14,12},{16,18},{18,... | collective-permute-start | bytes 1597448 | tf_op jit(solution)/shard_map/ppermute | solution.py:1242
  70.9 9.2 %collective-permute-start.12 = (bf16[2048,128]{1,0:T(8,128)(2,1)}, bf16[2048,128]{1,0:T(8,128)(2,1)}, u32[]{:S(2)}, u32[]{:S(2)}) collective-permute-start(bf16[2048,128]{1,0:T(8,128)(2,1)} %collective-permute-done.5.rest_8_), channel_id=1, source_target_pairs={{0,2},{2,0},{4,6},{6,4},{8,10},{10,8},{12,14},{14,12},{16,18},{18,... | collective-permute-start | bytes 1572872 | tf_op jit(solution)/shard_map/ppermute | solution.py:1242
  71.0 11.1 %collective-permute-start.14 = (bf16[2080,128]{1,0:T(8,128)(2,1)}, bf16[2080,128]{1,0:T(8,128)(2,1)}, u32[]{:S(2)}, u32[]{:S(2)}) collective-permute-start(bf16[2080,128]{1,0:T(8,128)(2,1)} %collective-permute-done.6.rest_12_), channel_id=1, source_target_pairs={{0,2},{2,0},{4,6},{6,4},{8,10},{10,8},{12,14},{14,12},{16,18},{18,... | collective-permute-start | bytes 1597448 | tf_op jit(solution)/shard_map/ppermute | solution.py:1242
  71.5 75.1 %copy-start.6 = (f32[1,128]{1,0:T(1,128)}, f32[1,128]{1,0:T(1,128)S(1)}, u32[]{:S(2)}) copy-start(f32[1,128]{1,0:T(1,128)S(1)} %get-tuple-element.312.decay_ref) | copy-start | bytes 1540
  72.4 5.8 %collective-permute-start.9 = (bf16[16,5248]{1,0:T(8,128)(2,1)}, bf16[16,5248]{1,0:T(8,128)(2,1)S(1)}, u32[]{:S(2)}, u32[]{:S(2)}) collective-permute-start(bf16[16,5248]{1,0:T(8,128)(2,1)} %copy-done.41), channel_id=1, source_target_pairs={{0,2},{2,0},{4,6},{6,4},{8,10},{10,8},{12,14},{14,12},{16,18},{18,... | collective-permute-start | bytes 503816 | tf_op jit(solution)/shard_map/ppermute | solution.py:1242
  72.5 7.6 %collective-permute-start.10 = (bf16[16,5248]{1,0:T(8,128)(2,1)S(1)}, bf16[16,5248]{1,0:T(8,128)(2,1)}, u32[]{:S(2)}, u32[]{:S(2)}) collective-permute-start(bf16[16,5248]{1,0:T(8,128)(2,1)S(1)} %collective-permute-done.7.rest_2_), channel_id=1, source_target_pairs={{0,2},{2,0},{4,6},{6,4},{8,10},{10,8},{12,14},{14,12},{16,18},{18,... | collective-permute-start | bytes 503816 | tf_op jit(solution)/shard_map/ppermute | solution.py:1242
  78.2 27.6 %collective-permute-start.16 = (bf16[144,2048]{1,0:T(8,128)(2,1)S(1)}, bf16[144,2048]{1,0:T(8,128)(2,1)S(1)}, u32[]{:S(2)}, u32[]{:S(2)}) collective-permute-start(bf16[144,2048]{1,0:T(8,128)(2,1)S(1)} %get-tuple-element.226), channel_id=1, source_target_pairs={{0,1},{1,0},{2,3},{3,2},{4,5},{5,4},{6,7},{7,6},{8,9},{9,8},{10,11... | collective-permute-start | bytes 1769480 | tf_op jit(solution)/shard_map/ppermute | solution.py:1238
  78.3 48.4 %collective-permute-start.17 = (bf16[272,1024]{1,0:T(8,128)(2,1)}, bf16[272,1024]{1,0:T(8,128)(2,1)}, u32[]{:S(2)}, u32[]{:S(2)}) collective-permute-start(bf16[272,1024]{1,0:T(8,128)(2,1)} %copy-done.39), channel_id=1, source_target_pairs={{0,4},{2,6},{4,0},{6,2},{8,12},{10,14},{12,8},{14,10},{16,20},{18,... | collective-permute-start | bytes 1671176 | tf_op jit(solution)/shard_map/ppermute | solution.py:1242
  80.1 57.7 %collective-permute-start.23 = (bf16[272,1024]{1,0:T(8,128)(2,1)}, bf16[272,1024]{1,0:T(8,128)(2,1)}, u32[]{:S(2)}, u32[]{:S(2)}) collective-permute-start(bf16[272,1024]{1,0:T(8,128)(2,1)} %copy-done.39), channel_id=1, source_target_pairs={{0,2},{2,0},{4,6},{6,4},{8,10},{10,8},{12,14},{14,12},{16,18},{18,... | collective-permute-start | bytes 1671176 | tf_op jit(solution)/shard_map/ppermute | solution.py:1242
  80.1 25.7 %collective-permute-start.15 = (bf16[16,5120]{1,0:T(8,128)(2,1)S(1)}, bf16[16,5120]{1,0:T(8,128)(2,1)S(1)}, u32[]{:S(2)}, u32[]{:S(2)}) collective-permute-start(bf16[16,5120]{1,0:T(8,128)(2,1)S(1)} %constant_dynamic-slice_fusion), channel_id=1, source_target_pairs={{0,1},{1,0},{2,3},{3,2},{4,5},{5,4},{6,7},{7,6},{8,9},{9,8},{10,11... | collective-permute-start | bytes 491528 | tf_op jit(solution)/shard_map/ppermute | solution.py:1238
  105.6 26.0 %collective-permute-start.18 = (bf16[144,2048]{1,0:T(8,128)(2,1)S(1)}, bf16[144,2048]{1,0:T(8,128)(2,1)}, u32[]{:S(2)}, u32[]{:S(2)}) collective-permute-start(bf16[144,2048]{1,0:T(8,128)(2,1)S(1)} %get-tuple-element.231), channel_id=1, source_target_pairs={{0,1},{1,0},{2,3},{3,2},{4,5},{5,4},{6,7},{7,6},{8,9},{9,8},{10,11... | collective-permute-start | bytes 1769480 | tf_op jit(solution)/shard_map/ppermute | solution.py:1238
  106.7 70.6 %all-to-all-start.1 = ((bf16[32,32,1024]{2,1,0:T(8,128)(2,1)}), bf16[32,32,1024]{2,1,0:T(8,128)(2,1)}, u32[]{:S(2)}, u32[]{:S(2)}) async-start(bf16[32,32,1024]{2,1,0:T(8,128)(2,1)} %bitcast.94), calls=%async_computation.1 | async-start | bytes 4194304 | tf_op jit(solution)/shard_map/all_to_all | solution.py:1362
  131.6 14.1 %collective-permute-start.24 = (bf16[272,1024]{1,0:T(8,128)(2,1)}, bf16[272,1024]{1,0:T(8,128)(2,1)S(1)}, u32[]{:S(2)}, u32[]{:S(2)}) collective-permute-start(bf16[272,1024]{1,0:T(8,128)(2,1)} %collective-permute-done.17.rest_8_), channel_id=1, source_target_pairs={{0,2},{2,0},{4,6},{6,4},{8,10},{10,8},{12,14},{14,12},{16,18},{18,... | collective-permute-start | bytes 1671176 | tf_op jit(solution)/shard_map/ppermute | solution.py:1242
  131.8 13.0 %collective-permute-start.22 = (bf16[16,5120]{1,0:T(8,128)(2,1)S(1)}, bf16[16,5120]{1,0:T(8,128)(2,1)S(1)}, u32[]{:S(2)}, u32[]{:S(2)}) collective-permute-start(bf16[16,5120]{1,0:T(8,128)(2,1)S(1)} %copy-done.45), channel_id=1, source_target_pairs={{0,4},{2,6},{4,0},{6,2},{8,12},{10,14},{12,8},{14,10},{16,20},{18,... | collective-permute-start | bytes 491528 | tf_op jit(solution)/shard_map/ppermute | solution.py:1242
  137.1 8.6 %collective-permute-start.27 = (bf16[16,5120]{1,0:T(8,128)(2,1)S(1)}, bf16[16,5120]{1,0:T(8,128)(2,1)S(1)}, u32[]{:S(2)}, u32[]{:S(2)}) collective-permute-start(bf16[16,5120]{1,0:T(8,128)(2,1)S(1)} %copy-done.45), channel_id=1, source_target_pairs={{0,2},{2,0},{4,6},{6,4},{8,10},{10,8},{12,14},{14,12},{16,18},{18,... | collective-permute-start | bytes 491528 | tf_op jit(solution)/shard_map/ppermute | solution.py:1242
  137.3 33.3 %collective-permute-start.20 = (bf16[144,2048]{1,0:T(8,128)(2,1)S(1)}, bf16[144,2048]{1,0:T(8,128)(2,1)}, u32[]{:S(2)}, u32[]{:S(2)}) collective-permute-start(bf16[144,2048]{1,0:T(8,128)(2,1)S(1)} %copy-done.35), channel_id=1, source_target_pairs={{0,4},{2,6},{4,0},{6,2},{8,12},{10,14},{12,8},{14,10},{16,20},{18,... | collective-permute-start | bytes 1769480 | tf_op jit(solution)/shard_map/ppermute | solution.py:1242
  137.7 35.9 %collective-permute-start.25 = (bf16[144,2048]{1,0:T(8,128)(2,1)S(1)}, bf16[144,2048]{1,0:T(8,128)(2,1)S(1)}, u32[]{:S(2)}, u32[]{:S(2)}) collective-permute-start(bf16[144,2048]{1,0:T(8,128)(2,1)S(1)} %copy-done.35), channel_id=1, source_target_pairs={{0,2},{2,0},{4,6},{6,4},{8,10},{10,8},{12,14},{14,12},{16,18},{18,... | collective-permute-start | bytes 1769480 | tf_op jit(solution)/shard_map/ppermute | solution.py:1242
  144.8 28.8 %collective-permute-start.21 = (bf16[144,2048]{1,0:T(8,128)(2,1)}, bf16[144,2048]{1,0:T(8,128)(2,1)}, u32[]{:S(2)}, u32[]{:S(2)}) collective-permute-start(bf16[144,2048]{1,0:T(8,128)(2,1)} %collective-permute-done.18.rest_22_), channel_id=1, source_target_pairs={{0,4},{2,6},{4,0},{6,2},{8,12},{10,14},{12,8},{14,10},{16,20},{18,... | collective-permute-start | bytes 1769480 | tf_op jit(solution)/shard_map/ppermute | solution.py:1242
  145.7 27.9 %collective-permute-start.26 = (bf16[144,2048]{1,0:T(8,128)(2,1)}, bf16[144,2048]{1,0:T(8,128)(2,1)S(1)}, u32[]{:S(2)}, u32[]{:S(2)}) collective-permute-start(bf16[144,2048]{1,0:T(8,128)(2,1)} %collective-permute-done.18.rest_22_), channel_id=1, source_target_pairs={{0,2},{2,0},{4,6},{6,4},{8,10},{10,8},{12,14},{14,12},{16,18},{18,... | collective-permute-start | bytes 1769480 | tf_op jit(solution)/shard_map/ppermute | solution.py:1242
  145.7 30.5 %collective-permute-start.19 = (bf16[544,1024]{1,0:T(8,128)(2,1)S(1)}, bf16[544,1024]{1,0:T(8,128)(2,1)}, u32[]{:S(2)}, u32[]{:S(2)}) collective-permute-start(bf16[544,1024]{1,0:T(8,128)(2,1)S(1)} %copy-done.15), channel_id=1, source_target_pairs={{0,1},{1,0},{2,3},{3,2},{4,5},{5,4},{6,7},{7,6},{8,9},{9,8},{10,11... | collective-permute-start | bytes 3342344 | tf_op jit(solution)/shard_map/ppermute | solution.py:1238
  176.2 6.4 %collective-permute-start.31 = (bf16[544,1024]{1,0:T(8,128)(2,1)}, bf16[544,1024]{1,0:T(8,128)(2,1)}, u32[]{:S(2)}, u32[]{:S(2)}) collective-permute-start(bf16[544,1024]{1,0:T(8,128)(2,1)} %collective-permute-done.19.rest_33_), channel_id=1, source_target_pairs={{0,2},{2,0},{4,6},{6,4},{8,10},{10,8},{12,14},{14,12},{16,18},{18,... | collective-permute-start | bytes 3342344 | tf_op jit(solution)/shard_map/ppermute | solution.py:1242
  176.2 6.3 %collective-permute-start.29 = (bf16[144,2048]{1,0:T(8,128)(2,1)}, bf16[144,2048]{1,0:T(8,128)(2,1)S(1)}, u32[]{:S(2)}, u32[]{:S(2)}) collective-permute-start(bf16[144,2048]{1,0:T(8,128)(2,1)} %collective-permute-done.20.rest_19_), channel_id=1, source_target_pairs={{0,2},{2,0},{4,6},{6,4},{8,10},{10,8},{12,14},{14,12},{16,18},{18,... | collective-permute-start | bytes 1769480 | tf_op jit(solution)/shard_map/ppermute | solution.py:1242
  176.7 5.8 %collective-permute-start.30 = (bf16[144,2048]{1,0:T(8,128)(2,1)}, bf16[144,2048]{1,0:T(8,128)(2,1)}, u32[]{:S(2)}, u32[]{:S(2)}) collective-permute-start(bf16[144,2048]{1,0:T(8,128)(2,1)} %collective-permute-done.21.rest_23_), channel_id=1, source_target_pairs={{0,2},{2,0},{4,6},{6,4},{8,10},{10,8},{12,14},{14,12},{16,18},{18,... | collective-permute-start | bytes 1769480 | tf_op jit(solution)/shard_map/ppermute | solution.py:1242
  176.8 5.7 %collective-permute-start.28 = (bf16[16,5120]{1,0:T(8,128)(2,1)}, bf16[16,5120]{1,0:T(8,128)(2,1)S(1)}, u32[]{:S(2)}, u32[]{:S(2)}) collective-permute-start(bf16[16,5120]{1,0:T(8,128)(2,1)} %copy-done.46), channel_id=1, source_target_pairs={{0,2},{2,0},{4,6},{6,4},{8,10},{10,8},{12,14},{14,12},{16,18},{18,... | collective-permute-start | bytes 491528 | tf_op jit(solution)/shard_map/ppermute | solution.py:1242
  270.4 3.6 collective-permute-start.32
  276.2 19.5 %collective-permute-start.33 = (bf16[64,5632]{1,0:T(8,128)(2,1)S(1)}, bf16[64,5632]{1,0:T(8,128)(2,1)S(1)}, u32[]{:S(2)}, u32[]{:S(2)}) collective-permute-start(bf16[64,5632]{1,0:T(8,128)(2,1)S(1)} %dynamic-slice_convert_fusion), channel_id=1, source_target_pairs={{0,1},{1,0},{2,3},{3,2},{4,5},{5,4},{6,7},{7,6},{8,9},{9,8},{10,11... | collective-permute-start | bytes 2162696 | tf_op jit(solution)/shard_map/ppermute | solution.py:1238
  296.7 66.5 %collective-permute-start.34 = (bf16[32,5632]{1,0:T(8,128)(2,1)}, bf16[32,5632]{1,0:T(8,128)(2,1)}, u32[]{:S(2)}, u32[]{:S(2)}) collective-permute-start(bf16[32,5632]{1,0:T(8,128)(2,1)} %dynamic-slice_convert_fusion.1), channel_id=1, source_target_pairs={{0,4},{2,6},{4,0},{6,2},{8,12},{10,14},{12,8},{14,10},{16,20},{18,... | collective-permute-start | bytes 1081352 | tf_op jit(solution)/shard_map/ppermute | solution.py:1242
  297.7 67.4 %all-to-all-start.2 = ((bf16[32,32,1024]{2,1,0:T(8,128)(2,1)}), bf16[32,32,1024]{2,1,0:T(8,128)(2,1)S(1)}, u32[]{:S(2)}, u32[]{:S(2)}) async-start(bf16[32,32,1024]{2,1,0:T(8,128)(2,1)} %bitcast.97), calls=%async_computation.2 | async-start | bytes 4194304 | tf_op jit(solution)/shard_map/all_to_all | solution.py:1362
  367.2 6.6 %collective-permute-start.35 = (bf16[128,2688]{1,0:T(8,128)(2,1)}, bf16[128,2688]{1,0:T(8,128)(2,1)}, u32[]{:S(2)}, u32[]{:S(2)}) collective-permute-start(bf16[128,2688]{1,0:T(8,128)(2,1)} %dynamic-slice_bitcast_fusion.2), channel_id=1, source_target_pairs={{0,2},{2,0},{4,6},{6,4},{8,10},{10,8},{12,14},{14,12},{16,18},{18,... | collective-permute-start | bytes 2064392 | tf_op jit(solution)/shard_map/ppermute | solution.py:1242
  369.4 13.4 %collective-permute-start.38 = (bf16[8,5632]{1,0:T(8,128)(2,1)}, bf16[8,5632]{1,0:T(8,128)(2,1)}, u32[]{:S(2)}, u32[]{:S(2)}) collective-permute-start(bf16[8,5632]{1,0:T(8,128)(2,1)} %get-tuple-element.305), channel_id=1, source_target_pairs={{0,24},{2,26},{4,28},{6,30},{8,16},{10,18},{12,20},{14,22},{16,8},... | collective-permute-start | bytes 270344 | tf_op jit(solution)/shard_map/ppermute | solution.py:1242
  372.9 9.9 %collective-permute-start.37 = (bf16[8,5632]{1,0:T(8,128)(2,1)}, bf16[8,5632]{1,0:T(8,128)(2,1)}, u32[]{:S(2)}, u32[]{:S(2)}) collective-permute-start(bf16[8,5632]{1,0:T(8,128)(2,1)} %get-tuple-element.306), channel_id=1, source_target_pairs={{0,16},{2,18},{4,20},{6,22},{8,24},{10,26},{12,28},{14,30},{16,0},... | collective-permute-start | bytes 270344 | tf_op jit(solution)/shard_map/ppermute | solution.py:1242
  372.9 9.9 %collective-permute-start.36 = (bf16[8,5632]{1,0:T(8,128)(2,1)}, bf16[8,5632]{1,0:T(8,128)(2,1)}, u32[]{:S(2)}, u32[]{:S(2)}) collective-permute-start(bf16[8,5632]{1,0:T(8,128)(2,1)} %get-tuple-element.304), channel_id=1, source_target_pairs={{0,8},{2,10},{4,12},{6,14},{8,0},{10,2},{12,4},{14,6},{16,24},{18,... | collective-permute-start | bytes 270344 | tf_op jit(solution)/shard_map/ppermute | solution.py:1242
  375.9 27.3 %all-to-all-start.3 = ((bf16[16,8,2688]{2,1,0:T(8,128)(2,1)}), bf16[16,8,2688]{2,1,0:T(8,128)(2,1)S(1)}, u32[]{:S(2)}, u32[]{:S(2)}) async-start(bf16[16,8,2688]{2,1,0:T(8,128)(2,1)} %bitcast.68), calls=%async_computation.3 | async-start | bytes 1376256 | tf_op jit(solution)/shard_map/all_to_all | solution.py:1275
  408.7 14.6 %collective-permute-start.41 = (bf16[8,8320]{1,0:T(8,128)(2,1)S(1)}, bf16[8,8320]{1,0:T(8,128)(2,1)S(1)}, u32[]{:S(2)}, u32[]{:S(2)}) collective-permute-start(bf16[8,8320]{1,0:T(8,128)(2,1)S(1)} %pad_maximum_fusion.6), channel_id=1, source_target_pairs={{0,24},{2,26},{4,28},{6,30},{8,16},{10,18},{12,20},{14,22},{16,8},... | collective-permute-start | bytes 399368 | tf_op jit(solution)/shard_map/while/body/ppermute | solution.py:1242
  412.6 10.7 %collective-permute-start.40 = (bf16[8,8320]{1,0:T(8,128)(2,1)S(1)}, bf16[8,8320]{1,0:T(8,128)(2,1)S(1)}, u32[]{:S(2)}, u32[]{:S(2)}) collective-permute-start(bf16[8,8320]{1,0:T(8,128)(2,1)S(1)} %pad_maximum_fusion.6), channel_id=1, source_target_pairs={{0,16},{2,18},{4,20},{6,22},{8,24},{10,26},{12,28},{14,30},{16,0},... | collective-permute-start | bytes 399368 | tf_op jit(solution)/shard_map/while/body/ppermute | solution.py:1242
  412.6 10.7 %collective-permute-start.39 = (bf16[8,8320]{1,0:T(8,128)(2,1)S(1)}, bf16[8,8320]{1,0:T(8,128)(2,1)S(1)}, u32[]{:S(2)}, u32[]{:S(2)}) collective-permute-start(bf16[8,8320]{1,0:T(8,128)(2,1)S(1)} %pad_maximum_fusion.6), channel_id=1, source_target_pairs={{0,8},{2,10},{4,12},{6,14},{8,0},{10,2},{12,4},{14,6},{16,24},{18,... | collective-permute-start | bytes 399368 | tf_op jit(solution)/shard_map/while/body/ppermute | solution.py:1242
  417.0 54.9 %all-to-all-start.4 = ((bf16[32,32,1024]{2,1,0:T(8,128)(2,1)}), bf16[32,32,1024]{2,1,0:T(8,128)(2,1)}, u32[]{:S(2)}, u32[]{:S(2)}) async-start(bf16[32,32,1024]{2,1,0:T(8,128)(2,1)} %bitcast.36), calls=%async_computation.4 | async-start | bytes 4194304 | tf_op jit(solution)/shard_map/all_to_all | solution.py:1362
  425.0 31.3 %collective-permute-start = (bf16[32,8320]{1,0:T(8,128)(2,1)S(1)}, bf16[32,8320]{1,0:T(8,128)(2,1)S(1)}, u32[]{:S(2)}, u32[]{:S(2)}) collective-permute-start(bf16[32,8320]{1,0:T(8,128)(2,1)S(1)} %bitcast.84), channel_id=1, source_target_pairs={{0,4},{2,6},{4,0},{6,2},{8,12},{10,14},{12,8},{14,10},{16,20},{18,... | collective-permute-start | bytes 1597448 | tf_op jit(solution)/shard_map/while/body/ppermute | solution.py:1242
  456.5 2.7 collective-permute-start.1
  (50 other events, 851.7 us)
